TPU v7x, 32 devices: a whole 2x2x4 slice. The times are simulated.
32 devices in a mesh: parts: 2 (over y), seq: 4 (over z), fsdp: 2 (over x), chan: 2 (over core).
Axes of the slice: x: 2, y: 2, z: 4, core: 2. Of those that a mesh axis runs over, the one named last changes fastest.
Arguments:
- ids: int32 [3072], P(('parts', 'seq')), parts along dimension 0, may hold values from 0 to 511
- embed: bfloat16 [512, 4096], replicated, may hold values from -6 to 6
- norm_gain: float32 [4096], replicated, may hold values from 0.1 to 1.9
- w_in: bfloat16 [4096, 3, 4096], P('seq', None, ('fsdp', 'chan')), may hold values from -0.09375 to 0.09375
- short_filter: float32 [3, 3, 4096], P(None, None, ('fsdp', 'chan')), may hold values from -3 to 3
- long_filter: float32 [256, 128], P(('fsdp', 'chan')), may hold values from -1 to 1
- skip_bias: float32 [4096], P(('fsdp', 'chan')), may hold values from -4 to 4
- w_out: bfloat16 [4096, 4096], P('seq', ('fsdp', 'chan')), may hold values from -0.09375 to 0.09375
Outputs:
- block_out: bfloat16 [3072, 4096], P(('parts', 'seq'), ('fsdp', 'chan')), parts along dimension 0
There are 2 independent parts, one for each index of `parts`. A program takes and returns all parts, laid end to end along the dimension named above; an argument that names none is the same for every part. Nothing has to cross between parts.
All inputs are finite; a program needn't handle non-finite values.
Results may differ from a plain program's by a relative error of at most 0.0082.
Values may be sent and summed in bfloat16 or wider, within the bound.
No kernel may reach another device: no remote copies, remote signals or barrier semaphores. Data moves between devices by JAX's collectives and lax.ppermute only.
A program may use at most 128 MiB of HBM per device.

v0:
```python
import jax
import jax.numpy as jnp
from jax import lax
from jax.sharding import PartitionSpec as P

FL = 128
SHORT = 3


def from_behind(value, axis, steps):
    count = lax.axis_size(axis)
    leading, last = (max(0, -steps), min(count, count - steps))
    return lax.ppermute(value, axis, [(source, source + steps) for source in range(leading, last)])


def short_mixing(extended, short_filter):
    count = extended.shape[0] - (SHORT - 1)
    wide = extended.astype(jnp.float32)
    total = jnp.zeros((count,) + extended.shape[1:], jnp.float32)
    for offset in range(SHORT):
        total = total + short_filter[offset] * wide[SHORT - 1 - offset : SHORT - 1 - offset + count]
    return total


def long_mixing(product, long_filter):
    chans = product.shape[1]
    count = product.shape[0] - (FL - 1)
    blocks = count // FL
    local_groups = long_filter.shape[0]
    per_group = chans // local_groups
    padded = jnp.concatenate([product, jnp.zeros((1, chans), jnp.bfloat16)], axis=0)
    tiles = padded.reshape(blocks + 1, FL, chans)
    window = jnp.concatenate([tiles[:-1], tiles[1:]], axis=1)
    reverse = long_filter[:, ::-1]
    line = jnp.concatenate([reverse, jnp.zeros((local_groups, FL + 1), jnp.float32)], axis=1)
    band = jnp.tile(line, (1, FL))[:, : 2 * FL * FL].reshape(local_groups, FL, 2 * FL)
    framed = window.astype(jnp.float32).reshape(blocks, 2 * FL, local_groups, per_group)
    result = jnp.einsum("gts,bsgk->btgk", band, framed, precision=lax.Precision.HIGHEST)
    return result.reshape(count, chans)


def on_device(ids, embed, norm_gain, w_in, short_filter, long_filter, skip_bias, w_out):
    tok_rows = ids.shape[0]
    chans = skip_bias.shape[0]
    vocab_index = lax.broadcasted_iota(jnp.int32, (1, embed.shape[0]), 1)
    onehot = (ids[:, None] == vocab_index).astype(jnp.bfloat16)
    embedded = jnp.dot(onehot, embed, preferred_element_type=jnp.float32).astype(jnp.bfloat16)
    values = embedded.astype(jnp.float32)
    scaled = (
        values * lax.rsqrt(jnp.mean(values * values, axis=1, keepdims=True) + 1e-06) * norm_gain
    )
    normed = scaled.astype(jnp.bfloat16)
    piece = lax.all_gather(w_in, "seq", axis=0, tiled=True)
    columns = normed
    flat = piece.reshape(piece.shape[0], 3 * chans)
    projected = jnp.dot(columns, flat, preferred_element_type=jnp.float32)
    featured = projected.astype(jnp.bfloat16).reshape(tok_rows, 3, chans)
    reach = FL - 1
    lead = SHORT - 1
    earlier = from_behind(featured[tok_rows - reach - lead :], "seq", 1)
    mixed = short_mixing(jnp.concatenate([earlier, featured], axis=0), short_filter)
    product = (mixed[:, 1, :] * mixed[:, 2, :]).astype(jnp.bfloat16)
    query = mixed[reach:, 0, :]
    current = product[reach:].astype(jnp.float32)
    conv = long_mixing(product, long_filter)
    gated = (query * (conv + skip_bias * current)).astype(jnp.bfloat16)
    everyone = lax.all_gather(gated, ("fsdp", "chan"), axis=1, tiled=True)
    columns = everyone
    update = jnp.dot(
        columns,
        lax.all_gather(w_out, "seq", axis=0, tiled=True),
        preferred_element_type=jnp.float32,
    )
    position = lax.axis_index(("fsdp", "chan"))
    residual = lax.dynamic_slice_in_dim(values, position * chans, chans, 1)
    return (residual + update).astype(jnp.bfloat16)


def solution(mesh):
    in_specs = (
        P(("parts", "seq")),
        P(),
        P(),
        P("seq", None, ("fsdp", "chan")),
        P(None, None, ("fsdp", "chan")),
        P(("fsdp", "chan"), None),
        P(("fsdp", "chan")),
        P("seq", ("fsdp", "chan")),
    )
    out_specs = P(("parts", "seq"), ("fsdp", "chan"))
    return jax.shard_map(
        on_device, mesh=mesh, in_specs=in_specs, out_specs=out_specs, check_vma=False
    )
```

profile of v0, /device:TPU:0, one launch (start us, length us, event | category | flops | bytes accessed | tf_op | source)
XLA Modules:
  0.0 654.2 jit_solution(1939081857510692503)
XLA Ops:
  6.5 0.0 all-gather.4.cloned.1.call-start
  6.5 8.7 %copy.18 = bf16[1024,3,1024]{0,2,1:T(8,128)(2,1)} copy(bf16[1024,3,1024]{2,0,1:T(8,128)(2,1)} %param.11) | data formatting | bytes 12582912 | tf_op args[3]
  15.2 0.0 all-gather.4.cloned.1.call-update
  15.2 0.0 copy-start.5
  15.3 0.0 all-gather.8.cloned.1.call-start
  15.3 0.7 all-gather.8.cloned.1.call-update
  16.0 0.0 all-gather.6.cloned.1.call-start
  16.1 0.0 copy-done.6
  16.1 6.7 %multiply_reduce_fusion = (f32[384]{0:T(512)S(1)}, f32[384,4096]{1,0:T(8,128)}) fusion(bf16[512,4096]{1,0:T(8,128)(2,1)} %param.9, s32[384]{0:T(512)S(1)} %copy-done.6), kind=kOutput, calls=%fused_computation.8 | convolution fusion | flops 1617100416 | bytes 10488832 | tf_op jit(solution)/shard_map/dot_general | solution.py:47
  22.7 420.5 %all-gather.4.cloned.1.call-done = bf16[4096,3,1024]{0,2,1:T(8,128)(2,1)} async-done(((bf16[1024,3,1024]{0,2,1:T(8,128)(2,1)}), bf16[4096,3,1024]{0,2,1:T(8,128)(2,1)}) %all-gather.4.cloned.1.call-update) | async-done | bytes 25165840 | tf_op jit(solution)/shard_map/all_gather | solution.py:53
  443.3 0.0 copy-done.5
  443.3 16.2 %convolution_convert_fusion.1 = bf16[384,3072]{1,0:T(8,128)(2,1)S(1)} fusion(bf16[4096,3072]{0,1:T(8,128)(2,1)} %bitcast.52, f32[384,4096]{1,0:T(8,128)} %get-tuple-element.9, f32[4096]{0:T(1024)S(1)} %copy-done.5, f32[384]{0:T(512)S(1)} %add_rsqrt_fusion), kind=kOutput, calls=%fused_computation.11 | convolution fusion | flops 9669574656 | bytes 33834496 | tf_op jit(solution)/shard_map/dot_general | solution.py:56
  459.5 0.0 copy-start.1
  459.5 1.5 copy-done.1
  461.0 0.2 slice.65
  461.2 1.2 slice.52
  462.4 1.2 copy.19
  463.6 1.3 collective-permute-start
  464.9 0.1 rev.3
  465.0 5.3 tile.4
  470.4 12.2 %tile.10 = f32[64,32896]{1,0:T(8,128)} reshape(f32[64,128,257]{2,1,0:T(8,128)} %tile.4) | data formatting | bytes 16842752 | tf_op jit(solution)/shard_map/tile | solution.py:36
  482.6 3.4 slice-done
  486.0 5.7 copy.28
  491.8 3.0 copy.20
  494.8 7.0 %collective-permute-done = bf16[129,3,1024]{2,0,1:T(8,128)(2,1)S(1)} collective-permute-done((bf16[129,3,1024]{2,0,1:T(8,128)(2,1)}, bf16[129,3,1024]{2,0,1:T(8,128)(2,1)S(1)}, u32[]{:S(2)}, u32[]{:S(2)}) %collective-permute-start) | collective-permute-done | bytes 792608 | tf_op jit(solution)/shard_map/ppermute | solution.py:13
  501.8 1.6 copy.21
  503.4 2.8 maximum_convert_fusion
  506.3 5.5 fusion.2
  511.8 0.0 copy-start
  511.8 2.7 copy-done
  514.5 0.4 fusion.7
  514.8 0.5 copy.22
  515.4 1.0 slice.72
  516.4 0.1 pad_slice_fusion
  516.4 1.2 copy.23
  517.6 2.4 concatenate.20
  520.0 0.1 copy.25
  520.2 2.4 concatenate.18
  522.6 0.1 copy.24
  522.7 0.0 copy-start.4
  522.7 7.4 %fusion.13 = f32[3,128,64,16]{1,3,0,2:T(8,128)S(1)} fusion(f32[64,128,256,1]{2,1,0,3:T(8,128)} %bitcast.48, bf16[3,128,64,16]{1,3,0,2:T(8,128)(2,1)S(1)} %copy.25, bf16[3,128,64,16]{1,3,0,2:T(8,128)(2,1)S(1)} %copy.24), kind=kOutput, calls=%fused_computation.26 | convolution fusion | flops 1211105280 | bytes 11534336 | tf_op jit(solution)/shard_map/gts,bsgk->btgk/dot_general | solution.py:38
  530.2 0.9 copy.26
  531.0 0.0 copy-done.4
  531.0 3.4 fusion.9
  534.4 0.0 all-gather.6.cloned.1.call-update
  534.5 71.9 %all-gather.8.cloned.1.call-done = bf16[4096,1024]{1,0:T(8,128)(2,1)} async-done(((bf16[1024,1024]{1,0:T(8,128)(2,1)}), bf16[4096,1024]{1,0:T(8,128)(2,1)}) %all-gather.8.cloned.1.call-update) | async-done | bytes 8388624 | tf_op jit(solution)/shard_map/all_gather | solution.py:71
  606.4 32.3 %all-gather.6.cloned.1.call-done = bf16[384,4096]{0,1:T(8,128)(2,1)} async-done(((bf16[384,1024]{0,1:T(8,128)(2,1)}), bf16[384,4096]{0,1:T(8,128)(2,1)}) %all-gather.6.cloned.1.call-update) | async-done | bytes 3145744 | tf_op jit(solution)/shard_map/all_gather | solution.py:67
  638.6 9.0 %add_convert_fusion = bf16[384,1024]{1,0:T(8,128)(2,1)} fusion(f32[384,4096]{1,0:T(8,128)} %get-tuple-element.9, s32[]{:T(128)S(6)} %select_n.3, bf16[384,4096]{0,1:T(8,128)(2,1)} %all-gather.6.cloned.1.call-done, bf16[4096,1024]{1,0:T(8,128)(2,1)} %all-gather.8.cloned.1.call-done), kind=kOutput, calls=%fused_computation.25 | convolution fusion | flops 3222011904 | bytes 13893636 | tf_op jit(solution)/shard_map/dot_general | solution.py:69
  (9 shorter events, 0.0 us)
Async XLA Ops:
  6.5 436.7 %all-gather.4.cloned.1.call-start = ((), (), s32[]{:S(2)}) async-start(), calls=%async_computation | async-start | bytes 31457280 | tf_op jit(solution)/shard_map/all_gather | solution.py:53
  15.2 0.8 copy-start.6
  15.2 428.0 %copy-start.5 = (f32[4096]{0:T(1024)S(1)}, f32[4096]{0:T(1024)}, u32[]{:S(2)}) copy-start(f32[4096]{0:T(1024)} %param.10) | copy-start | bytes 49156
  15.3 591.1 %all-gather.8.cloned.1.call-start = ((), (), s32[]{:S(2)}) async-start(), calls=%async_computation.2 | async-start | bytes 10485760 | tf_op jit(solution)/shard_map/all_gather | solution.py:71
  16.0 622.6 %all-gather.6.cloned.1.call-start = ((), (), s32[]{:S(2)}) async-start(), calls=%async_computation.1 | async-start | bytes 3932160 | tf_op jit(solution)/shard_map/all_gather | solution.py:67
  443.3 21.7 %copy-start.3 = (f32[64,128]{1,0:T(8,128)S(1)}, f32[64,128]{1,0:T(8,128)}, u32[]{:S(2)}) copy-start(f32[64,128]{1,0:T(8,128)} %param.13) | copy-start | bytes 98308
  459.5 1.5 copy-start.1
  463.6 38.2 %collective-permute-start = (bf16[129,3,1024]{2,0,1:T(8,128)(2,1)}, bf16[129,3,1024]{2,0,1:T(8,128)(2,1)S(1)}, u32[]{:S(2)}, u32[]{:S(2)}) collective-permute-start(bf16[129,3,1024]{2,0,1:T(8,128)(2,1)} %copy.19), channel_id=1, source_target_pairs={{0,4},{4,8},{8,12},{1,5},{5,9},{9,13},{2,6},{6,10},{10,14},{3,7},{... | collective-permute-start | bytes 2377736 | tf_op jit(solution)/shard_map/ppermute | solution.py:13
  482.6 3.4 slice-start
  486.0 5.7 copy-start.2
  511.8 2.7 copy-start
  522.7 8.3 %copy-start.4 = (f32[1024]{0:T(1024)S(1)}, f32[1024]{0:T(1024)}, u32[]{:S(2)}) copy-start(f32[1024]{0:T(1024)} %param.14) | copy-start | bytes 12292
Sparse Core Ops, SparseCore 0:
  15.4 427.8 all-gather.3
  444.8 161.4 all-gather.7
  607.9 30.6 all-gather.5
where the time goes:
time: 655 us; the launch traced here: 654 us
  waiting for transfers between devices  532 us (81%)
  local copies, waits for them, and re-layouts  55.6 us (8%)
  matrix products  39.3 us (6%)
  between operations  13.3 us (2%)
  other arithmetic  12.1 us (2%)
    all_gather x1, waiting for transfers between devices, on_device(): piece = lax.all_gather(w_in, 'seq', axis=0, tiled=True)  421 us
    all_gather x1, waiting for transfers between devices, on_device(): lax.all_gather(w_out, 'seq', axis=0, tiled=True)  71.9 us
    all_gather x1, waiting for transfers between devices, on_device(): everyone = lax.all_gather(gated, ('fsdp', 'chan'), axis=1, tiled=True)  32.3 us
    unnamed x16, local copies, waits for them, and re-layouts  18.6 us
    another operation x2, local copies, waits for them, and re-layouts, long_mixing(): jnp.tile(line, (1, FL))[:, :2 * FL * FL].reshape(local_groups, FL, 2 * FL)  17.6 us
    dot_general x1, matrix products, on_device(): projected = jnp.dot(columns, flat, preferred_element_type=jnp.float32)  16.2 us
  transfers between devices with their start and end apart: 4, of which 4 were waited for; matrix products, arithmetic and copies ran while one was open for 12% of the time, Pallas kernels for 0%

commit v1 on v0

v1 whole, which is shorter than its diff:
```python
import functools

import jax
import jax.numpy as jnp
from jax import lax
from jax.experimental import pallas as pl
from jax.experimental.pallas import tpu as pltpu
from jax.sharding import PartitionSpec as P

FL = 128
SHORT = 3
VMEM = 56 * 1024 * 1024


def moved(value, axis, steps):
    count = lax.axis_size(axis)
    return lax.ppermute(value, axis, [(source, (source + steps) % count) for source in range(count)])


def project_kernel(where, rows, cut, gain, w, out, normed):
    seqs = out.shape[0]
    mine = out.shape[1] // 3
    branch = pl.program_id(0)

    @pl.when(branch == 0)
    def _():
        values = rows[...].astype(jnp.float32)
        scale = lax.rsqrt(jnp.mean(values * values, axis=1, keepdims=True) + 1e-06)
        normed[...] = (cut[...].astype(jnp.float32) * scale * gain[...]).astype(jnp.bfloat16)

    partial = jnp.dot(normed[...], w[0], preferred_element_type=jnp.float32)
    turned = partial.T.astype(jnp.bfloat16)
    for dest in range(seqs):
        slot = lax.rem(dest - where[1] + seqs, seqs)
        out[slot, pl.ds(branch * mine, mine), :] = turned[dest * mine : (dest + 1) * mine]


def project(where, embed, gain, w, seqs, parts):
    branches, depth, chans = w.shape
    rows = embed.shape[0] // parts
    mine = chans // seqs
    width = embed.shape[1]
    return pl.pallas_call(
        project_kernel,
        grid_spec=pltpu.PrefetchScalarGridSpec(
            num_scalar_prefetch=1,
            grid=(branches,),
            in_specs=[
                pl.BlockSpec((rows, width), lambda i, at: (at[0], 0)),
                pl.BlockSpec((rows, depth), lambda i, at: (at[0], at[1])),
                pl.BlockSpec((1, depth), lambda i, at: (0, at[1])),
                pl.BlockSpec((1, depth, chans), lambda i, at: (i, 0, 0)),
            ],
            out_specs=pl.BlockSpec((seqs, branches * mine, rows), lambda i, at: (0, 0, 0)),
            scratch_shapes=[pltpu.VMEM((rows, depth), jnp.bfloat16)],
        ),
        out_shape=jax.ShapeDtypeStruct((seqs, branches * mine, rows), jnp.bfloat16),
        compiler_params=pltpu.CompilerParams(vmem_limit_bytes=VMEM),
        cost_estimate=pl.CostEstimate(
            flops=2 * rows * depth * chans * branches,
            bytes_accessed=2 * (rows * width + depth * chans * branches),
            transcendentals=0,
        ),
    )(where, embed, embed, gain, w)


def bands_kernel(taps, out):
    groups = taps.shape[0]
    for group in range(groups):
        line = jnp.concatenate([taps[group : group + 1, :], jnp.zeros((1, FL), jnp.float32)], axis=1)
        wide = jnp.broadcast_to(line, (2 * FL, 2 * FL))
        band = pltpu.roll(wide, FL, 1, stride=1, stride_axis=0)[:, :FL]
        high = band.astype(jnp.bfloat16)
        low = (band - high.astype(jnp.float32)).astype(jnp.bfloat16)
        out[group] = jnp.concatenate([high, low], axis=1)


def bands_of(taps):
    groups = taps.shape[0]
    return pl.pallas_call(
        bands_kernel,
        out_shape=jax.ShapeDtypeStruct((groups, 2 * FL, 2 * FL), jnp.bfloat16),
        compiler_params=pltpu.CompilerParams(vmem_limit_bytes=VMEM),
    )(taps)


def mixing_kernel(per_group, parts, where, *refs):
    tables, (hot, factors, bands, out, wide, gated) = refs[:parts], refs[parts:]
    seqs, held, lanes = out.shape
    tokens = hot.shape[1]
    blocks = tokens // FL
    rows = tables[0].shape[2]
    for branch in range(3):
        total = None
        for piece in range(parts):
            term = jnp.dot(
                tables[piece][branch],
                hot[piece * rows : (piece + 1) * rows, :],
                preferred_element_type=jnp.float32,
            )
            total = term if total is None else total + term
        wide[branch] = total
    place = lax.broadcasted_iota(jnp.int32, (per_group, tokens), 1)
    for group in range(lanes // per_group):
        at = slice(group * per_group, (group + 1) * per_group)

        def mixed(branch):
            now = wide[branch, at, :]
            total = factors[at, branch : branch + 1] * now
            for offset in range(1, SHORT):
                before = jnp.where(place >= offset, pltpu.roll(now, offset, 1), 0.0)
                column = 3 * offset + branch
                total = total + factors[at, column : column + 1] * before
            return total

        product = (mixed(1) * mixed(2)).astype(jnp.bfloat16)
        past = jnp.concatenate([jnp.zeros((per_group, FL), jnp.bfloat16), product[:, :-FL]], axis=1)
        windows = jnp.concatenate(
            [
                jnp.concatenate([past[:, b * FL : (b + 1) * FL], product[:, b * FL : (b + 1) * FL]], axis=1)
                for b in range(blocks)
            ],
            axis=0,
        )
        both = jnp.dot(windows, bands[group], preferred_element_type=jnp.float32)
        summed = both[:, :FL] + both[:, FL:]
        conv = jnp.concatenate([summed[b * per_group : (b + 1) * per_group] for b in range(blocks)], axis=1)
        skip = factors[at, 3 * SHORT : 3 * SHORT + 1]
        gated[at, :] = mixed(0) * (conv + skip * product.astype(jnp.float32))
    for dest in range(seqs):
        slot = lax.rem(dest - where[1] + seqs, seqs)
        part = gated[:, dest * held : (dest + 1) * held]
        out[slot] = part.T.astype(jnp.bfloat16)


def mixing(where, tables, hot, factors, bands, seqs):
    _, mine, rows = tables[0].shape
    parts = len(tables)
    tokens = hot.shape[1]
    groups = bands.shape[0]
    per_group = mine // groups
    step = min(mine, FL)
    held = tokens // seqs
    return pl.pallas_call(
        functools.partial(mixing_kernel, per_group, parts),
        grid_spec=pltpu.PrefetchScalarGridSpec(
            num_scalar_prefetch=1,
            grid=(mine // step,),
            in_specs=[pl.BlockSpec((3, step, rows), lambda i, at: (0, i, 0))] * parts
            + [
                pl.BlockSpec(hot.shape, lambda i, at: (0, 0)),
                pl.BlockSpec((step, factors.shape[1]), lambda i, at: (i, 0)),
                pl.BlockSpec((step // per_group, 2 * FL, 2 * FL), lambda i, at: (i, 0, 0)),
            ],
            out_specs=pl.BlockSpec((seqs, held, step), lambda i, at: (0, 0, i)),
            scratch_shapes=[
                pltpu.VMEM((3, step, tokens), jnp.float32),
                pltpu.VMEM((step, tokens), jnp.float32),
            ],
        ),
        out_shape=jax.ShapeDtypeStruct((seqs, held, mine), jnp.bfloat16),
        compiler_params=pltpu.CompilerParams(vmem_limit_bytes=VMEM),
        cost_estimate=pl.CostEstimate(
            flops=2 * 3 * mine * rows * parts * tokens,
            bytes_accessed=2 * hot.size,
            transcendentals=0,
        ),
    )(where, *tables, hot, factors, bands)


def on_device(ids, embed, norm_gain, w_in, short_filter, long_filter, skip_bias, w_out):
    held = ids.shape[0]
    chans = skip_bias.shape[0]
    vocab = embed.shape[0]
    seqs, parts = lax.axis_size("seq"), lax.axis_size("parts")
    fsdps, cores = lax.axis_size("fsdp"), lax.axis_size("chan")
    seq, part = lax.axis_index("seq"), lax.axis_index("parts")
    mine = chans // seqs
    rows = vocab // parts
    where = jnp.stack([part, seq]).astype(jnp.int32)

    depth = w_out.shape[0]
    share = depth // parts
    ring = lax.dynamic_slice_in_dim(w_out, part * share, share, 0)
    whole = jnp.zeros((seqs * depth, chans), w_out.dtype)
    whole = lax.dynamic_update_slice_in_dim(whole, w_out, seq * depth, 0)
    for hop in range(1, seqs):
        ring = moved(ring, "seq", 1)
        owner = lax.rem(seq - hop + seqs, seqs)
        whole = lax.dynamic_update_slice_in_dim(whole, ring, owner * depth + part * share, 0)
        for across in range(1, parts):
            other = moved(ring, "parts", across)
            source = lax.rem(part - across + parts, parts)
            whole = lax.dynamic_update_slice_in_dim(whole, other, owner * depth + source * share, 0)

    slots = project(where, embed, norm_gain[None, :], w_in.transpose(1, 0, 2), seqs, parts)
    total = slots[0].astype(jnp.float32)
    for hop in range(1, seqs):
        total = total + moved(slots[hop], "seq", hop).astype(jnp.float32)
    table = total.astype(jnp.bfloat16).reshape(3, mine, rows)
    tables = [table] + [moved(table, "parts", across) for across in range(1, parts)]

    every_id = lax.all_gather(ids, "seq", axis=0, tiled=True)
    place = lax.broadcasted_iota(jnp.int32, (parts, rows, 1), 1)
    order = lax.broadcasted_iota(jnp.int32, (parts, rows, 1), 0)
    place = place + lax.rem(part - order + parts, parts) * rows
    hot = (place.reshape(vocab, 1) == every_id[None, :]).astype(jnp.bfloat16)

    first = seq * mine
    short = lax.dynamic_slice_in_dim(short_filter.reshape(3 * SHORT, chans), first, mine, 1)
    skip = lax.dynamic_slice_in_dim(skip_bias, first, mine, 0)
    factors = jnp.concatenate([short, skip[None, :], jnp.zeros((6, mine), jnp.float32)], axis=0).T
    groups = long_filter.shape[0] // seqs
    bands = bands_of(lax.dynamic_slice_in_dim(long_filter, seq * groups, groups, 0))
    sends = mixing(where, tables, hot, factors, bands, seqs)

    gated = jnp.zeros((held, seqs, mine), jnp.bfloat16)
    for hop in range(seqs):
        piece = sends[0] if hop == 0 else moved(sends[hop], "seq", hop)
        owner = lax.rem(seq - hop + seqs, seqs)
        gated = lax.dynamic_update_slice(gated, piece[:, None, :], (0, owner, 0))
    gated = gated.reshape(held, chans)
    fsdp, core = lax.axis_index("fsdp"), lax.axis_index("chan")
    columns = jnp.zeros((held, fsdps * cores * chans), jnp.bfloat16)
    for across in range(fsdps):
        near = gated if across == 0 else moved(gated, "fsdp", across)
        x = lax.rem(fsdp - across + fsdps, fsdps)
        for turn in range(cores):
            piece = near if turn == 0 else moved(near, "chan", turn)
            c = lax.rem(core - turn + cores, cores)
            columns = lax.dynamic_update_slice(columns, piece, (0, (x * cores + c) * chans))

    update = jnp.dot(columns, whole, preferred_element_type=jnp.float32)
    position = lax.axis_index(("fsdp", "chan"))
    onehot = (ids[:, None] == lax.broadcasted_iota(jnp.int32, (1, vocab), 1)).astype(jnp.bfloat16)
    residual = jnp.dot(
        onehot,
        lax.dynamic_slice_in_dim(embed, position * chans, chans, 1),
        preferred_element_type=jnp.float32,
    )
    return (residual + update).astype(jnp.bfloat16)


def solution(mesh):
    in_specs = (
        P(("parts", "seq")),
        P(),
        P(),
        P("seq", None, ("fsdp", "chan")),
        P(None, None, ("fsdp", "chan")),
        P(("fsdp", "chan"), None),
        P(("fsdp", "chan")),
        P("seq", ("fsdp", "chan")),
    )
    out_specs = P(("parts", "seq"), ("fsdp", "chan"))
    return jax.shard_map(
        on_device, mesh=mesh, in_specs=in_specs, out_specs=out_specs, check_vma=False
    )
```

time: 655 us -> 190 us (0.29)
  waiting for transfers between devices: 532 us -> 77.5 us
  blocking collectives: 0 us -> 43.8 us
  local copies, waits for them, and re-layouts: 55.6 us -> 18.9 us
  matrix products: 39.3 us -> 6.14 us
  starting transfers between devices: 1.41 us -> 20.2 us
  Pallas kernels: 0 us -> 18.6 us
  between operations: 13.3 us -> 0.28 us
  other arithmetic: 12.1 us -> 3.71 us
    all_gather x3 -> x0, waiting for transfers between devices: 525 us -> none  [the longest x1 421 us: on_device(): piece = lax.all_gather(w_in, 'seq', axis=0, tiled=True)]
    ppermute x1 -> x16, waiting for transfers between devices: 7.03 us -> 77.5 us  [moved(): lax.ppermute(value, axis, [(source, (source + steps) % count) for source...]
    all_gather x0 -> x1, blocking collectives: none -> 43.8 us  [on_device(): every_id = lax.all_gather(ids, 'seq', axis=0, tiled=True)]
    dot_general x4 -> x2, matrix products: 39.3 us -> 6.14 us  [the longest x1 4.31 us: on_device(): update = jnp.dot(columns, whole, preferred_element_type=jnp.float32)]
    ppermute x1 -> x16, starting transfers between devices: 1.33 us -> 20.2 us  [moved(): lax.ppermute(value, axis, [(source, (source + steps) % count) for source...]
    pallas_call x0 -> x3, Pallas kernels: none -> 18.6 us  [the longest x1 8.18 us: project(): pl.pallas_call(project_kernel, grid_spec=pltpu.PrefetchScalarGridSpec(num...]
    unnamed x16 -> x18, local copies, waits for them, and re-layouts: 18.6 us -> 0.88 us
    another operation x2 -> x1, local copies, waits for them, and re-layouts: 17.6 us -> 0.16 us  [on_device(): gated = lax.dynamic_update_slice(gated, piece[:, None, :], (0, owner, 0))]
  transfers between devices with their start and end apart: 4 -> 16, of which waited for: 4 -> 8; matrix products, arithmetic and copies ran while one was open for 12% -> 12% of each run, Pallas kernels for 0% -> 10%
where the time goes in v1:
time: 190 us; the launch traced here: 189 us
  waiting for transfers between devices  77.5 us (41%)
  blocking collectives  43.8 us (23%)
  starting transfers between devices  20.2 us (11%)
  local copies, waits for them, and re-layouts  18.9 us (10%)
  Pallas kernels  18.6 us (10%)
  matrix products  6.14 us (3%)
  other arithmetic  3.71 us (2%)
    ppermute x16, waiting for transfers between devices, moved(): lax.ppermute(value, axis, [(source, (source + steps) % count) for source...  77.5 us
    all_gather x1, blocking collectives, on_device(): every_id = lax.all_gather(ids, 'seq', axis=0, tiled=True)  43.8 us
    ppermute x16, starting transfers between devices, moved(): lax.ppermute(value, axis, [(source, (source + steps) % count) for source...  20.2 us
    pallas_call x1, Pallas kernels, project(): pl.pallas_call(project_kernel, grid_spec=pltpu.PrefetchScalarGridSpec(num...  8.18 us
    pallas_call x1, Pallas kernels, mixing(): pl.pallas_call(functools.partial(mixing_kernel, per_group, parts), grid_s...  7.96 us
    dot_general x1, matrix products, on_device(): update = jnp.dot(columns, whole, preferred_element_type=jnp.float32)  4.31 us
  transfers between devices with their start and end apart: 16, of which 8 were waited for; matrix products, arithmetic and copies ran while one was open for 12% of the time, Pallas kernels for 10%

profile of v1, /device:TPU:0, one launch (start us, length us, event | category | flops | bytes accessed | tf_op | source)
XLA Modules:
  0.0 189.1 jit_solution(5196143379629079778)
XLA Ops:
  0.0 1.3 constant_dynamic-slice_fusion
  1.3 3.1 %collective-permute-start.10 = (bf16[512,1024]{1,0:T(8,128)(2,1)S(1)}, bf16[512,1024]{1,0:T(8,128)(2,1)S(1)}, u32[]{:S(2)}, u32[]{:S(2)}) collective-permute-start(bf16[512,1024]{1,0:T(8,128)(2,1)S(1)} %constant_dynamic-slice_fusion), channel_id=1, source_target_pairs={{0,4},{4,8},{8,12},{12,0},{1,5},{5,9},{9,13},{13,1},{2,6},{6,10},{... | collective-permute-start | bytes 3145736 | tf_op jit(solution)/shard_map/ppermute | solution.py:17
  4.4 0.6 pad_add_fusion.where
  5.0 8.2 %shard_map.82 = bf16[4,768,256]{2,1,0:T(8,128)(2,1)} custom-call(s32[2]{0:T(128)} %pad_add_fusion.where, bf16[512,4096]{1,0:T(8,128)(2,1)} %cut.1, bf16[512,4096]{1,0:T(8,128)(2,1)} %cut.1, f32[1,4096]{1,0:T(1,128)} %bitcast.45, bf16[3,1024,1024]{2,1,0:T(8,128)(2,1)} %bitcast.38), custom_call_target="tpu_custom_call" | custom-call | flops 1610612736 | bytes 8388608 | tf_op jit(solution)/shard_map/pallas_call | solution.py:43
  13.2 1.3 slice_bitcast_fusion.2
  14.5 1.6 collective-permute-start
  16.1 1.1 collective-permute-start.1
  17.2 2.8 %collective-permute-start.2 = (bf16[768,256]{1,0:T(8,128)(2,1)S(1)}, bf16[768,256]{1,0:T(8,128)(2,1)}, u32[]{:S(2)}, u32[]{:S(2)}) collective-permute-start(bf16[768,256]{1,0:T(8,128)(2,1)S(1)} %get-tuple-element.6), channel_id=1, source_target_pairs={{0,12},{4,0},{8,4},{12,8},{1,13},{5,1},{9,5},{13,9},{2,14},{6,2},{... | collective-permute-start | bytes 1179656 | tf_op jit(solution)/shard_map/ppermute | solution.py:17
  20.1 0.8 dynamic_slice.17
  21.1 0.6 constant_dynamic-slice_fusion.1.taps
  21.7 0.8 copy.16
  22.4 2.4 %shard_map.83.refs_4_ = bf16[16,256,256]{2,1,0:T(8,128)(2,1)} custom-call(f32[16,128]{1,0:T(8,128)} %constant_dynamic-slice_fusion.1.taps), custom_call_target="tpu_custom_call" | custom-call | tf_op jit(solution)/shard_map/pallas_call | solution.py:80
  24.9 43.8 %all-gather = s32[4,1,384]{2,1,0:T(1,128)S(1)} all-gather(s32[1,1,384]{2,1,0:T(1,128)S(1)} %reshape.53), channel_id=1, replica_groups=mesh['parts'=2,'seq'=4,'fsdp'=2,'chan'=2] {'seq'}, dimensions={0}, use_global_device_ids=true | all-gather | bytes 7680 | tf_op jit(solution)/shard_map/all_gather | solution.py:203
  68.8 1.5 fusion.4
  70.3 1.6 collective-permute-start.3
  71.9 1.5 compare_convert_fusion.refs_2_
  73.4 5.3 %collective-permute-done.3.refs_1_ = bf16[3,256,256]{2,1,0:T(8,128)(2,1)S(1)} collective-permute-done((bf16[3,256,256]{2,1,0:T(8,128)(2,1)S(1)}, bf16[3,256,256]{2,1,0:T(8,128)(2,1)S(1)}, u32[]{:S(2)}, u32[]{:S(2)}) %collective-permute-start.3) | collective-permute-done | bytes 393248 | tf_op jit(solution)/shard_map/ppermute | solution.py:17
  78.6 0.8 copy-done.3
  79.4 8.0 %shard_map.84 = bf16[4,384,256]{2,1,0:T(8,128)(2,1)} custom-call(s32[2]{0:T(128)} %pad_add_fusion.where, bf16[3,256,256]{2,1,0:T(8,128)(2,1)} %bitcast.43, bf16[3,256,256]{2,1,0:T(8,128)(2,1)} %copy-done.3, bf16[512,1536]{1,0:T(8,128)(2,1)} %compare_convert_fusion.refs_2_, f32[256,16]{1,0:T(8,128)} %bitcast.44, bf16[16,256,256]{2,1,0:T(8,128)(2,1)} %shard_map.83.refs_4_), custom_call_target="tpu_custom_call" | custom-call | flops 1207959552 | bytes 1572864 | tf_op jit(solution)/shard_map/pallas_call | solution.py:144
  87.4 1.9 %slice_bitcast_fusion.4 = (bf16[384,256]{1,0:T(8,128)(2,1)S(1)}, bf16[384,256]{1,0:T(8,128)(2,1)}, bf16[384,256]{1,0:T(8,128)(2,1)S(1)}, bf16[384,1,256]{2,0,1:T(8,128)(2,1)S(1)}) fusion(bf16[4,384,256]{2,1,0:T(8,128)(2,1)} %shard_map.84), kind=kLoop, calls=%fused_computation.14 | loop fusion | bytes 1572864 | tf_op jit(solution)/shard_map/squeeze | solution.py:219
  89.3 0.7 collective-permute-start.4
  90.0 2.4 %collective-permute-start.5 = (bf16[384,256]{1,0:T(8,128)(2,1)}, bf16[384,256]{1,0:T(8,128)(2,1)}, u32[]{:S(2)}, u32[]{:S(2)}) collective-permute-start(bf16[384,256]{1,0:T(8,128)(2,1)} %get-tuple-element.9), channel_id=1, source_target_pairs={{0,8},{4,12},{8,0},{12,4},{1,9},{5,13},{9,1},{13,5},{2,10},{6,14},... | collective-permute-start | bytes 589832 | tf_op jit(solution)/shard_map/ppermute | solution.py:17
  92.6 1.0 collective-permute-start.6
  93.7 10.6 %collective-permute-done.4 = bf16[384,256]{1,0:T(8,128)(2,1)} collective-permute-done((bf16[384,256]{1,0:T(8,128)(2,1)S(1)}, bf16[384,256]{1,0:T(8,128)(2,1)}, u32[]{:S(2)}, u32[]{:S(2)}) %collective-permute-start.4) | collective-permute-done | bytes 196640 | tf_op jit(solution)/shard_map/ppermute | solution.py:17
  104.3 1.1 copy.18
  105.3 3.2 %collective-permute-done.5 = bf16[384,256]{1,0:T(8,128)(2,1)} collective-permute-done((bf16[384,256]{1,0:T(8,128)(2,1)}, bf16[384,256]{1,0:T(8,128)(2,1)}, u32[]{:S(2)}, u32[]{:S(2)}) %collective-permute-start.5) | collective-permute-done | bytes 196640 | tf_op jit(solution)/shard_map/ppermute | solution.py:17
  108.6 1.1 copy.19
  109.7 1.7 collective-permute-start.14
  111.5 1.1 copy.20
  112.7 1.6 collective-permute-start.8
  114.2 0.5 collective-permute-start.11
  114.7 1.8 fusion
  116.6 1.6 collective-permute-start.13
  118.2 1.1 broadcast_in_dim.37
  119.2 0.3 constant_dynamic-update-slice_fusion.6
  119.5 11.2 %collective-permute-done.8 = bf16[384,1024]{0,1:T(8,128)(2,1)} collective-permute-done((bf16[384,1024]{0,1:T(8,128)(2,1)S(1)}, bf16[384,1024]{0,1:T(8,128)(2,1)}, u32[]{:S(2)}, u32[]{:S(2)}) %collective-permute-start.8) | collective-permute-done | bytes 786464 | tf_op jit(solution)/shard_map/ppermute | solution.py:17
  130.7 0.3 broadcast_in_dim.29
  131.2 5.7 %collective-permute-done.14 = bf16[512,1024]{1,0:T(8,128)(2,1)} collective-permute-done((bf16[512,1024]{1,0:T(8,128)(2,1)S(1)}, bf16[512,1024]{1,0:T(8,128)(2,1)}, u32[]{:S(2)}, u32[]{:S(2)}) %collective-permute-start.14) | collective-permute-done | bytes 1048608 | tf_op jit(solution)/shard_map/ppermute | solution.py:17
  136.9 0.5 collective-permute-start.15
  137.5 1.3 constant_dynamic-update-slice_fusion.9
  138.8 1.3 constant_dynamic-update-slice_fusion.8
  140.1 0.2 collective-permute-done.11
  140.3 1.3 constant_dynamic-update-slice_fusion.4
  141.7 0.2 constant_dynamic-update-slice_fusion.7
  141.9 20.7 %collective-permute-done.13 = bf16[512,1024]{1,0:T(8,128)(2,1)S(1)} collective-permute-done((bf16[512,1024]{1,0:T(8,128)(2,1)S(1)}, bf16[512,1024]{1,0:T(8,128)(2,1)S(1)}, u32[]{:S(2)}, u32[]{:S(2)}) %collective-permute-start.13) | collective-permute-done | bytes 1048608 | tf_op jit(solution)/shard_map/ppermute | solution.py:17
  162.8 1.3 constant_dynamic-update-slice_fusion.1
  164.1 20.6 %collective-permute-done.15 = bf16[512,1024]{1,0:T(8,128)(2,1)S(1)} collective-permute-done((bf16[512,1024]{1,0:T(8,128)(2,1)}, bf16[512,1024]{1,0:T(8,128)(2,1)S(1)}, u32[]{:S(2)}, u32[]{:S(2)}) %collective-permute-start.15) | collective-permute-done | bytes 1048608 | tf_op jit(solution)/shard_map/ppermute | solution.py:17
  184.8 4.3 %add_convert_fusion = bf16[384,1024]{1,0:T(8,128)(2,1)} fusion(f32[384,1024]{1,0:T(8,128)S(1)} %fusion, bf16[384,4096]{0,1:T(8,128)(2,1)S(1)} %constant_dynamic-update-slice_fusion.7, bf16[4096,1024]{1,0:T(8,128)(2,1)S(1)} %constant_dynamic-update-slice_fusion), kind=kOutput, calls=%fused_computation.1 | convolution fusion | flops 3222011904 | bytes 13893632 | tf_op jit(solution)/shard_map/dot_general | solution.py:233
  (47 shorter events, 1.3 us)
Async XLA Ops:
  0.0 21.1 %copy-start = (f32[64,128]{1,0:T(8,128)S(1)}, f32[64,128]{1,0:T(8,128)}, u32[]{:S(2)}) copy-start(f32[64,128]{1,0:T(8,128)} %param.13) | copy-start | bytes 98308
  1.3 70.6 %collective-permute-start.10 = (bf16[512,1024]{1,0:T(8,128)(2,1)S(1)}, bf16[512,1024]{1,0:T(8,128)(2,1)S(1)}, u32[]{:S(2)}, u32[]{:S(2)}) collective-permute-start(bf16[512,1024]{1,0:T(8,128)(2,1)S(1)} %constant_dynamic-slice_fusion), channel_id=1, source_target_pairs={{0,4},{4,8},{8,12},{12,0},{1,5},{5,9},{9,13},{13,1},{2,6},{6,10},{... | collective-permute-start | bytes 3145736 | tf_op jit(solution)/shard_map/ppermute | solution.py:17
  5.0 15.1 %copy-start.4 = (f32[3,3,1024]{2,1,0:T(4,128)S(1)}, f32[3,3,1024]{2,1,0:T(4,128)}, u32[]{:S(2)}) copy-start(f32[3,3,1024]{2,1,0:T(4,128)} %param.12) | copy-start | bytes 110596
  13.2 11.7 %copy-start.5 = (s32[384]{0:T(512)S(1)}, s32[384]{0:T(512)}, u32[]{:S(2)}) copy-start(s32[384]{0:T(512)} %param.8) | copy-start | bytes 4612
  14.5 54.2 %collective-permute-start = (bf16[768,256]{1,0:T(8,128)(2,1)S(1)}, bf16[768,256]{1,0:T(8,128)(2,1)}, u32[]{:S(2)}, u32[]{:S(2)}) collective-permute-start(bf16[768,256]{1,0:T(8,128)(2,1)S(1)} %get-tuple-element.5), channel_id=1, source_target_pairs={{0,4},{4,8},{8,12},{12,0},{1,5},{5,9},{9,13},{13,1},{2,6},{6,10},{... | collective-permute-start | bytes 1179656 | tf_op jit(solution)/shard_map/ppermute | solution.py:17
  16.1 52.6 %collective-permute-start.1 = (bf16[768,256]{1,0:T(8,128)(2,1)S(1)}, bf16[768,256]{1,0:T(8,128)(2,1)}, u32[]{:S(2)}, u32[]{:S(2)}) collective-permute-start(bf16[768,256]{1,0:T(8,128)(2,1)S(1)} %get-tuple-element.7), channel_id=1, source_target_pairs={{0,8},{4,12},{8,0},{12,4},{1,9},{5,13},{9,1},{13,5},{2,10},{6,14},... | collective-permute-start | bytes 1179656 | tf_op jit(solution)/shard_map/ppermute | solution.py:17
  17.2 51.6 %collective-permute-start.2 = (bf16[768,256]{1,0:T(8,128)(2,1)S(1)}, bf16[768,256]{1,0:T(8,128)(2,1)}, u32[]{:S(2)}, u32[]{:S(2)}) collective-permute-start(bf16[768,256]{1,0:T(8,128)(2,1)S(1)} %get-tuple-element.6), channel_id=1, source_target_pairs={{0,12},{4,0},{8,4},{12,8},{1,13},{5,1},{9,5},{13,9},{2,14},{6,2},{... | collective-permute-start | bytes 1179656 | tf_op jit(solution)/shard_map/ppermute | solution.py:17
  70.3 8.3 %copy-start.2 = (bf16[768,256]{1,0:T(8,128)(2,1)}, bf16[768,256]{1,0:T(8,128)(2,1)S(1)}, u32[]{:S(2)}) copy-start(bf16[768,256]{1,0:T(8,128)(2,1)S(1)} %fusion.4) | copy-start | bytes 1179652
  70.3 8.3 %collective-permute-start.3 = (bf16[3,256,256]{2,1,0:T(8,128)(2,1)S(1)}, bf16[3,256,256]{2,1,0:T(8,128)(2,1)S(1)}, u32[]{:S(2)}, u32[]{:S(2)}) collective-permute-start(bf16[3,256,256]{2,1,0:T(8,128)(2,1)S(1)} %bitcast.42), channel_id=1, source_target_pairs={{0,16},{16,0},{1,17},{17,1},{2,18},{18,2},{3,19},{19,3},{4,20},{20... | collective-permute-start | bytes 1179656 | tf_op jit(solution)/shard_map/ppermute | solution.py:17
  71.9 37.8 %collective-permute-start.12 = (bf16[512,1024]{1,0:T(8,128)(2,1)S(1)}, bf16[512,1024]{1,0:T(8,128)(2,1)S(1)}, u32[]{:S(2)}, u32[]{:S(2)}) collective-permute-start(bf16[512,1024]{1,0:T(8,128)(2,1)S(1)} %collective-permute-done.10), channel_id=1, source_target_pairs={{0,4},{4,8},{8,12},{12,0},{1,5},{5,9},{9,13},{13,1},{2,6},{6,10},{... | collective-permute-start | bytes 3145736 | tf_op jit(solution)/shard_map/ppermute | solution.py:17
  78.6 0.8 copy-start.3
  89.3 15.0 %collective-permute-start.4 = (bf16[384,256]{1,0:T(8,128)(2,1)S(1)}, bf16[384,256]{1,0:T(8,128)(2,1)}, u32[]{:S(2)}, u32[]{:S(2)}) collective-permute-start(bf16[384,256]{1,0:T(8,128)(2,1)S(1)} %get-tuple-element.10), channel_id=1, source_target_pairs={{0,4},{4,8},{8,12},{12,0},{1,5},{5,9},{9,13},{13,1},{2,6},{6,10},{... | collective-permute-start | bytes 589832 | tf_op jit(solution)/shard_map/ppermute | solution.py:17
  90.0 18.6 %collective-permute-start.5 = (bf16[384,256]{1,0:T(8,128)(2,1)}, bf16[384,256]{1,0:T(8,128)(2,1)}, u32[]{:S(2)}, u32[]{:S(2)}) collective-permute-start(bf16[384,256]{1,0:T(8,128)(2,1)} %get-tuple-element.9), channel_id=1, source_target_pairs={{0,8},{4,12},{8,0},{12,4},{1,9},{5,13},{9,1},{13,5},{2,10},{6,14},... | collective-permute-start | bytes 589832 | tf_op jit(solution)/shard_map/ppermute | solution.py:17
  92.6 18.9 %collective-permute-start.6 = (bf16[384,256]{1,0:T(8,128)(2,1)S(1)}, bf16[384,256]{1,0:T(8,128)(2,1)}, u32[]{:S(2)}, u32[]{:S(2)}) collective-permute-start(bf16[384,256]{1,0:T(8,128)(2,1)S(1)} %get-tuple-element.8), channel_id=1, source_target_pairs={{0,12},{4,0},{8,4},{12,8},{1,13},{5,1},{9,5},{13,9},{2,14},{6,2},{... | collective-permute-start | bytes 589832 | tf_op jit(solution)/shard_map/ppermute | solution.py:17
  109.7 27.1 %collective-permute-start.14 = (bf16[512,1024]{1,0:T(8,128)(2,1)S(1)}, bf16[512,1024]{1,0:T(8,128)(2,1)}, u32[]{:S(2)}, u32[]{:S(2)}) collective-permute-start(bf16[512,1024]{1,0:T(8,128)(2,1)S(1)} %collective-permute-done.12), channel_id=1, source_target_pairs={{0,4},{4,8},{8,12},{12,0},{1,5},{5,9},{9,13},{13,1},{2,6},{6,10},{... | collective-permute-start | bytes 3145736 | tf_op jit(solution)/shard_map/ppermute | solution.py:17
  112.7 18.1 %collective-permute-start.8 = (bf16[384,1024]{0,1:T(8,128)(2,1)S(1)}, bf16[384,1024]{0,1:T(8,128)(2,1)}, u32[]{:S(2)}, u32[]{:S(2)}) collective-permute-start(bf16[384,1024]{0,1:T(8,128)(2,1)S(1)} %bitcast.39), channel_id=1, source_target_pairs={{0,2},{2,0},{1,3},{3,1},{4,6},{6,4},{5,7},{7,5},{8,10},{10,8},{9,1... | collective-permute-start | bytes 2359304 | tf_op jit(solution)/shard_map/ppermute | solution.py:17
  114.2 23.3 %collective-permute-start.7 = (bf16[384,1024]{0,1:T(8,128)(2,1)S(1)}, bf16[384,1024]{0,1:T(8,128)(2,1)}, u32[]{:S(2)}, u32[]{:S(2)}) collective-permute-start(bf16[384,1024]{0,1:T(8,128)(2,1)S(1)} %bitcast.40), channel_id=1, source_target_pairs={{0,1},{1,0},{2,3},{3,2},{4,5},{5,4},{6,7},{7,6},{8,9},{9,8},{10,11... | collective-permute-start | bytes 2359304 | tf_op jit(solution)/shard_map/ppermute | solution.py:17
  114.2 26.1 %collective-permute-start.11 = (bf16[512,1024]{1,0:T(8,128)(2,1)S(1)}, bf16[512,1024]{1,0:T(8,128)(2,1)}, u32[]{:S(2)}, u32[]{:S(2)}) collective-permute-start(bf16[512,1024]{1,0:T(8,128)(2,1)S(1)} %collective-permute-done.10), channel_id=1, source_target_pairs={{0,16},{16,0},{1,17},{17,1},{2,18},{18,2},{3,19},{19,3},{4,20},{20... | collective-permute-start | bytes 3145736 | tf_op jit(solution)/shard_map/ppermute | solution.py:17
  116.6 2.7 %copy-start.1 = (bf16[1024,1024]{1,0:T(8,128)(2,1)S(1)}, bf16[1024,1024]{1,0:T(8,128)(2,1)}, u32[]{:S(2)}) copy-start(bf16[1024,1024]{1,0:T(8,128)(2,1)} %param.15) | copy-start | bytes 6291460
  116.6 46.1 %collective-permute-start.13 = (bf16[512,1024]{1,0:T(8,128)(2,1)S(1)}, bf16[512,1024]{1,0:T(8,128)(2,1)S(1)}, u32[]{:S(2)}, u32[]{:S(2)}) collective-permute-start(bf16[512,1024]{1,0:T(8,128)(2,1)S(1)} %collective-permute-done.12), channel_id=1, source_target_pairs={{0,16},{16,0},{1,17},{17,1},{2,18},{18,2},{3,19},{19,3},{4,20},{20... | collective-permute-start | bytes 3145736 | tf_op jit(solution)/shard_map/ppermute | solution.py:17
  130.7 11.0 %collective-permute-start.9 = (bf16[384,1024]{0,1:T(8,128)(2,1)}, bf16[384,1024]{0,1:T(8,128)(2,1)S(1)}, u32[]{:S(2)}, u32[]{:S(2)}) collective-permute-start(bf16[384,1024]{0,1:T(8,128)(2,1)} %collective-permute-done.8), channel_id=1, source_target_pairs={{0,1},{1,0},{2,3},{3,2},{4,5},{5,4},{6,7},{7,6},{8,9},{9,8},{10,11... | collective-permute-start | bytes 2359304 | tf_op jit(solution)/shard_map/ppermute | solution.py:17
  136.9 47.9 %collective-permute-start.15 = (bf16[512,1024]{1,0:T(8,128)(2,1)}, bf16[512,1024]{1,0:T(8,128)(2,1)S(1)}, u32[]{:S(2)}, u32[]{:S(2)}) collective-permute-start(bf16[512,1024]{1,0:T(8,128)(2,1)} %collective-permute-done.14), channel_id=1, source_target_pairs={{0,16},{16,0},{1,17},{17,1},{2,18},{18,2},{3,19},{19,3},{4,20},{20... | collective-permute-start | bytes 3145736 | tf_op jit(solution)/shard_map/ppermute | solution.py:17

commit v2 on v1

--- a/solution.py
+++ b/solution.py
@@ -9,7 +9,7 @@
 
 FL = 128
 SHORT = 3
-VMEM = 56 * 1024 * 1024
+VMEM = 28 * 1024 * 1024
 
 
 def moved(value, axis, steps):
@@ -17,9 +17,19 @@
     return lax.ppermute(value, axis, [(source, (source + steps) % count) for source in range(count)])
 
 
-def project_kernel(where, rows, cut, gain, w, out, normed):
-    seqs = out.shape[0]
-    mine = out.shape[1] // 3
+def swapped(value, axis, bits):
+    count = lax.axis_size(axis)
+    return lax.ppermute(value, axis, [(source, source ^ bits) for source in range(count)])
+
+
+def after(value, *others):
+    return lax.optimization_barrier((value,) + others)[0]
+
+
+def project_kernel(where, rows, cut, gain, w, *refs):
+    outs, (normed, turned) = refs[:-2], refs[-2:]
+    seqs = len(outs)
+    mine = outs[0].shape[0] // 3
     branch = pl.program_id(0)
 
     @pl.when(branch == 0)
@@ -28,11 +38,11 @@
         scale = lax.rsqrt(jnp.mean(values * values, axis=1, keepdims=True) + 1e-06)
         normed[...] = (cut[...].astype(jnp.float32) * scale * gain[...]).astype(jnp.bfloat16)
 
-    partial = jnp.dot(normed[...], w[0], preferred_element_type=jnp.float32)
-    turned = partial.T.astype(jnp.bfloat16)
-    for dest in range(seqs):
-        slot = lax.rem(dest - where[1] + seqs, seqs)
-        out[slot, pl.ds(branch * mine, mine), :] = turned[dest * mine : (dest + 1) * mine]
+    turned[...] = jnp.dot(normed[...], w[0], preferred_element_type=jnp.float32).T
+    for slot in range(seqs):
+        dest = where[1] ^ slot
+        piece = turned[pl.ds(pl.multiple_of(dest * mine, mine), mine), :]
+        outs[slot][pl.ds(pl.multiple_of(branch * mine, mine), mine), :] = piece.astype(outs[slot].dtype)
 
 
 def project(where, embed, gain, w, seqs, parts):
@@ -40,6 +50,7 @@
     rows = embed.shape[0] // parts
     mine = chans // seqs
     width = embed.shape[1]
+    kinds = [jnp.float32] + [jnp.bfloat16] * (seqs - 1)
     return pl.pallas_call(
         project_kernel,
         grid_spec=pltpu.PrefetchScalarGridSpec(
@@ -51,10 +62,10 @@
                 pl.BlockSpec((1, depth), lambda i, at: (0, at[1])),
                 pl.BlockSpec((1, depth, chans), lambda i, at: (i, 0, 0)),
             ],
-            out_specs=pl.BlockSpec((seqs, branches * mine, rows), lambda i, at: (0, 0, 0)),
-            scratch_shapes=[pltpu.VMEM((rows, depth), jnp.bfloat16)],
-        ),
-        out_shape=jax.ShapeDtypeStruct((seqs, branches * mine, rows), jnp.bfloat16),
+            out_specs=[pl.BlockSpec((branches * mine, rows), lambda i, at: (0, 0))] * seqs,
+            scratch_shapes=[pltpu.VMEM((rows, depth), jnp.bfloat16), pltpu.VMEM((chans, rows), jnp.float32)],
+        ),
+        out_shape=[jax.ShapeDtypeStruct((branches * mine, rows), kind) for kind in kinds],
         compiler_params=pltpu.CompilerParams(vmem_limit_bytes=VMEM),
         cost_estimate=pl.CostEstimate(
             flops=2 * rows * depth * chans * branches,
@@ -85,8 +96,10 @@
 
 
 def mixing_kernel(per_group, parts, where, *refs):
-    tables, (hot, factors, bands, out, wide, gated) = refs[:parts], refs[parts:]
-    seqs, held, lanes = out.shape
+    tables, (hot, factors, bands), rest = refs[:parts], refs[parts : parts + 3], refs[parts + 3 :]
+    outs, (wide, gated) = rest[:-2], rest[-2:]
+    seqs = len(outs)
+    lanes, held = outs[0].shape
     tokens = hot.shape[1]
     blocks = tokens // FL
     rows = tables[0].shape[2]
@@ -127,10 +140,9 @@
         conv = jnp.concatenate([summed[b * per_group : (b + 1) * per_group] for b in range(blocks)], axis=1)
         skip = factors[at, 3 * SHORT : 3 * SHORT + 1]
         gated[at, :] = mixed(0) * (conv + skip * product.astype(jnp.float32))
-    for dest in range(seqs):
-        slot = lax.rem(dest - where[1] + seqs, seqs)
-        part = gated[:, dest * held : (dest + 1) * held]
-        out[slot] = part.T.astype(jnp.bfloat16)
+    for slot in range(seqs):
+        dest = where[1] ^ slot
+        outs[slot][...] = gated[:, pl.ds(pl.multiple_of(dest * held, FL), held)].astype(jnp.bfloat16)
 
 
 def mixing(where, tables, hot, factors, bands, seqs):
@@ -152,13 +164,13 @@
                 pl.BlockSpec((step, factors.shape[1]), lambda i, at: (i, 0)),
                 pl.BlockSpec((step // per_group, 2 * FL, 2 * FL), lambda i, at: (i, 0, 0)),
             ],
-            out_specs=pl.BlockSpec((seqs, held, step), lambda i, at: (0, 0, i)),
+            out_specs=[pl.BlockSpec((step, held), lambda i, at: (i, 0))] * seqs,
             scratch_shapes=[
                 pltpu.VMEM((3, step, tokens), jnp.float32),
                 pltpu.VMEM((step, tokens), jnp.float32),
             ],
         ),
-        out_shape=jax.ShapeDtypeStruct((seqs, held, mine), jnp.bfloat16),
+        out_shape=[jax.ShapeDtypeStruct((mine, held), jnp.bfloat16)] * seqs,
         compiler_params=pltpu.CompilerParams(vmem_limit_bytes=VMEM),
         cost_estimate=pl.CostEstimate(
             flops=2 * 3 * mine * rows * parts * tokens,
@@ -166,6 +178,59 @@
             transcendentals=0,
         ),
     )(where, *tables, hot, factors, bands)
+
+
+def output_kernel(axes, stacks, layout, where, *refs):
+    parts, seqs, fsdps, cores, depth = axes
+    start, arrived, refs = refs[0], refs[1 : 1 + stacks], refs[1 + stacks :]
+    pieces, (out, gated, total) = refs[: len(layout)], refs[len(layout) :]
+    part, seq, fsdp, core = where[0], where[1], where[2], where[3]
+    chans = total.shape[1]
+    mine = chans // seqs
+    for across in range(fsdps):
+        for turn in range(cores):
+            block = lax.rem(fsdp - across + fsdps, fsdps) * cores + lax.rem(core - turn + cores, cores)
+            for hop in range(seqs):
+                row = block * chans + (seq ^ hop) * mine
+                piece = arrived[across * cores + turn][hop * mine : (hop + 1) * mine, :]
+                gated[pl.ds(pl.multiple_of(row, mine), mine), :] = piece
+    for index, (piece, (hop, across, first)) in enumerate(zip(pieces, layout)):
+        size = piece.shape[0]
+        row = lax.rem(seq - hop + seqs, seqs) * depth + first
+        if hop:
+            row = row + lax.rem(part - across + parts, parts) * (depth // parts)
+        term = lax.dot_general(
+            gated[pl.ds(pl.multiple_of(row, size), size), :],
+            piece[...],
+            (((0,), (0,)), ((), ())),
+            preferred_element_type=jnp.float32,
+        )
+        term = term + (total[...] if index else start[...])
+        if index == len(layout) - 1:
+            out[...] = term.astype(out.dtype)
+        else:
+            total[...] = term
+
+
+def output(axes, where, start, stacks, pieces, layout, kind):
+    parts, seqs, fsdps, cores, depth = axes
+    held, chans = start.shape
+    size = sum(piece.shape[0] for piece in pieces)
+    local = pl.BlockSpec(memory_space=pltpu.VMEM)
+    return pl.pallas_call(
+        functools.partial(output_kernel, axes, len(stacks), tuple(layout)),
+        in_specs=[pl.BlockSpec(memory_space=pltpu.SMEM)] + [local] * (1 + len(stacks) + len(pieces)),
+        out_specs=local,
+        scratch_shapes=[
+            pltpu.VMEM((seqs * depth, held), jnp.bfloat16),
+            pltpu.VMEM((held, chans), jnp.float32),
+        ],
+        out_shape=jax.ShapeDtypeStruct((held, chans), kind),
+        compiler_params=pltpu.CompilerParams(vmem_limit_bytes=VMEM),
+        cost_estimate=pl.CostEstimate(
+            flops=2 * held * size * chans, bytes_accessed=2 * size * chans, transcendentals=0
+        ),
+    )(where, start, *stacks, *pieces)
 
 
 def on_device(ids, embed, norm_gain, w_in, short_filter, long_filter, skip_bias, w_out):
@@ -175,36 +240,57 @@
     seqs, parts = lax.axis_size("seq"), lax.axis_size("parts")
     fsdps, cores = lax.axis_size("fsdp"), lax.axis_size("chan")
     seq, part = lax.axis_index("seq"), lax.axis_index("parts")
+    fsdp, core = lax.axis_index("fsdp"), lax.axis_index("chan")
     mine = chans // seqs
     rows = vocab // parts
-    where = jnp.stack([part, seq]).astype(jnp.int32)
-
     depth = w_out.shape[0]
     share = depth // parts
-    ring = lax.dynamic_slice_in_dim(w_out, part * share, share, 0)
-    whole = jnp.zeros((seqs * depth, chans), w_out.dtype)
-    whole = lax.dynamic_update_slice_in_dim(whole, w_out, seq * depth, 0)
-    for hop in range(1, seqs):
-        ring = moved(ring, "seq", 1)
-        owner = lax.rem(seq - hop + seqs, seqs)
-        whole = lax.dynamic_update_slice_in_dim(whole, ring, owner * depth + part * share, 0)
-        for across in range(1, parts):
-            other = moved(ring, "parts", across)
-            source = lax.rem(part - across + parts, parts)
-            whole = lax.dynamic_update_slice_in_dim(whole, other, owner * depth + source * share, 0)
-
-    slots = project(where, embed, norm_gain[None, :], w_in.transpose(1, 0, 2), seqs, parts)
-    total = slots[0].astype(jnp.float32)
-    for hop in range(1, seqs):
-        total = total + moved(slots[hop], "seq", hop).astype(jnp.float32)
-    table = total.astype(jnp.bfloat16).reshape(3, mine, rows)
-    tables = [table] + [moved(table, "parts", across) for across in range(1, parts)]
-
-    every_id = lax.all_gather(ids, "seq", axis=0, tiled=True)
+    cuts = 1
+    cut = share // cuts
+    where = jnp.stack([part, seq, fsdp, core]).astype(jnp.int32)
+
+    rings = [[lax.dynamic_slice_in_dim(w_out, part * share + index * cut, cut, 0) for index in range(cuts)]]
+    swaps = [[]]
+
+    def turn(index, *waits):
+        hop = 1 + max(at for at, ring in enumerate(rings) if len(ring) > index)
+        value = rings[hop - 1][index]
+        if len(rings) == hop:
+            rings.append([])
+        rings[hop].append(moved(after(value, *waits) if waits else value, "seq", 1))
+
+    def swap(hop, index, *waits):
+        value = rings[hop][index]
+        if len(swaps) == hop:
+            swaps.append([])
+        swaps[hop].append([moved(after(value, *waits) if waits else value, "parts", across) for across in range(1, parts)])
+
+    for index in range(cuts):
+        turn(index)
+
+    slots = list(project(where, embed, norm_gain[None, :], w_in.transpose(1, 0, 2), seqs, parts))
+    later = after(ids, slots[-1])
+    near = [ids] + [moved(later, "seq", hop) for hop in range(1, seqs)]
+    turned = jnp.stack(near[::-1] + near[::-1])
+    every_id = lax.dynamic_slice_in_dim(turned, seqs - 1 - seq, seqs, 0).reshape(1, seqs * held)
     place = lax.broadcasted_iota(jnp.int32, (parts, rows, 1), 1)
     order = lax.broadcasted_iota(jnp.int32, (parts, rows, 1), 0)
     place = place + lax.rem(part - order + parts, parts) * rows
-    hot = (place.reshape(vocab, 1) == every_id[None, :]).astype(jnp.bfloat16)
+    hot = (place.reshape(vocab, 1) == every_id).astype(jnp.bfloat16)
+
+    bit = 1
+    while bit < seqs:
+        for slot in range(seqs - bit, 0, -2 * bit):
+            got = swapped(slots[slot].astype(jnp.bfloat16), "seq", bit)
+            if bit == 1 and slot == seqs - 1:
+                got = after(got, *rings[1])
+            slots[slot ^ bit] = slots[slot ^ bit].astype(jnp.float32) + got.astype(jnp.float32)
+        bit *= 2
+    table = slots[0].astype(jnp.bfloat16).reshape(3, mine, rows)
+    for index in range(cuts):
+        swap(1, index)
+    table = after(table, *[one[0] for one in swaps[1]])
+    tables = [table] + [moved(table, "parts", across) for across in range(1, parts)]
 
     first = seq * mine
     short = lax.dynamic_slice_in_dim(short_filter.reshape(3 * SHORT, chans), first, mine, 1)
@@ -212,33 +298,54 @@
     factors = jnp.concatenate([short, skip[None, :], jnp.zeros((6, mine), jnp.float32)], axis=0).T
     groups = long_filter.shape[0] // seqs
     bands = bands_of(lax.dynamic_slice_in_dim(long_filter, seq * groups, groups, 0))
+    cuts = 2
+    size = share // cuts
+    one = rings[1][0]
+    rings[1] = [lax.slice_in_dim(one, index * size, (index + 1) * size, axis=0) for index in range(cuts)]
+    for hop in range(2, seqs - 1):
+        for index in range(cuts):
+            turn(index, *([table] if hop == 2 else []))
+    rings[1] = [one]
     sends = mixing(where, tables, hot, factors, bands, seqs)
 
-    gated = jnp.zeros((held, seqs, mine), jnp.bfloat16)
-    for hop in range(seqs):
-        piece = sends[0] if hop == 0 else moved(sends[hop], "seq", hop)
-        owner = lax.rem(seq - hop + seqs, seqs)
-        gated = lax.dynamic_update_slice(gated, piece[:, None, :], (0, owner, 0))
-    gated = gated.reshape(held, chans)
-    fsdp, core = lax.axis_index("fsdp"), lax.axis_index("chan")
-    columns = jnp.zeros((held, fsdps * cores * chans), jnp.bfloat16)
+    sends = list(after(tuple(sends), rings[2][0]))
+    for hop in range(2, seqs - 1):
+        for index in range(cuts):
+            swap(hop, index)
+    got = [swapped(sends[hop], "seq", hop) for hop in range(1, seqs)]
+    got[0] = after(got[0], *rings[2])
+    got[-1] = after(got[-1], swaps[2][0][0])
+    for index in range(cuts):
+        turn(index, *got)
+        swap(seqs - 1, index)
+    stack = jnp.concatenate([sends[0]] + got, axis=0)
+    stacks = []
     for across in range(fsdps):
-        near = gated if across == 0 else moved(gated, "fsdp", across)
-        x = lax.rem(fsdp - across + fsdps, fsdps)
-        for turn in range(cores):
-            piece = near if turn == 0 else moved(near, "chan", turn)
-            c = lax.rem(core - turn + cores, cores)
-            columns = lax.dynamic_update_slice(columns, piece, (0, (x * cores + c) * chans))
-
-    update = jnp.dot(columns, whole, preferred_element_type=jnp.float32)
-    position = lax.axis_index(("fsdp", "chan"))
+        near = stack if across == 0 else moved(stack, "fsdp", across)
+        if across:
+            near = after(near, swaps[2][1][0])
+        stacks += [near] + [moved(near, "chan", turn) for turn in range(1, cores)]
+
+    position = fsdp * cores + core
     onehot = (ids[:, None] == lax.broadcasted_iota(jnp.int32, (1, vocab), 1)).astype(jnp.bfloat16)
     residual = jnp.dot(
         onehot,
         lax.dynamic_slice_in_dim(embed, position * chans, chans, 1),
         preferred_element_type=jnp.float32,
     )
-    return (residual + update).astype(jnp.bfloat16)
+    axes = (parts, seqs, fsdps, cores, depth)
+    early, late = [(w_out, (0, 0, 0))], []
+    for hop in range(1, seqs):
+        size = share // len(rings[hop])
+        for index, ring in enumerate(rings[hop]):
+            early.append((ring, (hop, 0, index * size)))
+            for across in range(1, parts):
+                last = hop == seqs - 1 and index == len(rings[hop]) - 1
+                (late if last else early).append((swaps[hop][index][across - 1], (hop, across, index * size)))
+    begun = output(axes, where, residual, stacks, *zip(*early), jnp.float32 if late else jnp.bfloat16)
+    if not late:
+        return begun
+    return output(axes, where, begun, stacks, *zip(*late), jnp.bfloat16)
 
 
 def solution(mesh):

time: 190 us -> 155 us (0.82)
  blocking collectives: 43.8 us -> 0 us
  waiting for transfers between devices: 77.5 us -> 90.4 us
  matrix products: 6.14 us -> 1.84 us
  local copies, waits for them, and re-layouts: 18.9 us -> 14.7 us
  starting transfers between devices: 20.2 us -> 23.7 us
    all_gather x1 -> x0, blocking collectives: 43.8 us -> none  [on_device(): every_id = lax.all_gather(ids, 'seq', axis=0, tiled=True)]
    ppermute x0 -> x6, waiting for transfers between devices: none -> 35.5 us  [swapped(): lax.ppermute(value, axis, [(source, source ^ bits) for source in range(co...]
    ppermute x16 -> x17, waiting for transfers between devices: 77.5 us -> 55 us  [moved(): lax.ppermute(value, axis, [(source, (source + steps) % count) for source...]
    pallas_call x0 -> x2, Pallas kernels: none -> 9.9 us  [output(): pl.pallas_call(functools.partial(output_kernel, axes, len(stacks), tuple(...]
    unnamed x18 -> x35, local copies, waits for them, and re-layouts: 0.88 us -> 10.6 us
    ppermute x0 -> x6, starting transfers between devices: none -> 7.26 us  [swapped(): lax.ppermute(value, axis, [(source, source ^ bits) for source in range(co...]
    dynamic_update_slice x15 -> x0, local copies, waits for them, and re-layouts: 6.45 us -> none  [the longest x4 2.92 us: on_device(): lax.dynamic_update_slice(columns, piece, (0, (x * cores + c) * chans))]
    broadcast_in_dim x6 -> x0, local copies, waits for them, and re-layouts: 4.67 us -> none  [the longest x3 3.27 us: on_device(): gated = lax.dynamic_update_slice(gated, piece[:, None, :], (0, owner, 0))]
  transfers between devices with their start and end apart: 16 -> 23, of which waited for: 8 -> 13; matrix products, arithmetic and copies ran while one was open for 12% -> 6% of each run, Pallas kernels for 10% -> 11%
where the time goes in v2:
time: 155 us
  waiting for transfers between devices  90.4 us (58%)
  starting transfers between devices  23.7 us (15%)
  Pallas kernels  20.3 us (13%)
  local copies, waits for them, and re-layouts  14.7 us (9%)
  other arithmetic  3.35 us (2%)
  matrix products  1.84 us (1%)
    ppermute x17, waiting for transfers between devices, moved(): lax.ppermute(value, axis, [(source, (source + steps) % count) for source...  55 us
    ppermute x6, waiting for transfers between devices, swapped(): lax.ppermute(value, axis, [(source, source ^ bits) for source in range(co...  35.5 us
    ppermute x17, starting transfers between devices, moved(): lax.ppermute(value, axis, [(source, (source + steps) % count) for source...  16.5 us
    unnamed x35, local copies, waits for them, and re-layouts  10.6 us
    pallas_call x2, Pallas kernels, output(): pl.pallas_call(functools.partial(output_kernel, axes, len(stacks), tuple(...  9.9 us
    ppermute x6, starting transfers between devices, swapped(): lax.ppermute(value, axis, [(source, source ^ bits) for source in range(co...  7.26 us
    pallas_call x1, Pallas kernels, mixing(): pl.pallas_call(functools.partial(mixing_kernel, per_group, parts), grid_s...  5.19 us
    pallas_call x1, Pallas kernels, project(): pl.pallas_call(project_kernel, grid_spec=pltpu.PrefetchScalarGridSpec(num...  4.82 us
  transfers between devices with their start and end apart: 23, of which 13 were waited for; matrix products, arithmetic and copies ran while one was open for 6% of the time, Pallas kernels for 11%

profile of v2, /device:TPU:0, one launch (start us, length us, event | category | flops | bytes accessed | tf_op | source)
XLA Modules:
  0.0 154.5 jit_solution(7252989076513592128)
XLA Ops:
  0.0 1.3 constant_dynamic-slice_fusion.3
  1.3 3.1 %collective-permute-start.2 = (bf16[512,1024]{1,0:T(8,128)(2,1)S(1)}, bf16[512,1024]{1,0:T(8,128)(2,1)S(1)}, u32[]{:S(2)}, u32[]{:S(2)}) collective-permute-start(bf16[512,1024]{1,0:T(8,128)(2,1)S(1)} %constant_dynamic-slice_fusion.3), channel_id=1, source_target_pairs={{0,4},{4,8},{8,12},{12,0},{1,5},{5,9},{9,13},{13,1},{2,6},{6,10},{... | collective-permute-start | bytes 3145736 | tf_op jit(solution)/shard_map/ppermute | solution.py:17
  4.5 2.2 %copy-done.1 = bf16[512,4096]{1,0:T(8,128)(2,1)S(1)} copy-done((bf16[512,4096]{1,0:T(8,128)(2,1)S(1)}, bf16[512,4096]{1,0:T(8,128)(2,1)}, u32[]{:S(2)}) %copy-start.1) | copy-done | bytes 4194328
  6.7 2.8 %copy-done.2 = bf16[1024,3,1024]{2,0,1:T(8,128)(2,1)S(1)} copy-done((bf16[1024,3,1024]{2,0,1:T(8,128)(2,1)S(1)}, bf16[1024,3,1024]{2,0,1:T(8,128)(2,1)}, u32[]{:S(2)}) %copy-start.2) | copy-done | bytes 6291480
  9.5 4.8 %shard_map.82 = (f32[768,256]{1,0:T(8,128)S(1)}, bf16[768,256]{1,0:T(8,128)(2,1)}, bf16[768,256]{1,0:T(8,128)(2,1)S(1)}, bf16[768,256]{1,0:T(8,128)(2,1)S(1)}) custom-call(s32[4]{0:T(128)S(1)} %pad_add_fusion.where, bf16[512,4096]{1,0:T(8,128)(2,1)S(1)} %copy-done.1, bf16[512,4096]{1,0:T(8,128)(2,1)S(1)} %copy-done.1, f32[1,4096]{1,0:T(1,128)S(1)} %bitcast.19, ...), custom_call_target="tpu_custom_call" | custom-call | flops 1610612736 | bytes 8388608 | tf_op jit(solution)/shard_map/pallas_call | solution.py:54
  14.3 0.9 copy-done.5
  15.2 1.6 %collective-permute-start.1 = (bf16[768,256]{1,0:T(8,128)(2,1)S(1)}, bf16[768,256]{1,0:T(8,128)(2,1)S(1)}, u32[]{:S(2)}, u32[]{:S(2)}) collective-permute-start(bf16[768,256]{1,0:T(8,128)(2,1)S(1)} %get-tuple-element.30), channel_id=1, source_target_pairs={{0,4},{4,0},{8,12},{12,8},{1,5},{5,1},{9,13},{13,9},{2,6},{6,2},{1... | collective-permute-start | bytes 1179656 | tf_op jit(solution)/shard_map/ppermute | solution.py:22
  16.7 2.5 %collective-permute-start.6 = (s32[384]{0:T(512)S(1)}, s32[384]{0:T(512)S(1)}, u32[]{:S(2)}, u32[]{:S(2)}) collective-permute-start(s32[384]{0:T(512)S(1)} %copy-done.13), channel_id=1, source_target_pairs={{0,12},{4,0},{8,4},{12,8},{1,13},{5,1},{9,5},{13,9},{2,14},{6,2},{... | collective-permute-start | bytes 4616 | tf_op jit(solution)/shard_map/ppermute | solution.py:17
  19.2 0.6 collective-permute-start
  19.9 0.8 dynamic_slice.22
  20.8 17.3 %collective-permute-done.1 = bf16[768,256]{1,0:T(8,128)(2,1)S(1)} collective-permute-done((bf16[768,256]{1,0:T(8,128)(2,1)S(1)}, bf16[768,256]{1,0:T(8,128)(2,1)S(1)}, u32[]{:S(2)}, u32[]{:S(2)}) %collective-permute-start.1) | collective-permute-done | bytes 393248 | tf_op jit(solution)/shard_map/ppermute | solution.py:22
  38.1 1.5 collective-permute-start.4
  39.7 0.8 add_convert_fusion.1
  40.5 1.6 %collective-permute-start.3 = (bf16[768,256]{1,0:T(8,128)(2,1)}, bf16[768,256]{1,0:T(8,128)(2,1)}, u32[]{:S(2)}, u32[]{:S(2)}) collective-permute-start(bf16[768,256]{1,0:T(8,128)(2,1)} %add_convert_fusion.1), channel_id=1, source_target_pairs={{0,8},{4,12},{8,0},{12,4},{1,9},{5,13},{9,1},{13,5},{2,10},{6,14},... | collective-permute-start | bytes 1179656 | tf_op jit(solution)/shard_map/ppermute | solution.py:22
  42.1 1.9 %collective-permute-start.8 = (s32[384]{0:T(512)S(1)}, s32[384]{0:T(512)S(1)}, u32[]{:S(2)}, u32[]{:S(2)}) collective-permute-start(s32[384]{0:T(512)S(1)} %copy-done.13), channel_id=1, source_target_pairs={{0,4},{4,8},{8,12},{12,0},{1,5},{5,9},{9,13},{13,1},{2,6},{6,10},{... | collective-permute-start | bytes 4616 | tf_op jit(solution)/shard_map/ppermute | solution.py:17
  44.1 0.4 shard_map.83.refs_4_
  44.5 10.6 %collective-permute-done.8 = s32[384]{0:T(512)S(1)} collective-permute-done((s32[384]{0:T(512)S(1)}, s32[384]{0:T(512)S(1)}, u32[]{:S(2)}, u32[]{:S(2)}) %collective-permute-start.8) | collective-permute-done | bytes 1568 | tf_op jit(solution)/shard_map/ppermute | solution.py:17
  55.2 1.0 fusion.7
  56.2 4.7 %collective-permute-done.3 = bf16[768,256]{1,0:T(8,128)(2,1)} collective-permute-done((bf16[768,256]{1,0:T(8,128)(2,1)}, bf16[768,256]{1,0:T(8,128)(2,1)}, u32[]{:S(2)}, u32[]{:S(2)}) %collective-permute-start.3) | collective-permute-done | bytes 393248 | tf_op jit(solution)/shard_map/ppermute | solution.py:22
  60.9 2.0 %add_convert_fusion = bf16[768,256]{1,0:T(8,128)(2,1)} fusion(bf16[768,256]{1,0:T(8,128)(2,1)} %collective-permute-done.3, f32[768,256]{1,0:T(8,128)S(1)} %copy-done.6, bf16[768,256]{1,0:T(8,128)(2,1)} %collective-permute-done), kind=kLoop, calls=%fused_computation.3 | loop fusion | flops 983040 | bytes 1966080 | tf_op jit(solution)/shard_map/convert_element_type | solution.py:289
  63.3 1.6 %collective-permute-start.5 = (bf16[3,256,256]{2,1,0:T(8,128)(2,1)}, bf16[3,256,256]{2,1,0:T(8,128)(2,1)S(1)}, u32[]{:S(2)}, u32[]{:S(2)}) collective-permute-start(bf16[3,256,256]{2,1,0:T(8,128)(2,1)} %bitcast.16), channel_id=1, source_target_pairs={{0,16},{16,0},{1,17},{17,1},{2,18},{18,2},{3,19},{19,3},{4,20},{20... | collective-permute-start | bytes 1179656 | tf_op jit(solution)/shard_map/ppermute | solution.py:17
  64.9 0.5 collective-permute-start.11
  65.6 14.6 %collective-permute-done.9.refs_8_ = bf16[256,1024]{1,0:T(8,128)(2,1)} collective-permute-done((bf16[256,1024]{1,0:T(8,128)(2,1)}, bf16[256,1024]{1,0:T(8,128)(2,1)}, u32[]{:S(2)}, u32[]{:S(2)}) %collective-permute-start.9) | collective-permute-done | bytes 524320 | tf_op jit(solution)/shard_map/ppermute | solution.py:17
  80.3 1.5 collective-permute-start.14
  81.7 1.0 copy-done.4
  82.7 5.2 %shard_map.84 = (bf16[256,384]{1,0:T(8,128)(2,1)S(1)}, bf16[256,384]{1,0:T(8,128)(2,1)S(1)}, bf16[256,384]{1,0:T(8,128)(2,1)S(1)}, bf16[256,384]{1,0:T(8,128)(2,1)S(1)}) custom-call(s32[4]{0:T(128)S(1)} %pad_add_fusion.where, bf16[3,256,256]{2,1,0:T(8,128)(2,1)S(1)} %bitcast.17, bf16[3,256,256]{2,1,0:T(8,128)(2,1)S(1)} %collective-permute-done.5.refs_1_, ...), custom_call_target="tpu_custom_call" | custom-call | flops 1207959552 | bytes 1572864 | tf_op jit(solution)/shard_map/pallas_call | solution.py:156
  88.1 3.4 %collective-permute-start.12 = (bf16[256,384]{1,0:T(8,128)(2,1)S(1)}, bf16[256,384]{1,0:T(8,128)(2,1)S(1)}, u32[]{:S(2)}, u32[]{:S(2)}) collective-permute-start(bf16[256,384]{1,0:T(8,128)(2,1)S(1)} %get-tuple-element.43), channel_id=1, source_target_pairs={{0,8},{4,12},{8,0},{12,4},{1,9},{5,13},{9,1},{13,5},{2,10},{6,14},... | collective-permute-start | bytes 589832 | tf_op jit(solution)/shard_map/ppermute | solution.py:22
  91.5 0.7 constant_dynamic-update-slice_fusion.3
  92.2 6.5 %collective-permute-done.10 = bf16[256,384]{1,0:T(8,128)(2,1)S(1)} collective-permute-done((bf16[256,384]{1,0:T(8,128)(2,1)S(1)}, bf16[256,384]{1,0:T(8,128)(2,1)S(1)}, u32[]{:S(2)}, u32[]{:S(2)}) %collective-permute-start.10) | collective-permute-done | bytes 196640 | tf_op jit(solution)/shard_map/ppermute | solution.py:22
  98.7 0.7 constant_dynamic-update-slice_fusion.2
  99.4 7.0 %collective-permute-done.12 = bf16[256,384]{1,0:T(8,128)(2,1)S(1)} collective-permute-done((bf16[256,384]{1,0:T(8,128)(2,1)S(1)}, bf16[256,384]{1,0:T(8,128)(2,1)S(1)}, u32[]{:S(2)}, u32[]{:S(2)}) %collective-permute-start.12) | collective-permute-done | bytes 196640 | tf_op jit(solution)/shard_map/ppermute | solution.py:22
  106.4 0.7 constant_dynamic-update-slice_fusion.1
  107.1 0.8 copy-done.7
  107.9 0.7 constant_dynamic-update-slice_fusion.refs_1_
  108.6 1.5 collective-permute-start.16
  110.1 1.4 collective-permute-start.17
  111.6 9.2 %collective-permute-done.17.refs_11_ = bf16[256,1024]{1,0:T(8,128)(2,1)S(1)} collective-permute-done((bf16[256,1024]{1,0:T(8,128)(2,1)}, bf16[256,1024]{1,0:T(8,128)(2,1)S(1)}, u32[]{:S(2)}, u32[]{:S(2)}) %collective-permute-start.17) | collective-permute-done | bytes 524320 | tf_op jit(solution)/shard_map/ppermute | solution.py:17
  120.8 0.8 copy-done.9
  121.6 3.7 %collective-permute-done.16.refs_3_ = bf16[1024,384]{1,0:T(8,128)(2,1)} collective-permute-done((bf16[1024,384]{1,0:T(8,128)(2,1)}, bf16[1024,384]{1,0:T(8,128)(2,1)}, u32[]{:S(2)}, u32[]{:S(2)}) %collective-permute-start.16) | collective-permute-done | bytes 786464 | tf_op jit(solution)/shard_map/ppermute | solution.py:17
  125.3 3.1 %collective-permute-done.19.refs_12_ = bf16[256,1024]{1,0:T(8,128)(2,1)} collective-permute-done((bf16[256,1024]{1,0:T(8,128)(2,1)}, bf16[256,1024]{1,0:T(8,128)(2,1)}, u32[]{:S(2)}, u32[]{:S(2)}) %collective-permute-start.19) | collective-permute-done | bytes 524320 | tf_op jit(solution)/shard_map/ppermute | solution.py:17
  128.4 0.7 collective-permute-start.20
  129.1 6.3 %collective-permute-done.21.refs_14_ = bf16[256,1024]{1,0:T(8,128)(2,1)} collective-permute-done((bf16[256,1024]{1,0:T(8,128)(2,1)}, bf16[256,1024]{1,0:T(8,128)(2,1)}, u32[]{:S(2)}, u32[]{:S(2)}) %collective-permute-start.21) | collective-permute-done | bytes 524320 | tf_op jit(solution)/shard_map/ppermute | solution.py:17
  135.4 0.3 collective-permute-start.22
  135.7 1.8 %fusion.refs_0_ = f32[384,1024]{1,0:T(8,128)S(1)} fusion(bf16[512,4096]{1,0:T(8,128)(2,1)} %cut.1, s32[]{:T(128)S(6)} %select_n.16, s32[384]{0:T(512)S(1)} %copy-done.13), kind=kOutput, calls=%fused_computation.1 | convolution fusion | flops 402849792 | bytes 2622980 | tf_op jit(solution)/shard_map/dot_general | solution.py:331
  137.6 6.1 %collective-permute-done.20.refs_13_ = bf16[256,1024]{1,0:T(8,128)(2,1)} collective-permute-done((bf16[256,1024]{1,0:T(8,128)(2,1)}, bf16[256,1024]{1,0:T(8,128)(2,1)}, u32[]{:S(2)}, u32[]{:S(2)}) %collective-permute-start.20) | collective-permute-done | bytes 524320 | tf_op jit(solution)/shard_map/ppermute | solution.py:17
  143.6 6.5 %shard_map.85.refs_0_ = f32[384,1024]{1,0:T(8,128)S(1)} custom-call(s32[4]{0:T(128)S(1)} %pad_add_fusion.where, f32[384,1024]{1,0:T(8,128)S(1)} %fusion.refs_0_, bf16[1024,384]{1,0:T(8,128)(2,1)} %constant_dynamic-update-slice_fusion.refs_1_, bf16[1024,384]{1,0:T(8,128)(2,1)} %collective-permute-done.15.refs_2_, ...), custom_call_target="tpu_custom_call" | custom-call | flops 3019898880 | bytes 7864320 | tf_op jit(solution)/shard_map/pallas_call | solution.py:220
  150.1 1.0 collective-permute-done.22.refs_5_
  151.1 3.4 %shard_map.86 = bf16[384,1024]{1,0:T(8,128)(2,1)} custom-call(s32[4]{0:T(128)S(1)} %pad_add_fusion.where, f32[384,1024]{1,0:T(8,128)S(1)} %shard_map.85.refs_0_, bf16[1024,384]{1,0:T(8,128)(2,1)} %constant_dynamic-update-slice_fusion.refs_1_, bf16[1024,384]{1,0:T(8,128)(2,1)} %collective-permute-done.15.refs_2_, ...), custom_call_target="tpu_custom_call" | custom-call | flops 201326592 | bytes 524288 | tf_op jit(solution)/shard_map/pallas_call | solution.py:220
  (63 shorter events, 1.5 us)
Async XLA Ops:
  0.0 44.0 %copy-start = (f32[64,128]{1,0:T(8,128)S(1)}, f32[64,128]{1,0:T(8,128)}, u32[]{:S(2)}) copy-start(f32[64,128]{1,0:T(8,128)} %param.13) | copy-start | bytes 98308
  0.0 4.5 %copy-start.11 = (f32[4096]{0:T(1024)S(1)}, f32[4096]{0:T(1024)}, u32[]{:S(2)}) copy-start(f32[4096]{0:T(1024)} %param.10) | copy-start | bytes 49156
  1.3 36.8 %collective-permute-start.2 = (bf16[512,1024]{1,0:T(8,128)(2,1)S(1)}, bf16[512,1024]{1,0:T(8,128)(2,1)S(1)}, u32[]{:S(2)}, u32[]{:S(2)}) collective-permute-start(bf16[512,1024]{1,0:T(8,128)(2,1)S(1)} %constant_dynamic-slice_fusion.3), channel_id=1, source_target_pairs={{0,4},{4,8},{8,12},{12,0},{1,5},{5,9},{9,13},{13,1},{2,6},{6,10},{... | collective-permute-start | bytes 3145736 | tf_op jit(solution)/shard_map/ppermute | solution.py:17
  4.5 2.2 %copy-start.1 = (bf16[512,4096]{1,0:T(8,128)(2,1)S(1)}, bf16[512,4096]{1,0:T(8,128)(2,1)}, u32[]{:S(2)}) copy-start(bf16[512,4096]{1,0:T(8,128)(2,1)} %cut.1) | copy-start | bytes 12582916
  6.7 2.8 %copy-start.2 = (bf16[1024,3,1024]{2,0,1:T(8,128)(2,1)S(1)}, bf16[1024,3,1024]{2,0,1:T(8,128)(2,1)}, u32[]{:S(2)}) copy-start(bf16[1024,3,1024]{2,0,1:T(8,128)(2,1)} %param.11) | copy-start | bytes 18874372
  9.5 7.3 %copy-start.13 = (s32[384]{0:T(512)S(1)}, s32[384]{0:T(512)}, u32[]{:S(2)}) copy-start(s32[384]{0:T(512)} %param.8) | copy-start | bytes 4612
  9.5 10.4 %copy-start.12 = (f32[3,3,1024]{2,1,0:T(4,128)S(1)}, f32[3,3,1024]{2,1,0:T(4,128)}, u32[]{:S(2)}) copy-start(f32[3,3,1024]{2,1,0:T(4,128)} %param.12) | copy-start | bytes 110596
  14.3 0.9 copy-start.5
  15.2 23.0 %collective-permute-start.1 = (bf16[768,256]{1,0:T(8,128)(2,1)S(1)}, bf16[768,256]{1,0:T(8,128)(2,1)S(1)}, u32[]{:S(2)}, u32[]{:S(2)}) collective-permute-start(bf16[768,256]{1,0:T(8,128)(2,1)S(1)} %get-tuple-element.30), channel_id=1, source_target_pairs={{0,4},{4,0},{8,12},{12,8},{1,5},{5,1},{9,13},{13,9},{2,6},{6,2},{1... | collective-permute-start | bytes 1179656 | tf_op jit(solution)/shard_map/ppermute | solution.py:22
  16.7 25.4 %collective-permute-start.6 = (s32[384]{0:T(512)S(1)}, s32[384]{0:T(512)S(1)}, u32[]{:S(2)}, u32[]{:S(2)}) collective-permute-start(s32[384]{0:T(512)S(1)} %copy-done.13), channel_id=1, source_target_pairs={{0,12},{4,0},{8,4},{12,8},{1,13},{5,1},{9,5},{13,9},{2,14},{6,2},{... | collective-permute-start | bytes 4616 | tf_op jit(solution)/shard_map/ppermute | solution.py:17
  19.2 25.3 %collective-permute-start.7 = (s32[384]{0:T(512)S(1)}, s32[384]{0:T(512)S(1)}, u32[]{:S(2)}, u32[]{:S(2)}) collective-permute-start(s32[384]{0:T(512)S(1)} %copy-done.13), channel_id=1, source_target_pairs={{0,8},{4,12},{8,0},{12,4},{1,9},{5,13},{9,1},{13,5},{2,10},{6,14},... | collective-permute-start | bytes 4616 | tf_op jit(solution)/shard_map/ppermute | solution.py:17
  19.2 37.0 %collective-permute-start = (bf16[768,256]{1,0:T(8,128)(2,1)}, bf16[768,256]{1,0:T(8,128)(2,1)}, u32[]{:S(2)}, u32[]{:S(2)}) collective-permute-start(bf16[768,256]{1,0:T(8,128)(2,1)} %get-tuple-element.28), channel_id=1, source_target_pairs={{0,4},{4,0},{8,12},{12,8},{1,5},{5,1},{9,13},{13,9},{2,6},{6,2},{1... | collective-permute-start | bytes 1179656 | tf_op jit(solution)/shard_map/ppermute | solution.py:22
  38.1 25.1 %collective-permute-start.4 = (bf16[512,1024]{1,0:T(8,128)(2,1)S(1)}, bf16[512,1024]{1,0:T(8,128)(2,1)}, u32[]{:S(2)}, u32[]{:S(2)}) collective-permute-start(bf16[512,1024]{1,0:T(8,128)(2,1)S(1)} %collective-permute-done.2.refs_6_), channel_id=1, source_target_pairs={{0,16},{16,0},{1,17},{17,1},{2,18},{18,2},{3,19},{19,3},{4,20},{20... | collective-permute-start | bytes 3145736 | tf_op jit(solution)/shard_map/ppermute | solution.py:17
  40.5 20.4 %collective-permute-start.3 = (bf16[768,256]{1,0:T(8,128)(2,1)}, bf16[768,256]{1,0:T(8,128)(2,1)}, u32[]{:S(2)}, u32[]{:S(2)}) collective-permute-start(bf16[768,256]{1,0:T(8,128)(2,1)} %add_convert_fusion.1), channel_id=1, source_target_pairs={{0,8},{4,12},{8,0},{12,4},{1,9},{5,13},{9,1},{13,5},{2,10},{6,14},... | collective-permute-start | bytes 1179656 | tf_op jit(solution)/shard_map/ppermute | solution.py:22
  42.1 13.1 %collective-permute-start.8 = (s32[384]{0:T(512)S(1)}, s32[384]{0:T(512)S(1)}, u32[]{:S(2)}, u32[]{:S(2)}) collective-permute-start(s32[384]{0:T(512)S(1)} %copy-done.13), channel_id=1, source_target_pairs={{0,4},{4,8},{8,12},{12,0},{1,5},{5,9},{9,13},{13,1},{2,6},{6,10},{... | collective-permute-start | bytes 4616 | tf_op jit(solution)/shard_map/ppermute | solution.py:17
  55.2 5.7 %copy-start.6 = (f32[768,256]{1,0:T(8,128)S(1)}, f32[768,256]{1,0:T(8,128)}, u32[]{:S(2)}) copy-start(f32[768,256]{1,0:T(8,128)} %copy-done.5) | copy-start | bytes 2359300
  63.2 17.0 %collective-permute-start.9 = (bf16[256,1024]{1,0:T(8,128)(2,1)}, bf16[256,1024]{1,0:T(8,128)(2,1)}, u32[]{:S(2)}, u32[]{:S(2)}) collective-permute-start(bf16[256,1024]{1,0:T(8,128)(2,1)} %get-tuple-element.38), channel_id=1, source_target_pairs={{0,4},{4,8},{8,12},{12,0},{1,5},{5,9},{9,13},{13,1},{2,6},{6,10},{... | collective-permute-start | bytes 1572872 | tf_op jit(solution)/shard_map/ppermute | solution.py:17
  63.3 18.5 %collective-permute-start.5 = (bf16[3,256,256]{2,1,0:T(8,128)(2,1)}, bf16[3,256,256]{2,1,0:T(8,128)(2,1)S(1)}, u32[]{:S(2)}, u32[]{:S(2)}) collective-permute-start(bf16[3,256,256]{2,1,0:T(8,128)(2,1)} %bitcast.16), channel_id=1, source_target_pairs={{0,16},{16,0},{1,17},{17,1},{2,18},{18,2},{3,19},{19,3},{4,20},{20... | collective-permute-start | bytes 1179656 | tf_op jit(solution)/shard_map/ppermute | solution.py:17
  64.9 27.3 %collective-permute-start.11 = (bf16[256,1024]{1,0:T(8,128)(2,1)}, bf16[256,1024]{1,0:T(8,128)(2,1)}, u32[]{:S(2)}, u32[]{:S(2)}) collective-permute-start(bf16[256,1024]{1,0:T(8,128)(2,1)} %get-tuple-element.41), channel_id=1, source_target_pairs={{0,4},{4,8},{8,12},{12,0},{1,5},{5,9},{9,13},{13,1},{2,6},{6,10},{... | collective-permute-start | bytes 1572872 | tf_op jit(solution)/shard_map/ppermute | solution.py:17
  80.3 26.8 %collective-permute-start.14 = (bf16[256,1024]{1,0:T(8,128)(2,1)}, bf16[256,1024]{1,0:T(8,128)(2,1)S(1)}, u32[]{:S(2)}, u32[]{:S(2)}) collective-permute-start(bf16[256,1024]{1,0:T(8,128)(2,1)} %collective-permute-done.9.refs_8_), channel_id=1, source_target_pairs={{0,16},{16,0},{1,17},{17,1},{2,18},{18,2},{3,19},{19,3},{4,20},{20... | collective-permute-start | bytes 1572872 | tf_op jit(solution)/shard_map/ppermute | solution.py:17
  81.7 1.0 copy-start.4
  87.9 55.7 %copy-start.3 = (bf16[1024,1024]{1,0:T(8,128)(2,1)S(1)}, bf16[1024,1024]{1,0:T(8,128)(2,1)}, u32[]{:S(2)}) copy-start(bf16[1024,1024]{1,0:T(8,128)(2,1)} %refs_5_.1) | copy-start | bytes 6291460
  88.0 10.7 %collective-permute-start.10 = (bf16[256,384]{1,0:T(8,128)(2,1)S(1)}, bf16[256,384]{1,0:T(8,128)(2,1)S(1)}, u32[]{:S(2)}, u32[]{:S(2)}) collective-permute-start(bf16[256,384]{1,0:T(8,128)(2,1)S(1)} %get-tuple-element.40), channel_id=1, source_target_pairs={{0,4},{4,0},{8,12},{12,8},{1,5},{5,1},{9,13},{13,9},{2,6},{6,2},{1... | collective-permute-start | bytes 589832 | tf_op jit(solution)/shard_map/ppermute | solution.py:22
  88.0 19.1 %collective-permute-start.13 = (bf16[256,384]{1,0:T(8,128)(2,1)S(1)}, bf16[256,384]{1,0:T(8,128)(2,1)S(1)}, u32[]{:S(2)}, u32[]{:S(2)}) collective-permute-start(bf16[256,384]{1,0:T(8,128)(2,1)S(1)} %get-tuple-element.44), channel_id=1, source_target_pairs={{0,12},{4,8},{8,4},{12,0},{1,13},{5,9},{9,5},{13,1},{2,14},{6,10},... | collective-permute-start | bytes 589832 | tf_op jit(solution)/shard_map/ppermute | solution.py:22
  88.1 18.3 %collective-permute-start.12 = (bf16[256,384]{1,0:T(8,128)(2,1)S(1)}, bf16[256,384]{1,0:T(8,128)(2,1)S(1)}, u32[]{:S(2)}, u32[]{:S(2)}) collective-permute-start(bf16[256,384]{1,0:T(8,128)(2,1)S(1)} %get-tuple-element.43), channel_id=1, source_target_pairs={{0,8},{4,12},{8,0},{12,4},{1,9},{5,13},{9,1},{13,5},{2,10},{6,14},... | collective-permute-start | bytes 589832 | tf_op jit(solution)/shard_map/ppermute | solution.py:22
  107.1 0.8 copy-start.7
  108.6 16.7 %collective-permute-start.16 = (bf16[1024,384]{1,0:T(8,128)(2,1)}, bf16[1024,384]{1,0:T(8,128)(2,1)}, u32[]{:S(2)}, u32[]{:S(2)}) collective-permute-start(bf16[1024,384]{1,0:T(8,128)(2,1)} %constant_dynamic-update-slice_fusion.refs_1_), channel_id=1, source_target_pairs={{0,2},{2,0},{1,3},{3,1},{4,6},{6,4},{5,7},{7,5},{8,10},{10,8},{9,1... | collective-permute-start | bytes 2359304 | tf_op jit(solution)/shard_map/ppermute | solution.py:17
  110.1 10.7 %collective-permute-start.17 = (bf16[256,1024]{1,0:T(8,128)(2,1)}, bf16[256,1024]{1,0:T(8,128)(2,1)S(1)}, u32[]{:S(2)}, u32[]{:S(2)}) collective-permute-start(bf16[256,1024]{1,0:T(8,128)(2,1)} %collective-permute-done.11.refs_10_), channel_id=1, source_target_pairs={{0,16},{16,0},{1,17},{17,1},{2,18},{18,2},{3,19},{19,3},{4,20},{20... | collective-permute-start | bytes 1572872 | tf_op jit(solution)/shard_map/ppermute | solution.py:17
  111.5 17.0 %collective-permute-start.19 = (bf16[256,1024]{1,0:T(8,128)(2,1)}, bf16[256,1024]{1,0:T(8,128)(2,1)}, u32[]{:S(2)}, u32[]{:S(2)}) collective-permute-start(bf16[256,1024]{1,0:T(8,128)(2,1)} %collective-permute-done.9.refs_8_), channel_id=1, source_target_pairs={{0,4},{4,8},{8,12},{12,0},{1,5},{5,9},{9,13},{13,1},{2,6},{6,10},{... | collective-permute-start | bytes 1572872 | tf_op jit(solution)/shard_map/ppermute | solution.py:17
  111.5 23.9 %collective-permute-start.21 = (bf16[256,1024]{1,0:T(8,128)(2,1)}, bf16[256,1024]{1,0:T(8,128)(2,1)}, u32[]{:S(2)}, u32[]{:S(2)}) collective-permute-start(bf16[256,1024]{1,0:T(8,128)(2,1)} %collective-permute-done.11.refs_10_), channel_id=1, source_target_pairs={{0,4},{4,8},{8,12},{12,0},{1,5},{5,9},{9,13},{13,1},{2,6},{6,10},{... | collective-permute-start | bytes 1572872 | tf_op jit(solution)/shard_map/ppermute | solution.py:17
  111.6 26.0 %collective-permute-start.15 = (bf16[1024,384]{1,0:T(8,128)(2,1)}, bf16[1024,384]{1,0:T(8,128)(2,1)}, u32[]{:S(2)}, u32[]{:S(2)}) collective-permute-start(bf16[1024,384]{1,0:T(8,128)(2,1)} %constant_dynamic-update-slice_fusion.refs_1_), channel_id=1, source_target_pairs={{0,1},{1,0},{2,3},{3,2},{4,5},{5,4},{6,7},{7,6},{8,9},{9,8},{10,11... | collective-permute-start | bytes 2359304 | tf_op jit(solution)/shard_map/ppermute | solution.py:17
  120.8 0.8 copy-start.9
  125.3 18.3 %collective-permute-start.18 = (bf16[1024,384]{1,0:T(8,128)(2,1)}, bf16[1024,384]{1,0:T(8,128)(2,1)}, u32[]{:S(2)}, u32[]{:S(2)}) collective-permute-start(bf16[1024,384]{1,0:T(8,128)(2,1)} %collective-permute-done.16.refs_3_), channel_id=1, source_target_pairs={{0,1},{1,0},{2,3},{3,2},{4,5},{5,4},{6,7},{7,6},{8,9},{9,8},{10,11... | collective-permute-start | bytes 2359304 | tf_op jit(solution)/shard_map/ppermute | solution.py:17
  128.4 15.2 %collective-permute-start.20 = (bf16[256,1024]{1,0:T(8,128)(2,1)}, bf16[256,1024]{1,0:T(8,128)(2,1)}, u32[]{:S(2)}, u32[]{:S(2)}) collective-permute-start(bf16[256,1024]{1,0:T(8,128)(2,1)} %collective-permute-done.19.refs_12_), channel_id=1, source_target_pairs={{0,16},{16,0},{1,17},{17,1},{2,18},{18,2},{3,19},{19,3},{4,20},{20... | collective-permute-start | bytes 1572872 | tf_op jit(solution)/shard_map/ppermute | solution.py:17
  129.1 14.5 %copy-start.8 = (bf16[256,1024]{1,0:T(8,128)(2,1)S(1)}, bf16[256,1024]{1,0:T(8,128)(2,1)}, u32[]{:S(2)}) copy-start(bf16[256,1024]{1,0:T(8,128)(2,1)} %copy-done.7) | copy-start | bytes 1572868
  129.1 14.5 %copy-start.10 = (bf16[256,1024]{1,0:T(8,128)(2,1)S(1)}, bf16[256,1024]{1,0:T(8,128)(2,1)}, u32[]{:S(2)}) copy-start(bf16[256,1024]{1,0:T(8,128)(2,1)} %copy-done.9) | copy-start | bytes 1572868
  135.4 15.8 %collective-permute-start.22 = (bf16[256,1024]{1,0:T(8,128)(2,1)}, bf16[256,1024]{1,0:T(8,128)(2,1)S(1)}, u32[]{:S(2)}, u32[]{:S(2)}) collective-permute-start(bf16[256,1024]{1,0:T(8,128)(2,1)} %collective-permute-done.21.refs_14_), channel_id=1, source_target_pairs={{0,16},{16,0},{1,17},{17,1},{2,18},{18,2},{3,19},{19,3},{4,20},{20... | collective-permute-start | bytes 1572872 | tf_op jit(solution)/shard_map/ppermute | solution.py:17

commit v3 on v2

--- a/solution.py
+++ b/solution.py
@@ -180,28 +180,37 @@
     )(where, *tables, hot, factors, bands)
 
 
-def output_kernel(axes, stacks, layout, where, *refs):
+def output_kernel(axes, stacks, layout, count, where, *refs):
     parts, seqs, fsdps, cores, depth = axes
     start, arrived, refs = refs[0], refs[1 : 1 + stacks], refs[1 + stacks :]
-    pieces, (out, gated, total) = refs[: len(layout)], refs[len(layout) :]
+    pieces, (out, gated, total) = refs[:count], refs[count:]
     part, seq, fsdp, core = where[0], where[1], where[2], where[3]
     chans = total.shape[1]
     mine = chans // seqs
+    whole = layout[0][2] is None
+    shard = layout[0][1](seq) * depth
     for across in range(fsdps):
         for turn in range(cores):
             block = lax.rem(fsdp - across + fsdps, fsdps) * cores + lax.rem(core - turn + cores, cores)
             for hop in range(seqs):
                 row = block * chans + (seq ^ hop) * mine
-                piece = arrived[across * cores + turn][hop * mine : (hop + 1) * mine, :]
-                gated[pl.ds(pl.multiple_of(row, mine), mine), :] = piece
-    for index, (piece, (hop, across, first)) in enumerate(zip(pieces, layout)):
-        size = piece.shape[0]
-        row = lax.rem(seq - hop + seqs, seqs) * depth + first
-        if hop:
+
+                def place(row=row, hop=hop, at=across * cores + turn):
+                    gated[pl.ds(pl.multiple_of(row, mine), mine), :] = arrived[at][hop * mine : (hop + 1) * mine, :]
+
+                if whole:
+                    place()
+                else:
+                    pl.when((row < shard + depth) & (row + mine > shard))(place)
+    for index, (size, owner, across, first, sources) in enumerate(layout):
+        row = owner(seq) * depth + first
+        if across is not None:
             row = row + lax.rem(part - across + parts, parts) * (depth // parts)
+        found = [pieces[at][offset : offset + size, :] for at, offset in sources]
+        value = found[0] if len(found) == 1 else jnp.where((seq == 0) | (seq == seqs - 1), found[1], found[0])
         term = lax.dot_general(
             gated[pl.ds(pl.multiple_of(row, size), size), :],
-            piece[...],
+            value,
             (((0,), (0,)), ((), ())),
             preferred_element_type=jnp.float32,
         )
@@ -212,13 +221,21 @@
             total[...] = term
 
 
-def output(axes, where, start, stacks, pieces, layout, kind):
+def output(axes, where, start, stacks, layout, kind):
     parts, seqs, fsdps, cores, depth = axes
     held, chans = start.shape
-    size = sum(piece.shape[0] for piece in pieces)
+    pieces, entries = [], []
+    for size, owner, across, first, sources in layout:
+        spots = []
+        for array, offset in sources:
+            if not any(array is piece for piece in pieces):
+                pieces.append(array)
+            spots.append(([array is piece for piece in pieces].index(True), offset))
+        entries.append((size, owner, across, first, tuple(spots)))
+    size = sum(entry[0] for entry in entries)
     local = pl.BlockSpec(memory_space=pltpu.VMEM)
     return pl.pallas_call(
-        functools.partial(output_kernel, axes, len(stacks), tuple(layout)),
+        functools.partial(output_kernel, axes, len(stacks), tuple(entries), len(pieces)),
         in_specs=[pl.BlockSpec(memory_space=pltpu.SMEM)] + [local] * (1 + len(stacks) + len(pieces)),
         out_specs=local,
         scratch_shapes=[
@@ -245,28 +262,30 @@
     rows = vocab // parts
     depth = w_out.shape[0]
     share = depth // parts
-    cuts = 1
-    cut = share // cuts
     where = jnp.stack([part, seq, fsdp, core]).astype(jnp.int32)
-
-    rings = [[lax.dynamic_slice_in_dim(w_out, part * share + index * cut, cut, 0) for index in range(cuts)]]
-    swaps = [[]]
-
-    def turn(index, *waits):
-        hop = 1 + max(at for at, ring in enumerate(rings) if len(ring) > index)
-        value = rings[hop - 1][index]
-        if len(rings) == hop:
-            rings.append([])
-        rings[hop].append(moved(after(value, *waits) if waits else value, "seq", 1))
-
-    def swap(hop, index, *waits):
-        value = rings[hop][index]
-        if len(swaps) == hop:
-            swaps.append([])
-        swaps[hop].append([moved(after(value, *waits) if waits else value, "parts", across) for across in range(1, parts)])
-
-    for index in range(cuts):
-        turn(index)
+    line = seqs == 4
+
+    def along(value, pairs):
+        return lax.ppermute(value, "seq", pairs)
+
+    def swap(value, planes=None):
+        if planes is None:
+            return moved(value, "parts", 1)
+        pairs = [(p * seqs + s, (p + 1) % parts * seqs + s) for p in range(parts) for s in planes]
+        return lax.ppermute(value, ("parts", "seq"), pairs)
+
+    share_of = lax.dynamic_slice_in_dim(w_out, part * share, share, 0)
+    layout = [(depth, lambda s: s, None, 0, [(w_out, 0)])]
+    last = []
+    inner, outer, middle, outward = (1, 2), (0, 3), [(1, 2), (2, 1)], [(1, 0), (2, 3)]
+    if line:
+        first_near = along(share_of, [(s, s ^ 1) for s in range(seqs)])
+        first_mid = along(share_of, middle)
+    else:
+        ring, nears = share_of, []
+        for hop in range(1, seqs):
+            ring = moved(ring, "seq", 1)
+            nears.append((ring, swap(ring)))
 
     slots = list(project(where, embed, norm_gain[None, :], w_in.transpose(1, 0, 2), seqs, parts))
     later = after(ids, slots[-1])
@@ -277,20 +296,27 @@
     order = lax.broadcasted_iota(jnp.int32, (parts, rows, 1), 0)
     place = place + lax.rem(part - order + parts, parts) * rows
     hot = (place.reshape(vocab, 1) == every_id).astype(jnp.bfloat16)
-
     bit = 1
     while bit < seqs:
         for slot in range(seqs - bit, 0, -2 * bit):
             got = swapped(slots[slot].astype(jnp.bfloat16), "seq", bit)
-            if bit == 1 and slot == seqs - 1:
-                got = after(got, *rings[1])
+            if line and bit == 1 and slot == seqs - 1:
+                got = after(got, first_near, first_mid, *near[1:])
+                pass
             slots[slot ^ bit] = slots[slot ^ bit].astype(jnp.float32) + got.astype(jnp.float32)
         bit *= 2
+        if line and bit == 2:
+            pass
     table = slots[0].astype(jnp.bfloat16).reshape(3, mine, rows)
-    for index in range(cuts):
-        swap(1, index)
-    table = after(table, *[one[0] for one in swaps[1]])
+    if line:
+        near_y = swap(first_near)
+        table = after(table, near_y)
     tables = [table] + [moved(table, "parts", across) for across in range(1, parts)]
+    if line:
+        pass
+        cross = along(after(first_near, table), middle)
+        out_second = along(after(first_mid, table), outward)
+        mid_y = swap(after(first_mid, tables[1]), inner)
 
     first = seq * mine
     short = lax.dynamic_slice_in_dim(short_filter.reshape(3 * SHORT, chans), first, mine, 1)
@@ -298,32 +324,26 @@
     factors = jnp.concatenate([short, skip[None, :], jnp.zeros((6, mine), jnp.float32)], axis=0).T
     groups = long_filter.shape[0] // seqs
     bands = bands_of(lax.dynamic_slice_in_dim(long_filter, seq * groups, groups, 0))
-    cuts = 2
-    size = share // cuts
-    one = rings[1][0]
-    rings[1] = [lax.slice_in_dim(one, index * size, (index + 1) * size, axis=0) for index in range(cuts)]
-    for hop in range(2, seqs - 1):
-        for index in range(cuts):
-            turn(index, *([table] if hop == 2 else []))
-    rings[1] = [one]
     sends = mixing(where, tables, hot, factors, bands, seqs)
-
-    sends = list(after(tuple(sends), rings[2][0]))
-    for hop in range(2, seqs - 1):
-        for index in range(cuts):
-            swap(hop, index)
+    if line:
+        pass
+        second_y = swap(out_second, outer)
+        cross_y = swap(cross, inner)
+
     got = [swapped(sends[hop], "seq", hop) for hop in range(1, seqs)]
-    got[0] = after(got[0], *rings[2])
-    got[-1] = after(got[-1], swaps[2][0][0])
-    for index in range(cuts):
-        turn(index, *got)
-        swap(seqs - 1, index)
+    if line:
+        pass
+        got[0] = after(got[0], out_second, cross)
+        pieces = [lax.slice_in_dim(cross, i * (share // 1), (i + 1) * (share // 1), axis=0) for i in range(1)] if 1 > 1 else [cross]
+        out_third = [along(after(piece, got[0]), outward) for piece in pieces]
+        third_y = [swap(piece, outer) for piece in out_third]
     stack = jnp.concatenate([sends[0]] + got, axis=0)
     stacks = []
     for across in range(fsdps):
         near = stack if across == 0 else moved(stack, "fsdp", across)
-        if across:
-            near = after(near, swaps[2][1][0])
+        if line and across:
+            pass
+            near = after(near, second_y, cross_y, mid_y, *out_third)
         stacks += [near] + [moved(near, "chan", turn) for turn in range(1, cores)]
 
     position = fsdp * cores + core
@@ -334,18 +354,24 @@
         preferred_element_type=jnp.float32,
     )
     axes = (parts, seqs, fsdps, cores, depth)
-    early, late = [(w_out, (0, 0, 0))], []
-    for hop in range(1, seqs):
-        size = share // len(rings[hop])
-        for index, ring in enumerate(rings[hop]):
-            early.append((ring, (hop, 0, index * size)))
-            for across in range(1, parts):
-                last = hop == seqs - 1 and index == len(rings[hop]) - 1
-                (late if last else early).append((swaps[hop][index][across - 1], (hop, across, index * size)))
-    begun = output(axes, where, residual, stacks, *zip(*early), jnp.float32 if late else jnp.bfloat16)
-    if not late:
+    if line:
+        second = lambda s: jnp.where(s < 2, 2, 1)
+        third = lambda s: jnp.where(s < 2, 3, 0)
+        layout += [(share, lambda s: s ^ 1, 0, 0, [(first_near, 0)]), (share, lambda s: s ^ 1, 1, 0, [(near_y, 0)])]
+        layout += [(share, second, 0, 0, [(first_mid, 0), (out_second, 0)]), (share, second, 1, 0, [(mid_y, 0), (second_y, 0)])]
+        size = share // len(out_third)
+        for index, (piece, piece_y) in enumerate(zip(out_third, third_y)):
+            layout.append((size, third, 0, index * size, [(cross, index * size), (piece, 0)]))
+            (last if index == len(out_third) - 1 else layout).append((size, third, 1, index * size, [(cross_y, index * size), (piece_y, 0)]))
+        pass
+    else:
+        for hop, (one, other) in enumerate(nears, 1):
+            owner = functools.partial(lambda hop, s: lax.rem(s - hop + seqs, seqs), hop)
+            layout += [(share, owner, 0, 0, [(one, 0)]), (share, owner, 1, 0, [(other, 0)])]
+    begun = output(axes, where, residual, stacks, layout, jnp.float32 if last else jnp.bfloat16)
+    if not last:
         return begun
-    return output(axes, where, begun, stacks, *zip(*late), jnp.bfloat16)
+    return output(axes, where, begun, stacks, last, jnp.bfloat16)
 
 
 def solution(mesh):

time: 155 us -> 152 us (0.981)
  waiting for transfers between devices: 90.4 us -> 72.3 us
  starting transfers between devices: 23.7 us -> 40.9 us
  local copies, waits for them, and re-layouts: 14.7 us -> 12.8 us
    ppermute x17 -> x8, waiting for transfers between devices: 55 us -> 29 us  [moved(): lax.ppermute(value, axis, [(source, (source + steps) % count) for source...]
    ppermute x0 -> x9, starting transfers between devices: none -> 16.3 us  [the longest x4 8.28 us: swap(): return lax.ppermute(value, ('parts', 'seq'), pairs)]
    ppermute x0 -> x9, waiting for transfers between devices: none -> 15.7 us  [the longest x4 14.5 us: swap(): return lax.ppermute(value, ('parts', 'seq'), pairs)]
    ppermute x6, waiting for transfers between devices: 35.5 us -> 27.6 us  [swapped(): lax.ppermute(value, axis, [(source, source ^ bits) for source in range(co...]
    ppermute x6, starting transfers between devices: 7.26 us -> 10.2 us  [swapped(): lax.ppermute(value, axis, [(source, source ^ bits) for source in range(co...]
    ppermute x17 -> x8, starting transfers between devices: 16.5 us -> 14.4 us  [moved(): lax.ppermute(value, axis, [(source, (source + steps) % count) for source...]
    unnamed x35 -> x39, local copies, waits for them, and re-layouts: 10.6 us -> 9.46 us
  transfers between devices with their start and end apart: 23 -> 23, of which waited for: 13 -> 10; matrix products, arithmetic and copies ran while one was open for 6% -> 4% of each run, Pallas kernels for 11% -> 11%
where the time goes in v3:
time: 152 us; the launch traced here: 151 us
  waiting for transfers between devices  72.3 us (48%)
  starting transfers between devices  40.9 us (27%)
  Pallas kernels  20.5 us (13%)
  local copies, waits for them, and re-layouts  12.8 us (8%)
  other arithmetic  2.67 us (2%)
  matrix products  1.99 us (1%)
    ppermute x8, waiting for transfers between devices, moved(): lax.ppermute(value, axis, [(source, (source + steps) % count) for source...  29 us
    ppermute x6, waiting for transfers between devices, swapped(): lax.ppermute(value, axis, [(source, source ^ bits) for source in range(co...  27.6 us
    ppermute x4, waiting for transfers between devices, swap(): return lax.ppermute(value, ('parts', 'seq'), pairs)  14.5 us
    ppermute x8, starting transfers between devices, moved(): lax.ppermute(value, axis, [(source, (source + steps) % count) for source...  14.4 us
    pallas_call x2, Pallas kernels, output(): pl.pallas_call(functools.partial(output_kernel, axes, len(stacks), tuple(...  10.2 us
    ppermute x6, starting transfers between devices, swapped(): lax.ppermute(value, axis, [(source, source ^ bits) for source in range(co...  10.2 us
    unnamed x39, local copies, waits for them, and re-layouts  9.46 us
    ppermute x4, starting transfers between devices, swap(): return lax.ppermute(value, ('parts', 'seq'), pairs)  8.28 us
  transfers between devices with their start and end apart: 23, of which 10 were waited for; matrix products, arithmetic and copies ran while one was open for 4% of the time, Pallas kernels for 11%

profile of v3, /device:TPU:0, one launch (start us, length us, event | category | flops | bytes accessed | tf_op | source)
XLA Modules:
  0.0 151.4 jit_solution(7311074220104207829)
XLA Ops:
  0.0 2.3 %constant_dynamic-slice_fusion.3 = bf16[512,1024]{1,0:T(8,128)(2,1)} fusion(bf16[1024,1024]{1,0:T(8,128)(2,1)} %refs_5_.1, s32[]{:T(128)S(6)} %select_n.17), kind=kLoop, calls=%fused_computation.21 | loop fusion | bytes 2097156 | tf_op jit(solution)/shard_map/dynamic_slice | solution.py:277
  2.3 3.0 %collective-permute-start.2 = (bf16[512,1024]{1,0:T(8,128)(2,1)}, bf16[512,1024]{1,0:T(8,128)(2,1)}, u32[]{:S(2)}, u32[]{:S(2)}) collective-permute-start(bf16[512,1024]{1,0:T(8,128)(2,1)} %constant_dynamic-slice_fusion.3), channel_id=1, source_target_pairs={{0,4},{4,0},{8,12},{12,8},{1,5},{5,1},{9,13},{13,9},{2,6},{6,2},{1... | collective-permute-start | bytes 3145736 | tf_op jit(solution)/shard_map/ppermute | solution.py:269
  5.3 0.7 collective-permute-start.3
  6.0 0.1 pad_add_fusion.where
  6.1 2.2 %copy-done.1 = bf16[512,4096]{1,0:T(8,128)(2,1)S(1)} copy-done((bf16[512,4096]{1,0:T(8,128)(2,1)S(1)}, bf16[512,4096]{1,0:T(8,128)(2,1)}, u32[]{:S(2)}) %copy-start.1) | copy-done | bytes 4194328
  8.3 2.8 %copy-done.2 = bf16[1024,3,1024]{2,0,1:T(8,128)(2,1)S(1)} copy-done((bf16[1024,3,1024]{2,0,1:T(8,128)(2,1)S(1)}, bf16[1024,3,1024]{2,0,1:T(8,128)(2,1)}, u32[]{:S(2)}) %copy-start.2) | copy-done | bytes 6291480
  11.1 4.7 %shard_map.82 = (f32[768,256]{1,0:T(8,128)S(1)}, bf16[768,256]{1,0:T(8,128)(2,1)}, bf16[768,256]{1,0:T(8,128)(2,1)S(1)}, bf16[768,256]{1,0:T(8,128)(2,1)S(1)}) custom-call(s32[4]{0:T(128)S(1)} %pad_add_fusion.where, bf16[512,4096]{1,0:T(8,128)(2,1)S(1)} %copy-done.1, bf16[512,4096]{1,0:T(8,128)(2,1)S(1)} %copy-done.1, f32[1,4096]{1,0:T(1,128)S(1)} %bitcast.19, ...), custom_call_target="tpu_custom_call" | custom-call | flops 1610612736 | bytes 8388608 | tf_op jit(solution)/shard_map/pallas_call | solution.py:54
  15.8 2.5 %collective-permute-start.6 = (s32[384]{0:T(512)S(1)}, s32[384]{0:T(512)S(1)}, u32[]{:S(2)}, u32[]{:S(2)}) collective-permute-start(s32[384]{0:T(512)S(1)} %copy-done.15), channel_id=1, source_target_pairs={{0,12},{4,0},{8,4},{12,8},{1,13},{5,1},{9,5},{13,9},{2,14},{6,2},{... | collective-permute-start | bytes 4616 | tf_op jit(solution)/shard_map/ppermute | solution.py:17
  18.3 3.3 %collective-permute-start.5 = (s32[384]{0:T(512)S(1)}, s32[384]{0:T(512)S(1)}, u32[]{:S(2)}, u32[]{:S(2)}) collective-permute-start(s32[384]{0:T(512)S(1)} %copy-done.15), channel_id=1, source_target_pairs={{0,8},{4,12},{8,0},{12,4},{1,9},{5,13},{9,1},{13,5},{2,10},{6,14},... | collective-permute-start | bytes 4616 | tf_op jit(solution)/shard_map/ppermute | solution.py:17
  21.8 7.9 %collective-permute-done.6 = s32[384]{0:T(512)S(1)} collective-permute-done((s32[384]{0:T(512)S(1)}, s32[384]{0:T(512)S(1)}, u32[]{:S(2)}, u32[]{:S(2)}) %collective-permute-start.6) | collective-permute-done | bytes 1568 | tf_op jit(solution)/shard_map/ppermute | solution.py:17
  29.6 3.9 %collective-permute-start.4 = (s32[384]{0:T(512)S(1)}, s32[384]{0:T(512)S(1)}, u32[]{:S(2)}, u32[]{:S(2)}) collective-permute-start(s32[384]{0:T(512)S(1)} %copy-done.15), channel_id=1, source_target_pairs={{0,4},{4,8},{8,12},{12,0},{1,5},{5,9},{9,13},{13,1},{2,6},{6,10},{... | collective-permute-start | bytes 4616 | tf_op jit(solution)/shard_map/ppermute | solution.py:17
  33.6 1.5 %collective-permute-start.8 = (bf16[512,1024]{1,0:T(8,128)(2,1)}, bf16[512,1024]{1,0:T(8,128)(2,1)}, u32[]{:S(2)}, u32[]{:S(2)}) collective-permute-start(bf16[512,1024]{1,0:T(8,128)(2,1)} %collective-permute-done.2.refs_6_), channel_id=1, source_target_pairs={{0,16},{16,0},{1,17},{17,1},{2,18},{18,2},{3,19},{19,3},{4,20},{20... | collective-permute-start | bytes 3145736 | tf_op jit(solution)/shard_map/ppermute | solution.py:17
  35.1 5.5 %collective-permute-done.4 = s32[384]{0:T(512)S(1)} collective-permute-done((s32[384]{0:T(512)S(1)}, s32[384]{0:T(512)S(1)}, u32[]{:S(2)}, u32[]{:S(2)}) %collective-permute-start.4) | collective-permute-done | bytes 1568 | tf_op jit(solution)/shard_map/ppermute | solution.py:17
  40.6 1.0 add_convert_fusion.1
  41.5 0.5 collective-permute-start.7
  42.1 0.8 dynamic_slice.22
  43.0 0.1 copy.12
  43.1 0.4 shard_map.83.refs_4_
  43.5 7.4 %collective-permute-done = bf16[768,256]{1,0:T(8,128)(2,1)} collective-permute-done((bf16[768,256]{1,0:T(8,128)(2,1)}, bf16[768,256]{1,0:T(8,128)(2,1)}, u32[]{:S(2)}, u32[]{:S(2)}) %collective-permute-start) | collective-permute-done | bytes 393248 | tf_op jit(solution)/shard_map/ppermute | solution.py:22
  50.9 8.9 %collective-permute-done.7 = bf16[768,256]{1,0:T(8,128)(2,1)} collective-permute-done((bf16[768,256]{1,0:T(8,128)(2,1)}, bf16[768,256]{1,0:T(8,128)(2,1)}, u32[]{:S(2)}, u32[]{:S(2)}) %collective-permute-start.7) | collective-permute-done | bytes 393248 | tf_op jit(solution)/shard_map/ppermute | solution.py:22
  59.8 1.2 add_convert_fusion
  61.0 1.3 collective-permute-start.11
  62.3 1.7 %collective-permute-start.12 = (bf16[512,1024]{1,0:T(8,128)(2,1)}, bf16[512,1024]{1,0:T(8,128)(2,1)}, u32[]{:S(2)}, u32[]{:S(2)}) collective-permute-start(bf16[512,1024]{1,0:T(8,128)(2,1)} %collective-permute-done.2.refs_6_), channel_id=1, source_target_pairs={{4,8},{8,4},{5,9},{9,5},{6,10},{10,6},{7,11},{11,7},{20,24},{24,20... | collective-permute-start | bytes 3145736 | tf_op jit(solution)/shard_map/ppermute | solution.py:269
  64.1 1.6 %collective-permute-start.9 = (bf16[3,256,256]{2,1,0:T(8,128)(2,1)S(1)}, bf16[3,256,256]{2,1,0:T(8,128)(2,1)S(1)}, u32[]{:S(2)}, u32[]{:S(2)}) collective-permute-start(bf16[3,256,256]{2,1,0:T(8,128)(2,1)S(1)} %bitcast.16), channel_id=1, source_target_pairs={{0,16},{16,0},{1,17},{17,1},{2,18},{18,2},{3,19},{19,3},{4,20},{20... | collective-permute-start | bytes 1179656 | tf_op jit(solution)/shard_map/ppermute | solution.py:17
  65.7 0.3 compare_convert_fusion.refs_2_
  66.0 5.9 %collective-permute-done.9.refs_1_ = bf16[3,256,256]{2,1,0:T(8,128)(2,1)S(1)} collective-permute-done((bf16[3,256,256]{2,1,0:T(8,128)(2,1)S(1)}, bf16[3,256,256]{2,1,0:T(8,128)(2,1)S(1)}, u32[]{:S(2)}, u32[]{:S(2)}) %collective-permute-start.9) | collective-permute-done | bytes 393248 | tf_op jit(solution)/shard_map/ppermute | solution.py:17
  71.9 5.1 %shard_map.84 = (bf16[256,384]{1,0:T(8,128)(2,1)S(1)}, bf16[256,384]{1,0:T(8,128)(2,1)S(1)}, bf16[256,384]{1,0:T(8,128)(2,1)S(1)}, bf16[256,384]{1,0:T(8,128)(2,1)S(1)}) custom-call(s32[4]{0:T(128)S(1)} %pad_add_fusion.where, bf16[3,256,256]{2,1,0:T(8,128)(2,1)S(1)} %bitcast.17, bf16[3,256,256]{2,1,0:T(8,128)(2,1)S(1)} %collective-permute-done.9.refs_1_, ...), custom_call_target="tpu_custom_call" | custom-call | flops 1207959552 | bytes 1572864 | tf_op jit(solution)/shard_map/pallas_call | solution.py:156
  77.0 5.0 %collective-permute-start.10 = (bf16[256,384]{1,0:T(8,128)(2,1)S(1)}, bf16[256,384]{1,0:T(8,128)(2,1)S(1)}, u32[]{:S(2)}, u32[]{:S(2)}) collective-permute-start(bf16[256,384]{1,0:T(8,128)(2,1)S(1)} %get-tuple-element.30), channel_id=1, source_target_pairs={{0,4},{4,0},{8,12},{12,8},{1,5},{5,1},{9,13},{13,9},{2,6},{6,2},{1... | collective-permute-start | bytes 589832 | tf_op jit(solution)/shard_map/ppermute | solution.py:22
  82.0 0.5 collective-permute-start.13
  82.5 0.7 collective-permute-start.19
  83.3 4.2 %collective-permute-done.10 = bf16[256,384]{1,0:T(8,128)(2,1)S(1)} collective-permute-done((bf16[256,384]{1,0:T(8,128)(2,1)S(1)}, bf16[256,384]{1,0:T(8,128)(2,1)S(1)}, u32[]{:S(2)}, u32[]{:S(2)}) %collective-permute-start.10) | collective-permute-done | bytes 196640 | tf_op jit(solution)/shard_map/ppermute | solution.py:22
  87.5 4.2 %collective-permute-start.14 = (bf16[256,384]{1,0:T(8,128)(2,1)S(1)}, bf16[256,384]{1,0:T(8,128)(2,1)S(1)}, u32[]{:S(2)}, u32[]{:S(2)}) collective-permute-start(bf16[256,384]{1,0:T(8,128)(2,1)S(1)} %get-tuple-element.35), channel_id=1, source_target_pairs={{0,12},{4,8},{8,4},{12,0},{1,13},{5,9},{9,5},{13,1},{2,14},{6,10},... | collective-permute-start | bytes 589832 | tf_op jit(solution)/shard_map/ppermute | solution.py:22
  91.7 1.3 collective-permute-start.20
  93.0 3.4 %collective-permute-start.17 = (bf16[512,1024]{1,0:T(8,128)(2,1)}, bf16[512,1024]{1,0:T(8,128)(2,1)S(1)}, u32[]{:S(2)}, u32[]{:S(2)}) collective-permute-start(bf16[512,1024]{1,0:T(8,128)(2,1)} %collective-permute-done.11.refs_9_), channel_id=1, source_target_pairs={{0,16},{12,28},{16,0},{28,12},{1,17},{13,29},{17,1},{29,13},{2,18}... | collective-permute-start | bytes 3145736 | tf_op jit(solution)/shard_map/ppermute | solution.py:275
  96.4 7.1 %collective-permute-done.13 = bf16[256,384]{1,0:T(8,128)(2,1)S(1)} collective-permute-done((bf16[256,384]{1,0:T(8,128)(2,1)S(1)}, bf16[256,384]{1,0:T(8,128)(2,1)S(1)}, u32[]{:S(2)}, u32[]{:S(2)}) %collective-permute-start.13) | collective-permute-done | bytes 196640 | tf_op jit(solution)/shard_map/ppermute | solution.py:22
  103.5 0.7 collective-permute-start.18
  104.4 1.6 %collective-permute-start.16 = (bf16[1024,384]{1,0:T(8,128)(2,1)S(1)}, bf16[1024,384]{1,0:T(8,128)(2,1)}, u32[]{:S(2)}, u32[]{:S(2)}) collective-permute-start(bf16[1024,384]{1,0:T(8,128)(2,1)S(1)} %constant_dynamic-update-slice_fusion.refs_1_), channel_id=1, source_target_pairs={{0,2},{2,0},{1,3},{3,1},{4,6},{6,4},{5,7},{7,5},{8,10},{10,8},{9,1... | collective-permute-start | bytes 2359304 | tf_op jit(solution)/shard_map/ppermute | solution.py:17
  105.9 1.0 copy-done.7
  106.9 9.7 %collective-permute-done.16.refs_3_ = bf16[1024,384]{1,0:T(8,128)(2,1)} collective-permute-done((bf16[1024,384]{1,0:T(8,128)(2,1)S(1)}, bf16[1024,384]{1,0:T(8,128)(2,1)}, u32[]{:S(2)}, u32[]{:S(2)}) %collective-permute-start.16) | collective-permute-done | bytes 786464 | tf_op jit(solution)/shard_map/ppermute | solution.py:17
  116.7 1.0 copy-done.9
  117.7 1.1 copy-done.11
  118.8 1.2 collective-permute-done.20.refs_13_
  120.0 3.4 %collective-permute-start.22 = (bf16[512,1024]{1,0:T(8,128)(2,1)}, bf16[512,1024]{1,0:T(8,128)(2,1)}, u32[]{:S(2)}, u32[]{:S(2)}) collective-permute-start(bf16[512,1024]{1,0:T(8,128)(2,1)} %collective-permute-done.20.refs_13_), channel_id=1, source_target_pairs={{0,16},{12,28},{16,0},{28,12},{1,17},{13,29},{17,1},{29,13},{2,18}... | collective-permute-start | bytes 3145736 | tf_op jit(solution)/shard_map/ppermute | solution.py:275
  123.4 2.0 %fusion.refs_0_ = f32[384,1024]{1,0:T(8,128)S(1)} fusion(bf16[512,4096]{1,0:T(8,128)(2,1)} %cut.1, s32[]{:T(128)S(6)} %select_n.16, s32[384]{0:T(512)S(1)} %copy-done.15), kind=kOutput, calls=%fused_computation.1 | convolution fusion | flops 402849792 | bytes 2622980 | tf_op jit(solution)/shard_map/dot_general | solution.py:351
  125.5 1.2 copy-done.10
  126.7 6.6 %shard_map.85.refs_0_ = f32[384,1024]{1,0:T(8,128)S(1)} custom-call(s32[4]{0:T(128)S(1)} %pad_add_fusion.where, f32[384,1024]{1,0:T(8,128)S(1)} %fusion.refs_0_, bf16[1024,384]{1,0:T(8,128)(2,1)S(1)} %constant_dynamic-update-slice_fusion.refs_1_, bf16[1024,384]{1,0:T(8,128)(2,1)} %collective-permute-done.15.refs_2_, ...), custom_call_target="tpu_custom_call" | custom-call | flops 2818572288 | bytes 7340032 | tf_op jit(solution)/shard_map/pallas_call | solution.py:237
  133.3 14.5 %collective-permute-done.22.refs_6_ = bf16[512,1024]{1,0:T(8,128)(2,1)} collective-permute-done((bf16[512,1024]{1,0:T(8,128)(2,1)}, bf16[512,1024]{1,0:T(8,128)(2,1)}, u32[]{:S(2)}, u32[]{:S(2)}) %collective-permute-start.22) | collective-permute-done | bytes 1048608 | tf_op jit(solution)/shard_map/ppermute | solution.py:275
  147.7 3.7 %shard_map.86 = bf16[384,1024]{1,0:T(8,128)(2,1)} custom-call(s32[4]{0:T(128)S(1)} %pad_add_fusion.where, f32[384,1024]{1,0:T(8,128)S(1)} %shard_map.85.refs_0_, bf16[1024,384]{1,0:T(8,128)(2,1)S(1)} %constant_dynamic-update-slice_fusion.refs_1_, bf16[1024,384]{1,0:T(8,128)(2,1)} %collective-permute-done.15.refs_2_, ...), custom_call_target="tpu_custom_call" | custom-call | flops 402653184 | bytes 1048576 | tf_op jit(solution)/shard_map/pallas_call | solution.py:237
  (66 shorter events, 0.6 us)
Async XLA Ops:
  0.0 43.1 %copy-start = (f32[64,128]{1,0:T(8,128)S(1)}, f32[64,128]{1,0:T(8,128)}, u32[]{:S(2)}) copy-start(f32[64,128]{1,0:T(8,128)} %param.13) | copy-start | bytes 98308
  0.0 6.1 %copy-start.13 = (f32[4096]{0:T(1024)S(1)}, f32[4096]{0:T(1024)}, u32[]{:S(2)}) copy-start(f32[4096]{0:T(1024)} %param.10) | copy-start | bytes 49156
  2.3 31.3 %collective-permute-start.2 = (bf16[512,1024]{1,0:T(8,128)(2,1)}, bf16[512,1024]{1,0:T(8,128)(2,1)}, u32[]{:S(2)}, u32[]{:S(2)}) collective-permute-start(bf16[512,1024]{1,0:T(8,128)(2,1)} %constant_dynamic-slice_fusion.3), channel_id=1, source_target_pairs={{0,4},{4,0},{8,12},{12,8},{1,5},{5,1},{9,13},{13,9},{2,6},{6,2},{1... | collective-permute-start | bytes 3145736 | tf_op jit(solution)/shard_map/ppermute | solution.py:269
  5.3 35.3 %collective-permute-start.3 = (bf16[512,1024]{1,0:T(8,128)(2,1)}, bf16[512,1024]{1,0:T(8,128)(2,1)S(1)}, u32[]{:S(2)}, u32[]{:S(2)}) collective-permute-start(bf16[512,1024]{1,0:T(8,128)(2,1)} %constant_dynamic-slice_fusion.3), channel_id=1, source_target_pairs={{4,8},{8,4},{5,9},{9,5},{6,10},{10,6},{7,11},{11,7},{20,24},{24,20... | collective-permute-start | bytes 3145736 | tf_op jit(solution)/shard_map/ppermute | solution.py:269
  6.1 2.2 %copy-start.1 = (bf16[512,4096]{1,0:T(8,128)(2,1)S(1)}, bf16[512,4096]{1,0:T(8,128)(2,1)}, u32[]{:S(2)}) copy-start(bf16[512,4096]{1,0:T(8,128)(2,1)} %cut.1) | copy-start | bytes 12582916
  8.3 2.8 %copy-start.2 = (bf16[1024,3,1024]{2,0,1:T(8,128)(2,1)S(1)}, bf16[1024,3,1024]{2,0,1:T(8,128)(2,1)}, u32[]{:S(2)}) copy-start(bf16[1024,3,1024]{2,0,1:T(8,128)(2,1)} %param.11) | copy-start | bytes 18874372
  11.1 4.7 %copy-start.15 = (s32[384]{0:T(512)S(1)}, s32[384]{0:T(512)}, u32[]{:S(2)}) copy-start(s32[384]{0:T(512)} %param.8) | copy-start | bytes 4612
  11.1 10.6 %copy-start.14 = (f32[3,3,1024]{2,1,0:T(4,128)S(1)}, f32[3,3,1024]{2,1,0:T(4,128)}, u32[]{:S(2)}) copy-start(f32[3,3,1024]{2,1,0:T(4,128)} %param.12) | copy-start | bytes 110596
  15.8 13.8 %collective-permute-start.6 = (s32[384]{0:T(512)S(1)}, s32[384]{0:T(512)S(1)}, u32[]{:S(2)}, u32[]{:S(2)}) collective-permute-start(s32[384]{0:T(512)S(1)} %copy-done.15), channel_id=1, source_target_pairs={{0,12},{4,0},{8,4},{12,8},{1,13},{5,1},{9,5},{13,9},{2,14},{6,2},{... | collective-permute-start | bytes 4616 | tf_op jit(solution)/shard_map/ppermute | solution.py:17
  18.3 16.8 %collective-permute-start.5 = (s32[384]{0:T(512)S(1)}, s32[384]{0:T(512)S(1)}, u32[]{:S(2)}, u32[]{:S(2)}) collective-permute-start(s32[384]{0:T(512)S(1)} %copy-done.15), channel_id=1, source_target_pairs={{0,8},{4,12},{8,0},{12,4},{1,9},{5,13},{9,1},{13,5},{2,10},{6,14},... | collective-permute-start | bytes 4616 | tf_op jit(solution)/shard_map/ppermute | solution.py:17
  21.6 18.9 %collective-permute-start.1 = (bf16[768,256]{1,0:T(8,128)(2,1)S(1)}, bf16[768,256]{1,0:T(8,128)(2,1)S(1)}, u32[]{:S(2)}, u32[]{:S(2)}) collective-permute-start(bf16[768,256]{1,0:T(8,128)(2,1)S(1)} %get-tuple-element.25), channel_id=1, source_target_pairs={{0,4},{4,0},{8,12},{12,8},{1,5},{5,1},{9,13},{13,9},{2,6},{6,2},{1... | collective-permute-start | bytes 1179656 | tf_op jit(solution)/shard_map/ppermute | solution.py:22
  29.6 11.0 %collective-permute-start.4 = (s32[384]{0:T(512)S(1)}, s32[384]{0:T(512)S(1)}, u32[]{:S(2)}, u32[]{:S(2)}) collective-permute-start(s32[384]{0:T(512)S(1)} %copy-done.15), channel_id=1, source_target_pairs={{0,4},{4,8},{8,12},{12,0},{1,5},{5,9},{9,13},{13,1},{2,6},{6,10},{... | collective-permute-start | bytes 4616 | tf_op jit(solution)/shard_map/ppermute | solution.py:17
  33.6 27.5 %collective-permute-start.8 = (bf16[512,1024]{1,0:T(8,128)(2,1)}, bf16[512,1024]{1,0:T(8,128)(2,1)}, u32[]{:S(2)}, u32[]{:S(2)}) collective-permute-start(bf16[512,1024]{1,0:T(8,128)(2,1)} %collective-permute-done.2.refs_6_), channel_id=1, source_target_pairs={{0,16},{16,0},{1,17},{17,1},{2,18},{18,2},{3,19},{19,3},{4,20},{20... | collective-permute-start | bytes 3145736 | tf_op jit(solution)/shard_map/ppermute | solution.py:17
  35.1 15.8 %collective-permute-start = (bf16[768,256]{1,0:T(8,128)(2,1)}, bf16[768,256]{1,0:T(8,128)(2,1)}, u32[]{:S(2)}, u32[]{:S(2)}) collective-permute-start(bf16[768,256]{1,0:T(8,128)(2,1)} %get-tuple-element.23), channel_id=1, source_target_pairs={{0,4},{4,0},{8,12},{12,8},{1,5},{5,1},{9,13},{13,9},{2,6},{6,2},{1... | collective-permute-start | bytes 1179656 | tf_op jit(solution)/shard_map/ppermute | solution.py:22
  40.6 2.5 %copy-start.4 = (bf16[512,1024]{1,0:T(8,128)(2,1)}, bf16[512,1024]{1,0:T(8,128)(2,1)S(1)}, u32[]{:S(2)}) copy-start(bf16[512,1024]{1,0:T(8,128)(2,1)S(1)} %collective-permute-done.3.refs_8_) | copy-start | bytes 3145732
  41.5 18.2 %collective-permute-start.7 = (bf16[768,256]{1,0:T(8,128)(2,1)}, bf16[768,256]{1,0:T(8,128)(2,1)}, u32[]{:S(2)}, u32[]{:S(2)}) collective-permute-start(bf16[768,256]{1,0:T(8,128)(2,1)} %add_convert_fusion.1), channel_id=1, source_target_pairs={{0,8},{4,12},{8,0},{12,4},{1,9},{5,13},{9,1},{13,5},{2,10},{6,14},... | collective-permute-start | bytes 1179656 | tf_op jit(solution)/shard_map/ppermute | solution.py:22
  61.0 30.6 %collective-permute-start.11 = (bf16[512,1024]{1,0:T(8,128)(2,1)}, bf16[512,1024]{1,0:T(8,128)(2,1)}, u32[]{:S(2)}, u32[]{:S(2)}) collective-permute-start(bf16[512,1024]{1,0:T(8,128)(2,1)} %copy-done.4), channel_id=1, source_target_pairs={{4,0},{8,12},{5,1},{9,13},{6,2},{10,14},{7,3},{11,15},{20,16},{24,... | collective-permute-start | bytes 3145736 | tf_op jit(solution)/shard_map/ppermute | solution.py:269
  62.3 29.3 %collective-permute-start.12 = (bf16[512,1024]{1,0:T(8,128)(2,1)}, bf16[512,1024]{1,0:T(8,128)(2,1)}, u32[]{:S(2)}, u32[]{:S(2)}) collective-permute-start(bf16[512,1024]{1,0:T(8,128)(2,1)} %collective-permute-done.2.refs_6_), channel_id=1, source_target_pairs={{4,8},{8,4},{5,9},{9,5},{6,10},{10,6},{7,11},{11,7},{20,24},{24,20... | collective-permute-start | bytes 3145736 | tf_op jit(solution)/shard_map/ppermute | solution.py:269
  64.1 7.8 %collective-permute-start.9 = (bf16[3,256,256]{2,1,0:T(8,128)(2,1)S(1)}, bf16[3,256,256]{2,1,0:T(8,128)(2,1)S(1)}, u32[]{:S(2)}, u32[]{:S(2)}) collective-permute-start(bf16[3,256,256]{2,1,0:T(8,128)(2,1)S(1)} %bitcast.16), channel_id=1, source_target_pairs={{0,16},{16,0},{1,17},{17,1},{2,18},{18,2},{3,19},{19,3},{4,20},{20... | collective-permute-start | bytes 1179656 | tf_op jit(solution)/shard_map/ppermute | solution.py:17
  71.9 10.6 %copy-start.5 = (bf16[512,1024]{1,0:T(8,128)(2,1)S(1)}, bf16[512,1024]{1,0:T(8,128)(2,1)}, u32[]{:S(2)}) copy-start(bf16[512,1024]{1,0:T(8,128)(2,1)} %copy-done.4) | copy-start | bytes 3145732
  77.0 10.5 %collective-permute-start.10 = (bf16[256,384]{1,0:T(8,128)(2,1)S(1)}, bf16[256,384]{1,0:T(8,128)(2,1)S(1)}, u32[]{:S(2)}, u32[]{:S(2)}) collective-permute-start(bf16[256,384]{1,0:T(8,128)(2,1)S(1)} %get-tuple-element.30), channel_id=1, source_target_pairs={{0,4},{4,0},{8,12},{12,8},{1,5},{5,1},{9,13},{13,9},{2,6},{6,2},{1... | collective-permute-start | bytes 589832 | tf_op jit(solution)/shard_map/ppermute | solution.py:22
  82.0 21.5 %collective-permute-start.13 = (bf16[256,384]{1,0:T(8,128)(2,1)S(1)}, bf16[256,384]{1,0:T(8,128)(2,1)S(1)}, u32[]{:S(2)}, u32[]{:S(2)}) collective-permute-start(bf16[256,384]{1,0:T(8,128)(2,1)S(1)} %get-tuple-element.34), channel_id=1, source_target_pairs={{0,8},{4,12},{8,0},{12,4},{1,9},{5,13},{9,1},{13,5},{2,10},{6,14},... | collective-permute-start | bytes 589832 | tf_op jit(solution)/shard_map/ppermute | solution.py:22
  82.5 23.4 %collective-permute-start.19 = (bf16[512,1024]{1,0:T(8,128)(2,1)S(1)}, bf16[512,1024]{1,0:T(8,128)(2,1)S(1)}, u32[]{:S(2)}, u32[]{:S(2)}) collective-permute-start(bf16[512,1024]{1,0:T(8,128)(2,1)S(1)} %copy-done.5), channel_id=1, source_target_pairs={{4,20},{8,24},{20,4},{24,8},{5,21},{9,25},{21,5},{25,9},{6,22},{10... | collective-permute-start | bytes 3145736 | tf_op jit(solution)/shard_map/ppermute | solution.py:275
  83.2 42.2 %copy-start.3 = (bf16[1024,1024]{1,0:T(8,128)(2,1)S(1)}, bf16[1024,1024]{1,0:T(8,128)(2,1)}, u32[]{:S(2)}) copy-start(bf16[1024,1024]{1,0:T(8,128)(2,1)} %refs_5_.1) | copy-start | bytes 6291460
  87.5 16.8 %collective-permute-start.14 = (bf16[256,384]{1,0:T(8,128)(2,1)S(1)}, bf16[256,384]{1,0:T(8,128)(2,1)S(1)}, u32[]{:S(2)}, u32[]{:S(2)}) collective-permute-start(bf16[256,384]{1,0:T(8,128)(2,1)S(1)} %get-tuple-element.35), channel_id=1, source_target_pairs={{0,12},{4,8},{8,4},{12,0},{1,13},{5,9},{9,5},{13,1},{2,14},{6,10},... | collective-permute-start | bytes 589832 | tf_op jit(solution)/shard_map/ppermute | solution.py:22
  91.7 28.3 %collective-permute-start.20 = (bf16[512,1024]{1,0:T(8,128)(2,1)}, bf16[512,1024]{1,0:T(8,128)(2,1)}, u32[]{:S(2)}, u32[]{:S(2)}) collective-permute-start(bf16[512,1024]{1,0:T(8,128)(2,1)} %collective-permute-done.12.refs_12_), channel_id=1, source_target_pairs={{4,0},{8,12},{5,1},{9,13},{6,2},{10,14},{7,3},{11,15},{20,16},{24,... | collective-permute-start | bytes 3145736 | tf_op jit(solution)/shard_map/ppermute | solution.py:269
  93.0 23.7 %collective-permute-start.17 = (bf16[512,1024]{1,0:T(8,128)(2,1)}, bf16[512,1024]{1,0:T(8,128)(2,1)S(1)}, u32[]{:S(2)}, u32[]{:S(2)}) collective-permute-start(bf16[512,1024]{1,0:T(8,128)(2,1)} %collective-permute-done.11.refs_9_), channel_id=1, source_target_pairs={{0,16},{12,28},{16,0},{28,12},{1,17},{13,29},{17,1},{29,13},{2,18}... | collective-permute-start | bytes 3145736 | tf_op jit(solution)/shard_map/ppermute | solution.py:275
  103.5 14.2 %collective-permute-start.18 = (bf16[512,1024]{1,0:T(8,128)(2,1)}, bf16[512,1024]{1,0:T(8,128)(2,1)S(1)}, u32[]{:S(2)}, u32[]{:S(2)}) collective-permute-start(bf16[512,1024]{1,0:T(8,128)(2,1)} %collective-permute-done.12.refs_12_), channel_id=1, source_target_pairs={{4,20},{8,24},{20,4},{24,8},{5,21},{9,25},{21,5},{25,9},{6,22},{10... | collective-permute-start | bytes 3145736 | tf_op jit(solution)/shard_map/ppermute | solution.py:275
  104.4 12.3 %collective-permute-start.16 = (bf16[1024,384]{1,0:T(8,128)(2,1)S(1)}, bf16[1024,384]{1,0:T(8,128)(2,1)}, u32[]{:S(2)}, u32[]{:S(2)}) collective-permute-start(bf16[1024,384]{1,0:T(8,128)(2,1)S(1)} %constant_dynamic-update-slice_fusion.refs_1_), channel_id=1, source_target_pairs={{0,2},{2,0},{1,3},{3,1},{4,6},{6,4},{5,7},{7,5},{8,10},{10,8},{9,1... | collective-permute-start | bytes 2359304 | tf_op jit(solution)/shard_map/ppermute | solution.py:17
  105.9 1.0 copy-start.7
  106.9 18.5 %collective-permute-start.15 = (bf16[1024,384]{1,0:T(8,128)(2,1)S(1)}, bf16[1024,384]{1,0:T(8,128)(2,1)}, u32[]{:S(2)}, u32[]{:S(2)}) collective-permute-start(bf16[1024,384]{1,0:T(8,128)(2,1)S(1)} %constant_dynamic-update-slice_fusion.refs_1_), channel_id=1, source_target_pairs={{0,1},{1,0},{2,3},{3,2},{4,5},{5,4},{6,7},{7,6},{8,9},{9,8},{10,11... | collective-permute-start | bytes 2359304 | tf_op jit(solution)/shard_map/ppermute | solution.py:17
  116.7 1.0 copy-start.9
  117.7 1.1 copy-start.11
  120.0 5.5 %collective-permute-start.21 = (bf16[1024,384]{1,0:T(8,128)(2,1)}, bf16[1024,384]{1,0:T(8,128)(2,1)}, u32[]{:S(2)}, u32[]{:S(2)}) collective-permute-start(bf16[1024,384]{1,0:T(8,128)(2,1)} %collective-permute-done.16.refs_3_), channel_id=1, source_target_pairs={{0,1},{1,0},{2,3},{3,2},{4,5},{5,4},{6,7},{7,6},{8,9},{9,8},{10,11... | collective-permute-start | bytes 2359304 | tf_op jit(solution)/shard_map/ppermute | solution.py:17
  120.0 27.8 %collective-permute-start.22 = (bf16[512,1024]{1,0:T(8,128)(2,1)}, bf16[512,1024]{1,0:T(8,128)(2,1)}, u32[]{:S(2)}, u32[]{:S(2)}) collective-permute-start(bf16[512,1024]{1,0:T(8,128)(2,1)} %collective-permute-done.20.refs_13_), channel_id=1, source_target_pairs={{0,16},{12,28},{16,0},{28,12},{1,17},{13,29},{17,1},{29,13},{2,18}... | collective-permute-start | bytes 3145736 | tf_op jit(solution)/shard_map/ppermute | solution.py:275
  123.4 2.0 %copy-start.6 = (bf16[512,1024]{1,0:T(8,128)(2,1)S(1)}, bf16[512,1024]{1,0:T(8,128)(2,1)}, u32[]{:S(2)}) copy-start(bf16[512,1024]{1,0:T(8,128)(2,1)} %copy-done.4) | copy-start | bytes 3145732
  123.4 2.0 %copy-start.8 = (bf16[512,1024]{1,0:T(8,128)(2,1)S(1)}, bf16[512,1024]{1,0:T(8,128)(2,1)}, u32[]{:S(2)}) copy-start(bf16[512,1024]{1,0:T(8,128)(2,1)} %copy-done.7) | copy-start | bytes 3145732
  125.5 1.2 copy-start.10
  126.7 21.0 %copy-start.12 = (bf16[512,1024]{1,0:T(8,128)(2,1)S(1)}, bf16[512,1024]{1,0:T(8,128)(2,1)}, u32[]{:S(2)}) copy-start(bf16[512,1024]{1,0:T(8,128)(2,1)} %copy-done.11) | copy-start | bytes 3145732

commit v4 on v3

--- a/solution.py
+++ b/solution.py
@@ -314,8 +314,8 @@
     tables = [table] + [moved(table, "parts", across) for across in range(1, parts)]
     if line:
         pass
-        cross = along(after(first_near, table), middle)
-        out_second = along(after(first_mid, table), outward)
+        cross = along(after(first_near, got), middle)
+        out_second = along(after(first_mid, got), outward)
         mid_y = swap(after(first_mid, tables[1]), inner)
 
     first = seq * mine

time: 152 us -> 151 us (level)
  local copies, waits for them, and re-layouts: 12.8 us -> 16.1 us
  waiting for transfers between devices: 72.3 us -> 70.2 us
    ppermute x5, waiting for transfers between devices: 1.22 us -> 6.49 us  [along(): return lax.ppermute(value, 'seq', pairs)]
    unnamed x39 -> x47, local copies, waits for them, and re-layouts: 9.46 us -> 13.7 us
    ppermute x6, waiting for transfers between devices: 27.6 us -> 23.4 us  [swapped(): lax.ppermute(value, axis, [(source, source ^ bits) for source in range(co...]
    ppermute x4, waiting for transfers between devices: 14.5 us -> 12.6 us  [swap(): return lax.ppermute(value, ('parts', 'seq'), pairs)]
  transfers between devices with their start and end apart: 23 -> 23, of which waited for: 10 -> 9; matrix products, arithmetic and copies ran while one was open for 4% -> 4% of each run, Pallas kernels for 11% -> 11%
where the time goes in v4:
time: 151 us
  waiting for transfers between devices  70.2 us (46%)
  starting transfers between devices  39.5 us (26%)
  Pallas kernels  19.9 us (13%)
  local copies, waits for them, and re-layouts  16.1 us (11%)
  other arithmetic  2.8 us (2%)
  matrix products  1.99 us (1%)
    ppermute x8, waiting for transfers between devices, moved(): lax.ppermute(value, axis, [(source, (source + steps) % count) for source...  27.7 us
    ppermute x6, waiting for transfers between devices, swapped(): lax.ppermute(value, axis, [(source, source ^ bits) for source in range(co...  23.4 us
    unnamed x47, local copies, waits for them, and re-layouts  13.7 us
    ppermute x8, starting transfers between devices, moved(): lax.ppermute(value, axis, [(source, (source + steps) % count) for source...  13.6 us
    ppermute x4, waiting for transfers between devices, swap(): return lax.ppermute(value, ('parts', 'seq'), pairs)  12.6 us
    pallas_call x2, Pallas kernels, output(): pl.pallas_call(functools.partial(output_kernel, axes, len(stacks), tuple(...  9.61 us
    ppermute x6, starting transfers between devices, swapped(): lax.ppermute(value, axis, [(source, source ^ bits) for source in range(co...  9.59 us
    ppermute x4, starting transfers between devices, swap(): return lax.ppermute(value, ('parts', 'seq'), pairs)  8.27 us
  transfers between devices with their start and end apart: 23, of which 9 were waited for; matrix products, arithmetic and copies ran while one was open for 4% of the time, Pallas kernels for 11%

profile of v4, /device:TPU:0, one launch (start us, length us, event | category | flops | bytes accessed | tf_op | source)
XLA Modules:
  0.0 150.7 jit_solution(11944431577959082976)
XLA Ops:
  0.0 1.3 constant_dynamic-slice_fusion.3
  1.3 3.1 %collective-permute-start.2 = (bf16[512,1024]{1,0:T(8,128)(2,1)S(1)}, bf16[512,1024]{1,0:T(8,128)(2,1)}, u32[]{:S(2)}, u32[]{:S(2)}) collective-permute-start(bf16[512,1024]{1,0:T(8,128)(2,1)S(1)} %constant_dynamic-slice_fusion.3), channel_id=1, source_target_pairs={{0,4},{4,0},{8,12},{12,8},{1,5},{5,1},{9,13},{13,9},{2,6},{6,2},{1... | collective-permute-start | bytes 3145736 | tf_op jit(solution)/shard_map/ppermute | solution.py:269
  4.4 1.6 %collective-permute-start.3 = (bf16[512,1024]{1,0:T(8,128)(2,1)S(1)}, bf16[512,1024]{1,0:T(8,128)(2,1)}, u32[]{:S(2)}, u32[]{:S(2)}) collective-permute-start(bf16[512,1024]{1,0:T(8,128)(2,1)S(1)} %constant_dynamic-slice_fusion.3), channel_id=1, source_target_pairs={{4,8},{8,4},{5,9},{9,5},{6,10},{10,6},{7,11},{11,7},{20,24},{24,20... | collective-permute-start | bytes 3145736 | tf_op jit(solution)/shard_map/ppermute | solution.py:269
  6.1 2.2 %copy-done.1 = bf16[512,4096]{1,0:T(8,128)(2,1)S(1)} copy-done((bf16[512,4096]{1,0:T(8,128)(2,1)S(1)}, bf16[512,4096]{1,0:T(8,128)(2,1)}, u32[]{:S(2)}) %copy-start.1) | copy-done | bytes 4194328
  8.3 2.8 %copy-done.2 = bf16[1024,3,1024]{2,0,1:T(8,128)(2,1)S(1)} copy-done((bf16[1024,3,1024]{2,0,1:T(8,128)(2,1)S(1)}, bf16[1024,3,1024]{2,0,1:T(8,128)(2,1)}, u32[]{:S(2)}) %copy-start.2) | copy-done | bytes 6291480
  11.1 4.8 %shard_map.82 = (f32[768,256]{1,0:T(8,128)S(1)}, bf16[768,256]{1,0:T(8,128)(2,1)}, bf16[768,256]{1,0:T(8,128)(2,1)S(1)}, bf16[768,256]{1,0:T(8,128)(2,1)S(1)}) custom-call(s32[4]{0:T(128)S(1)} %pad_add_fusion.where, bf16[512,4096]{1,0:T(8,128)(2,1)S(1)} %copy-done.1, bf16[512,4096]{1,0:T(8,128)(2,1)S(1)} %copy-done.1, f32[1,4096]{1,0:T(1,128)S(1)} %bitcast.19, ...), custom_call_target="tpu_custom_call" | custom-call | flops 1610612736 | bytes 8388608 | tf_op jit(solution)/shard_map/pallas_call | solution.py:54
  15.9 0.9 copy-done.16
  16.8 2.5 %collective-permute-start.6 = (s32[384]{0:T(512)S(1)}, s32[384]{0:T(512)S(1)}, u32[]{:S(2)}, u32[]{:S(2)}) collective-permute-start(s32[384]{0:T(512)S(1)} %copy-done.19), channel_id=1, source_target_pairs={{0,12},{4,0},{8,4},{12,8},{1,13},{5,1},{9,5},{13,9},{2,14},{6,2},{... | collective-permute-start | bytes 4616 | tf_op jit(solution)/shard_map/ppermute | solution.py:17
  19.2 2.4 %collective-permute-start.5 = (s32[384]{0:T(512)S(1)}, s32[384]{0:T(512)S(1)}, u32[]{:S(2)}, u32[]{:S(2)}) collective-permute-start(s32[384]{0:T(512)S(1)} %copy-done.19), channel_id=1, source_target_pairs={{0,8},{4,12},{8,0},{12,4},{1,9},{5,13},{9,1},{13,5},{2,10},{6,14},... | collective-permute-start | bytes 4616 | tf_op jit(solution)/shard_map/ppermute | solution.py:17
  21.8 0.8 dynamic_slice.22
  22.7 5.8 %collective-permute-done.6 = s32[384]{0:T(512)S(1)} collective-permute-done((s32[384]{0:T(512)S(1)}, s32[384]{0:T(512)S(1)}, u32[]{:S(2)}, u32[]{:S(2)}) %collective-permute-start.6) | collective-permute-done | bytes 1568 | tf_op jit(solution)/shard_map/ppermute | solution.py:17
  28.5 4.0 %collective-permute-start.4 = (s32[384]{0:T(512)S(1)}, s32[384]{0:T(512)S(1)}, u32[]{:S(2)}, u32[]{:S(2)}) collective-permute-start(s32[384]{0:T(512)S(1)} %copy-done.19), channel_id=1, source_target_pairs={{0,4},{4,8},{8,12},{12,0},{1,5},{5,9},{9,13},{13,1},{2,6},{6,10},{... | collective-permute-start | bytes 4616 | tf_op jit(solution)/shard_map/ppermute | solution.py:17
  32.5 1.5 %collective-permute-start.8 = (bf16[512,1024]{1,0:T(8,128)(2,1)}, bf16[512,1024]{1,0:T(8,128)(2,1)S(1)}, u32[]{:S(2)}, u32[]{:S(2)}) collective-permute-start(bf16[512,1024]{1,0:T(8,128)(2,1)} %collective-permute-done.2.refs_6_), channel_id=1, source_target_pairs={{0,16},{16,0},{1,17},{17,1},{2,18},{18,2},{3,19},{19,3},{4,20},{20... | collective-permute-start | bytes 3145736 | tf_op jit(solution)/shard_map/ppermute | solution.py:17
  34.1 5.3 %collective-permute-done.4 = s32[384]{0:T(512)S(1)} collective-permute-done((s32[384]{0:T(512)S(1)}, s32[384]{0:T(512)S(1)}, u32[]{:S(2)}, u32[]{:S(2)}) %collective-permute-start.4) | collective-permute-done | bytes 1568 | tf_op jit(solution)/shard_map/ppermute | solution.py:17
  39.5 0.8 add_convert_fusion.1
  40.3 0.5 collective-permute-start.7
  40.9 0.4 shard_map.83.refs_4_
  41.5 17.2 %collective-permute-done.7 = bf16[768,256]{1,0:T(8,128)(2,1)} collective-permute-done((bf16[768,256]{1,0:T(8,128)(2,1)}, bf16[768,256]{1,0:T(8,128)(2,1)}, u32[]{:S(2)}, u32[]{:S(2)}) %collective-permute-start.7) | collective-permute-done | bytes 393248 | tf_op jit(solution)/shard_map/ppermute | solution.py:22
  58.6 1.3 collective-permute-start.11
  59.9 0.7 collective-permute-start.12
  60.7 1.5 add_convert_fusion
  62.2 1.6 %collective-permute-start.9 = (bf16[3,256,256]{2,1,0:T(8,128)(2,1)S(1)}, bf16[3,256,256]{2,1,0:T(8,128)(2,1)S(1)}, u32[]{:S(2)}, u32[]{:S(2)}) collective-permute-start(bf16[3,256,256]{2,1,0:T(8,128)(2,1)S(1)} %bitcast.16), channel_id=1, source_target_pairs={{0,16},{16,0},{1,17},{17,1},{2,18},{18,2},{3,19},{19,3},{4,20},{20... | collective-permute-start | bytes 1179656 | tf_op jit(solution)/shard_map/ppermute | solution.py:17
  64.1 5.9 %collective-permute-done.9.refs_1_ = bf16[3,256,256]{2,1,0:T(8,128)(2,1)S(1)} collective-permute-done((bf16[3,256,256]{2,1,0:T(8,128)(2,1)S(1)}, bf16[3,256,256]{2,1,0:T(8,128)(2,1)S(1)}, u32[]{:S(2)}, u32[]{:S(2)}) %collective-permute-start.9) | collective-permute-done | bytes 393248 | tf_op jit(solution)/shard_map/ppermute | solution.py:17
  70.0 5.1 %shard_map.84 = (bf16[256,384]{1,0:T(8,128)(2,1)S(1)}, bf16[256,384]{1,0:T(8,128)(2,1)S(1)}, bf16[256,384]{1,0:T(8,128)(2,1)S(1)}, bf16[256,384]{1,0:T(8,128)(2,1)S(1)}) custom-call(s32[4]{0:T(128)S(1)} %pad_add_fusion.where, bf16[3,256,256]{2,1,0:T(8,128)(2,1)S(1)} %bitcast.17, bf16[3,256,256]{2,1,0:T(8,128)(2,1)S(1)} %collective-permute-done.9.refs_1_, ...), custom_call_target="tpu_custom_call" | custom-call | flops 1207959552 | bytes 1572864 | tf_op jit(solution)/shard_map/pallas_call | solution.py:156
  75.1 4.8 %collective-permute-start.10 = (bf16[256,384]{1,0:T(8,128)(2,1)S(1)}, bf16[256,384]{1,0:T(8,128)(2,1)S(1)}, u32[]{:S(2)}, u32[]{:S(2)}) collective-permute-start(bf16[256,384]{1,0:T(8,128)(2,1)S(1)} %get-tuple-element.30), channel_id=1, source_target_pairs={{0,4},{4,0},{8,12},{12,8},{1,5},{5,1},{9,13},{13,9},{2,6},{6,2},{1... | collective-permute-start | bytes 589832 | tf_op jit(solution)/shard_map/ppermute | solution.py:22
  79.9 0.7 collective-permute-start.13
  80.6 0.7 collective-permute-start.19
  81.4 4.7 %collective-permute-done.11.refs_9_ = bf16[512,1024]{1,0:T(8,128)(2,1)S(1)} collective-permute-done((bf16[512,1024]{1,0:T(8,128)(2,1)}, bf16[512,1024]{1,0:T(8,128)(2,1)S(1)}, u32[]{:S(2)}, u32[]{:S(2)}) %collective-permute-start.11) | collective-permute-done | bytes 1048608 | tf_op jit(solution)/shard_map/ppermute | solution.py:269
  86.0 3.5 %collective-permute-start.14 = (bf16[256,384]{1,0:T(8,128)(2,1)S(1)}, bf16[256,384]{1,0:T(8,128)(2,1)S(1)}, u32[]{:S(2)}, u32[]{:S(2)}) collective-permute-start(bf16[256,384]{1,0:T(8,128)(2,1)S(1)} %get-tuple-element.35), channel_id=1, source_target_pairs={{0,12},{4,8},{8,4},{12,0},{1,13},{5,9},{9,5},{13,1},{2,14},{6,10},... | collective-permute-start | bytes 589832 | tf_op jit(solution)/shard_map/ppermute | solution.py:22
  89.5 3.4 %collective-permute-start.17 = (bf16[512,1024]{1,0:T(8,128)(2,1)S(1)}, bf16[512,1024]{1,0:T(8,128)(2,1)S(1)}, u32[]{:S(2)}, u32[]{:S(2)}) collective-permute-start(bf16[512,1024]{1,0:T(8,128)(2,1)S(1)} %collective-permute-done.11.refs_9_), channel_id=1, source_target_pairs={{0,16},{12,28},{16,0},{28,12},{1,17},{13,29},{17,1},{29,13},{2,18}... | collective-permute-start | bytes 3145736 | tf_op jit(solution)/shard_map/ppermute | solution.py:275
  93.0 0.7 collective-permute-start.18
  93.7 6.2 %collective-permute-done.13 = bf16[256,384]{1,0:T(8,128)(2,1)S(1)} collective-permute-done((bf16[256,384]{1,0:T(8,128)(2,1)S(1)}, bf16[256,384]{1,0:T(8,128)(2,1)S(1)}, u32[]{:S(2)}, u32[]{:S(2)}) %collective-permute-start.13) | collective-permute-done | bytes 196640 | tf_op jit(solution)/shard_map/ppermute | solution.py:22
  99.9 1.3 collective-permute-start.20
  101.2 1.0 copy-done.8
  102.4 1.6 %collective-permute-start.16 = (bf16[1024,384]{1,0:T(8,128)(2,1)S(1)}, bf16[1024,384]{1,0:T(8,128)(2,1)}, u32[]{:S(2)}, u32[]{:S(2)}) collective-permute-start(bf16[1024,384]{1,0:T(8,128)(2,1)S(1)} %constant_dynamic-update-slice_fusion.refs_1_), channel_id=1, source_target_pairs={{0,2},{2,0},{1,3},{3,1},{4,6},{6,4},{5,7},{7,5},{8,10},{10,8},{9,1... | collective-permute-start | bytes 2359304 | tf_op jit(solution)/shard_map/ppermute | solution.py:17
  103.9 10.6 %collective-permute-done.16.refs_3_ = bf16[1024,384]{1,0:T(8,128)(2,1)} collective-permute-done((bf16[1024,384]{1,0:T(8,128)(2,1)S(1)}, bf16[1024,384]{1,0:T(8,128)(2,1)}, u32[]{:S(2)}, u32[]{:S(2)}) %collective-permute-start.16) | collective-permute-done | bytes 786464 | tf_op jit(solution)/shard_map/ppermute | solution.py:17
  114.5 1.0 copy-done.10
  115.5 1.0 copy-done.12
  116.5 1.0 copy-done.14
  117.5 1.8 %collective-permute-done.20.refs_13_ = bf16[512,1024]{1,0:T(8,128)(2,1)} collective-permute-done((bf16[512,1024]{1,0:T(8,128)(2,1)S(1)}, bf16[512,1024]{1,0:T(8,128)(2,1)}, u32[]{:S(2)}, u32[]{:S(2)}) %collective-permute-start.20) | collective-permute-done | bytes 1048608 | tf_op jit(solution)/shard_map/ppermute | solution.py:269
  119.3 3.4 %collective-permute-start.22 = (bf16[512,1024]{1,0:T(8,128)(2,1)}, bf16[512,1024]{1,0:T(8,128)(2,1)}, u32[]{:S(2)}, u32[]{:S(2)}) collective-permute-start(bf16[512,1024]{1,0:T(8,128)(2,1)} %collective-permute-done.20.refs_13_), channel_id=1, source_target_pairs={{0,16},{12,28},{16,0},{28,12},{1,17},{13,29},{17,1},{29,13},{2,18}... | collective-permute-start | bytes 3145736 | tf_op jit(solution)/shard_map/ppermute | solution.py:275
  122.8 2.0 %fusion.refs_0_ = f32[384,1024]{1,0:T(8,128)S(1)} fusion(bf16[512,4096]{1,0:T(8,128)(2,1)} %cut.1, s32[]{:T(128)S(6)} %select_n.16, s32[384]{0:T(512)S(1)} %copy-done.19), kind=kOutput, calls=%fused_computation.1 | convolution fusion | flops 402849792 | bytes 2622980 | tf_op jit(solution)/shard_map/dot_general | solution.py:351
  124.8 1.2 copy-done.9
  126.0 1.2 copy-done.11
  127.3 1.2 copy-done.13
  128.5 6.0 %shard_map.85.refs_0_ = f32[384,1024]{1,0:T(8,128)S(1)} custom-call(s32[4]{0:T(128)S(1)} %pad_add_fusion.where, f32[384,1024]{1,0:T(8,128)S(1)} %fusion.refs_0_, bf16[1024,384]{1,0:T(8,128)(2,1)S(1)} %constant_dynamic-update-slice_fusion.refs_1_, bf16[1024,384]{1,0:T(8,128)(2,1)} %collective-permute-done.15.refs_2_, ...), custom_call_target="tpu_custom_call" | custom-call | flops 2818572288 | bytes 7340032 | tf_op jit(solution)/shard_map/pallas_call | solution.py:237
  134.5 12.6 %collective-permute-done.22.refs_6_ = bf16[512,1024]{1,0:T(8,128)(2,1)} collective-permute-done((bf16[512,1024]{1,0:T(8,128)(2,1)}, bf16[512,1024]{1,0:T(8,128)(2,1)}, u32[]{:S(2)}, u32[]{:S(2)}) %collective-permute-start.22) | collective-permute-done | bytes 1048608 | tf_op jit(solution)/shard_map/ppermute | solution.py:275
  147.1 3.6 %shard_map.86 = bf16[384,1024]{1,0:T(8,128)(2,1)} custom-call(s32[4]{0:T(128)S(1)} %pad_add_fusion.where, f32[384,1024]{1,0:T(8,128)S(1)} %shard_map.85.refs_0_, bf16[1024,384]{1,0:T(8,128)(2,1)S(1)} %constant_dynamic-update-slice_fusion.refs_1_, bf16[1024,384]{1,0:T(8,128)(2,1)} %collective-permute-done.15.refs_2_, ...), custom_call_target="tpu_custom_call" | custom-call | flops 402653184 | bytes 1048576 | tf_op jit(solution)/shard_map/pallas_call | solution.py:237
  (74 shorter events, 1.1 us)
Async XLA Ops:
  0.0 34.1 %copy-start = (f32[64,128]{1,0:T(8,128)S(1)}, f32[64,128]{1,0:T(8,128)}, u32[]{:S(2)}) copy-start(f32[64,128]{1,0:T(8,128)} %param.13) | copy-start | bytes 98308
  0.0 6.1 %copy-start.17 = (f32[4096]{0:T(1024)S(1)}, f32[4096]{0:T(1024)}, u32[]{:S(2)}) copy-start(f32[4096]{0:T(1024)} %param.10) | copy-start | bytes 49156
  1.3 31.2 %collective-permute-start.2 = (bf16[512,1024]{1,0:T(8,128)(2,1)S(1)}, bf16[512,1024]{1,0:T(8,128)(2,1)}, u32[]{:S(2)}, u32[]{:S(2)}) collective-permute-start(bf16[512,1024]{1,0:T(8,128)(2,1)S(1)} %constant_dynamic-slice_fusion.3), channel_id=1, source_target_pairs={{0,4},{4,0},{8,12},{12,8},{1,5},{5,1},{9,13},{13,9},{2,6},{6,2},{1... | collective-permute-start | bytes 3145736 | tf_op jit(solution)/shard_map/ppermute | solution.py:269
  4.4 35.1 %collective-permute-start.3 = (bf16[512,1024]{1,0:T(8,128)(2,1)S(1)}, bf16[512,1024]{1,0:T(8,128)(2,1)}, u32[]{:S(2)}, u32[]{:S(2)}) collective-permute-start(bf16[512,1024]{1,0:T(8,128)(2,1)S(1)} %constant_dynamic-slice_fusion.3), channel_id=1, source_target_pairs={{4,8},{8,4},{5,9},{9,5},{6,10},{10,6},{7,11},{11,7},{20,24},{24,20... | collective-permute-start | bytes 3145736 | tf_op jit(solution)/shard_map/ppermute | solution.py:269
  6.1 2.2 %copy-start.1 = (bf16[512,4096]{1,0:T(8,128)(2,1)S(1)}, bf16[512,4096]{1,0:T(8,128)(2,1)}, u32[]{:S(2)}) copy-start(bf16[512,4096]{1,0:T(8,128)(2,1)} %cut.1) | copy-start | bytes 12582916
  8.3 2.8 %copy-start.2 = (bf16[1024,3,1024]{2,0,1:T(8,128)(2,1)S(1)}, bf16[1024,3,1024]{2,0,1:T(8,128)(2,1)}, u32[]{:S(2)}) copy-start(bf16[1024,3,1024]{2,0,1:T(8,128)(2,1)} %param.11) | copy-start | bytes 18874372
  11.1 5.6 %copy-start.19 = (s32[384]{0:T(512)S(1)}, s32[384]{0:T(512)}, u32[]{:S(2)}) copy-start(s32[384]{0:T(512)} %param.8) | copy-start | bytes 4612
  11.1 10.5 %copy-start.18 = (f32[3,3,1024]{2,1,0:T(4,128)S(1)}, f32[3,3,1024]{2,1,0:T(4,128)}, u32[]{:S(2)}) copy-start(f32[3,3,1024]{2,1,0:T(4,128)} %param.12) | copy-start | bytes 110596
  15.9 0.9 copy-start.16
  16.8 11.8 %collective-permute-start.6 = (s32[384]{0:T(512)S(1)}, s32[384]{0:T(512)S(1)}, u32[]{:S(2)}, u32[]{:S(2)}) collective-permute-start(s32[384]{0:T(512)S(1)} %copy-done.19), channel_id=1, source_target_pairs={{0,12},{4,0},{8,4},{12,8},{1,13},{5,1},{9,5},{13,9},{2,14},{6,2},{... | collective-permute-start | bytes 4616 | tf_op jit(solution)/shard_map/ppermute | solution.py:17
  19.2 14.8 %collective-permute-start.5 = (s32[384]{0:T(512)S(1)}, s32[384]{0:T(512)S(1)}, u32[]{:S(2)}, u32[]{:S(2)}) collective-permute-start(s32[384]{0:T(512)S(1)} %copy-done.19), channel_id=1, source_target_pairs={{0,8},{4,12},{8,0},{12,4},{1,9},{5,13},{9,1},{13,5},{2,10},{6,14},... | collective-permute-start | bytes 4616 | tf_op jit(solution)/shard_map/ppermute | solution.py:17
  21.6 17.8 %collective-permute-start.1 = (bf16[768,256]{1,0:T(8,128)(2,1)S(1)}, bf16[768,256]{1,0:T(8,128)(2,1)S(1)}, u32[]{:S(2)}, u32[]{:S(2)}) collective-permute-start(bf16[768,256]{1,0:T(8,128)(2,1)S(1)} %get-tuple-element.25), channel_id=1, source_target_pairs={{0,4},{4,0},{8,12},{12,8},{1,5},{5,1},{9,13},{13,9},{2,6},{6,2},{1... | collective-permute-start | bytes 1179656 | tf_op jit(solution)/shard_map/ppermute | solution.py:22
  28.5 11.0 %collective-permute-start.4 = (s32[384]{0:T(512)S(1)}, s32[384]{0:T(512)S(1)}, u32[]{:S(2)}, u32[]{:S(2)}) collective-permute-start(s32[384]{0:T(512)S(1)} %copy-done.19), channel_id=1, source_target_pairs={{0,4},{4,8},{8,12},{12,0},{1,5},{5,9},{9,13},{13,1},{2,6},{6,10},{... | collective-permute-start | bytes 4616 | tf_op jit(solution)/shard_map/ppermute | solution.py:17
  32.5 29.6 %collective-permute-start.8 = (bf16[512,1024]{1,0:T(8,128)(2,1)}, bf16[512,1024]{1,0:T(8,128)(2,1)S(1)}, u32[]{:S(2)}, u32[]{:S(2)}) collective-permute-start(bf16[512,1024]{1,0:T(8,128)(2,1)} %collective-permute-done.2.refs_6_), channel_id=1, source_target_pairs={{0,16},{16,0},{1,17},{17,1},{2,18},{18,2},{3,19},{19,3},{4,20},{20... | collective-permute-start | bytes 3145736 | tf_op jit(solution)/shard_map/ppermute | solution.py:17
  34.1 26.6 %collective-permute-start = (bf16[768,256]{1,0:T(8,128)(2,1)}, bf16[768,256]{1,0:T(8,128)(2,1)}, u32[]{:S(2)}, u32[]{:S(2)}) collective-permute-start(bf16[768,256]{1,0:T(8,128)(2,1)} %get-tuple-element.23), channel_id=1, source_target_pairs={{0,4},{4,0},{8,12},{12,8},{1,5},{5,1},{9,13},{13,9},{2,6},{6,2},{1... | collective-permute-start | bytes 1179656 | tf_op jit(solution)/shard_map/ppermute | solution.py:22
  40.3 18.3 %collective-permute-start.7 = (bf16[768,256]{1,0:T(8,128)(2,1)}, bf16[768,256]{1,0:T(8,128)(2,1)}, u32[]{:S(2)}, u32[]{:S(2)}) collective-permute-start(bf16[768,256]{1,0:T(8,128)(2,1)} %add_convert_fusion.1), channel_id=1, source_target_pairs={{0,8},{4,12},{8,0},{12,4},{1,9},{5,13},{9,1},{13,5},{2,10},{6,14},... | collective-permute-start | bytes 1179656 | tf_op jit(solution)/shard_map/ppermute | solution.py:22
  58.6 27.4 %collective-permute-start.11 = (bf16[512,1024]{1,0:T(8,128)(2,1)}, bf16[512,1024]{1,0:T(8,128)(2,1)S(1)}, u32[]{:S(2)}, u32[]{:S(2)}) collective-permute-start(bf16[512,1024]{1,0:T(8,128)(2,1)} %collective-permute-done.3.refs_8_), channel_id=1, source_target_pairs={{4,0},{8,12},{5,1},{9,13},{6,2},{10,14},{7,3},{11,15},{20,16},{24,... | collective-permute-start | bytes 3145736 | tf_op jit(solution)/shard_map/ppermute | solution.py:269
  59.9 29.6 %collective-permute-start.12 = (bf16[512,1024]{1,0:T(8,128)(2,1)}, bf16[512,1024]{1,0:T(8,128)(2,1)S(1)}, u32[]{:S(2)}, u32[]{:S(2)}) collective-permute-start(bf16[512,1024]{1,0:T(8,128)(2,1)} %collective-permute-done.2.refs_6_), channel_id=1, source_target_pairs={{4,8},{8,4},{5,9},{9,5},{6,10},{10,6},{7,11},{11,7},{20,24},{24,20... | collective-permute-start | bytes 3145736 | tf_op jit(solution)/shard_map/ppermute | solution.py:269
  62.2 12.9 %copy-start.4 = (bf16[512,1024]{1,0:T(8,128)(2,1)}, bf16[512,1024]{1,0:T(8,128)(2,1)S(1)}, u32[]{:S(2)}) copy-start(bf16[512,1024]{1,0:T(8,128)(2,1)S(1)} %collective-permute-done.8.refs_7_) | copy-start | bytes 3145732
  62.2 7.8 %collective-permute-start.9 = (bf16[3,256,256]{2,1,0:T(8,128)(2,1)S(1)}, bf16[3,256,256]{2,1,0:T(8,128)(2,1)S(1)}, u32[]{:S(2)}, u32[]{:S(2)}) collective-permute-start(bf16[3,256,256]{2,1,0:T(8,128)(2,1)S(1)} %bitcast.16), channel_id=1, source_target_pairs={{0,16},{16,0},{1,17},{17,1},{2,18},{18,2},{3,19},{19,3},{4,20},{20... | collective-permute-start | bytes 1179656 | tf_op jit(solution)/shard_map/ppermute | solution.py:17
  75.1 17.9 %collective-permute-start.10 = (bf16[256,384]{1,0:T(8,128)(2,1)S(1)}, bf16[256,384]{1,0:T(8,128)(2,1)S(1)}, u32[]{:S(2)}, u32[]{:S(2)}) collective-permute-start(bf16[256,384]{1,0:T(8,128)(2,1)S(1)} %get-tuple-element.30), channel_id=1, source_target_pairs={{0,4},{4,0},{8,12},{12,8},{1,5},{5,1},{9,13},{13,9},{2,6},{6,2},{1... | collective-permute-start | bytes 589832 | tf_op jit(solution)/shard_map/ppermute | solution.py:22
  79.9 20.0 %collective-permute-start.13 = (bf16[256,384]{1,0:T(8,128)(2,1)S(1)}, bf16[256,384]{1,0:T(8,128)(2,1)S(1)}, u32[]{:S(2)}, u32[]{:S(2)}) collective-permute-start(bf16[256,384]{1,0:T(8,128)(2,1)S(1)} %get-tuple-element.34), channel_id=1, source_target_pairs={{0,8},{4,12},{8,0},{12,4},{1,9},{5,13},{9,1},{13,5},{2,10},{6,14},... | collective-permute-start | bytes 589832 | tf_op jit(solution)/shard_map/ppermute | solution.py:22
  80.6 33.9 %collective-permute-start.19 = (bf16[512,1024]{1,0:T(8,128)(2,1)}, bf16[512,1024]{1,0:T(8,128)(2,1)S(1)}, u32[]{:S(2)}, u32[]{:S(2)}) collective-permute-start(bf16[512,1024]{1,0:T(8,128)(2,1)} %collective-permute-done.3.refs_8_), channel_id=1, source_target_pairs={{4,20},{8,24},{20,4},{24,8},{5,21},{9,25},{21,5},{25,9},{6,22},{10... | collective-permute-start | bytes 3145736 | tf_op jit(solution)/shard_map/ppermute | solution.py:275
  81.3 43.5 %copy-start.3 = (bf16[1024,1024]{1,0:T(8,128)(2,1)S(1)}, bf16[1024,1024]{1,0:T(8,128)(2,1)}, u32[]{:S(2)}) copy-start(bf16[1024,1024]{1,0:T(8,128)(2,1)} %refs_5_.1) | copy-start | bytes 6291460
  86.0 28.5 %copy-start.6 = (bf16[512,1024]{1,0:T(8,128)(2,1)}, bf16[512,1024]{1,0:T(8,128)(2,1)S(1)}, u32[]{:S(2)}) copy-start(bf16[512,1024]{1,0:T(8,128)(2,1)S(1)} %collective-permute-done.11.refs_9_) | copy-start | bytes 3145732
  86.0 16.3 %collective-permute-start.14 = (bf16[256,384]{1,0:T(8,128)(2,1)S(1)}, bf16[256,384]{1,0:T(8,128)(2,1)S(1)}, u32[]{:S(2)}, u32[]{:S(2)}) collective-permute-start(bf16[256,384]{1,0:T(8,128)(2,1)S(1)} %get-tuple-element.35), channel_id=1, source_target_pairs={{0,12},{4,8},{8,4},{12,0},{1,13},{5,9},{9,5},{13,1},{2,14},{6,10},... | collective-permute-start | bytes 589832 | tf_op jit(solution)/shard_map/ppermute | solution.py:22
  89.5 26.0 %collective-permute-start.17 = (bf16[512,1024]{1,0:T(8,128)(2,1)S(1)}, bf16[512,1024]{1,0:T(8,128)(2,1)S(1)}, u32[]{:S(2)}, u32[]{:S(2)}) collective-permute-start(bf16[512,1024]{1,0:T(8,128)(2,1)S(1)} %collective-permute-done.11.refs_9_), channel_id=1, source_target_pairs={{0,16},{12,28},{16,0},{28,12},{1,17},{13,29},{17,1},{29,13},{2,18}... | collective-permute-start | bytes 3145736 | tf_op jit(solution)/shard_map/ppermute | solution.py:275
  93.0 23.5 %collective-permute-start.18 = (bf16[512,1024]{1,0:T(8,128)(2,1)S(1)}, bf16[512,1024]{1,0:T(8,128)(2,1)S(1)}, u32[]{:S(2)}, u32[]{:S(2)}) collective-permute-start(bf16[512,1024]{1,0:T(8,128)(2,1)S(1)} %collective-permute-done.12.refs_12_), channel_id=1, source_target_pairs={{4,20},{8,24},{20,4},{24,8},{5,21},{9,25},{21,5},{25,9},{6,22},{10... | collective-permute-start | bytes 3145736 | tf_op jit(solution)/shard_map/ppermute | solution.py:275
  99.9 19.4 %collective-permute-start.20 = (bf16[512,1024]{1,0:T(8,128)(2,1)S(1)}, bf16[512,1024]{1,0:T(8,128)(2,1)}, u32[]{:S(2)}, u32[]{:S(2)}) collective-permute-start(bf16[512,1024]{1,0:T(8,128)(2,1)S(1)} %collective-permute-done.12.refs_12_), channel_id=1, source_target_pairs={{4,0},{8,12},{5,1},{9,13},{6,2},{10,14},{7,3},{11,15},{20,16},{24,... | collective-permute-start | bytes 3145736 | tf_op jit(solution)/shard_map/ppermute | solution.py:269
  101.2 1.1 copy-start.8
  102.4 12.2 %collective-permute-start.16 = (bf16[1024,384]{1,0:T(8,128)(2,1)S(1)}, bf16[1024,384]{1,0:T(8,128)(2,1)}, u32[]{:S(2)}, u32[]{:S(2)}) collective-permute-start(bf16[1024,384]{1,0:T(8,128)(2,1)S(1)} %constant_dynamic-update-slice_fusion.refs_1_), channel_id=1, source_target_pairs={{0,2},{2,0},{1,3},{3,1},{4,6},{6,4},{5,7},{7,5},{8,10},{10,8},{9,1... | collective-permute-start | bytes 2359304 | tf_op jit(solution)/shard_map/ppermute | solution.py:17
  114.5 10.2 %collective-permute-start.15 = (bf16[1024,384]{1,0:T(8,128)(2,1)S(1)}, bf16[1024,384]{1,0:T(8,128)(2,1)}, u32[]{:S(2)}, u32[]{:S(2)}) collective-permute-start(bf16[1024,384]{1,0:T(8,128)(2,1)S(1)} %constant_dynamic-update-slice_fusion.refs_1_), channel_id=1, source_target_pairs={{0,1},{1,0},{2,3},{3,2},{4,5},{5,4},{6,7},{7,6},{8,9},{9,8},{10,11... | collective-permute-start | bytes 2359304 | tf_op jit(solution)/shard_map/ppermute | solution.py:17
  114.5 1.0 copy-start.10
  115.5 1.0 copy-start.12
  116.5 1.0 copy-start.14
  119.3 5.5 %collective-permute-start.21 = (bf16[1024,384]{1,0:T(8,128)(2,1)}, bf16[1024,384]{1,0:T(8,128)(2,1)}, u32[]{:S(2)}, u32[]{:S(2)}) collective-permute-start(bf16[1024,384]{1,0:T(8,128)(2,1)} %collective-permute-done.16.refs_3_), channel_id=1, source_target_pairs={{0,1},{1,0},{2,3},{3,2},{4,5},{5,4},{6,7},{7,6},{8,9},{9,8},{10,11... | collective-permute-start | bytes 2359304 | tf_op jit(solution)/shard_map/ppermute | solution.py:17
  119.3 27.8 %collective-permute-start.22 = (bf16[512,1024]{1,0:T(8,128)(2,1)}, bf16[512,1024]{1,0:T(8,128)(2,1)}, u32[]{:S(2)}, u32[]{:S(2)}) collective-permute-start(bf16[512,1024]{1,0:T(8,128)(2,1)} %collective-permute-done.20.refs_13_), channel_id=1, source_target_pairs={{0,16},{12,28},{16,0},{28,12},{1,17},{13,29},{17,1},{29,13},{2,18}... | collective-permute-start | bytes 3145736 | tf_op jit(solution)/shard_map/ppermute | solution.py:275
  122.7 2.1 %copy-start.5 = (bf16[512,1024]{1,0:T(8,128)(2,1)S(1)}, bf16[512,1024]{1,0:T(8,128)(2,1)}, u32[]{:S(2)}) copy-start(bf16[512,1024]{1,0:T(8,128)(2,1)} %copy-done.4) | copy-start | bytes 3145732
  122.7 2.1 %copy-start.7 = (bf16[512,1024]{1,0:T(8,128)(2,1)S(1)}, bf16[512,1024]{1,0:T(8,128)(2,1)}, u32[]{:S(2)}) copy-start(bf16[512,1024]{1,0:T(8,128)(2,1)} %copy-done.6) | copy-start | bytes 3145732
  124.8 1.2 copy-start.9
  126.0 1.2 copy-start.11
  127.3 1.2 copy-start.13
  128.5 18.6 %copy-start.15 = (bf16[512,1024]{1,0:T(8,128)(2,1)S(1)}, bf16[512,1024]{1,0:T(8,128)(2,1)}, u32[]{:S(2)}) copy-start(bf16[512,1024]{1,0:T(8,128)(2,1)} %copy-done.14) | copy-start | bytes 3145732

commit v5 on v4

--- a/solution.py
+++ b/solution.py
@@ -307,6 +307,7 @@
         bit *= 2
         if line and bit == 2:
             pass
+            out_second = along(after(first_mid, got), outward)
     table = slots[0].astype(jnp.bfloat16).reshape(3, mine, rows)
     if line:
         near_y = swap(first_near)
@@ -315,7 +316,6 @@
     if line:
         pass
         cross = along(after(first_near, got), middle)
-        out_second = along(after(first_mid, got), outward)
         mid_y = swap(after(first_mid, tables[1]), inner)
 
     first = seq * mine
@@ -333,7 +333,7 @@
     got = [swapped(sends[hop], "seq", hop) for hop in range(1, seqs)]
     if line:
         pass
-        got[0] = after(got[0], out_second, cross)
+        got[0] = after(got[0], cross)
         pieces = [lax.slice_in_dim(cross, i * (share // 1), (i + 1) * (share // 1), axis=0) for i in range(1)] if 1 > 1 else [cross]
         out_third = [along(after(piece, got[0]), outward) for piece in pieces]
         third_y = [swap(piece, outer) for piece in out_third]

time: 151 us -> 150 us (level)
  waiting for transfers between devices: 70.2 us -> 76.4 us
  starting transfers between devices: 39.5 us -> 34.1 us
  local copies, waits for them, and re-layouts: 16.1 us -> 13.8 us
    ppermute x4, waiting for transfers between devices: 12.6 us -> 20.6 us  [swap(): return lax.ppermute(value, ('parts', 'seq'), pairs)]
    ppermute x8, waiting for transfers between devices: 27.7 us -> 21.6 us  [moved(): lax.ppermute(value, axis, [(source, (source + steps) % count) for source...]
    ppermute x6, starting transfers between devices: 9.59 us -> 5.03 us  [swapped(): lax.ppermute(value, axis, [(source, source ^ bits) for source in range(co...]
    ppermute x5, waiting for transfers between devices: 6.49 us -> 10.7 us  [along(): return lax.ppermute(value, 'seq', pairs)]
    unnamed x47 -> x43, local copies, waits for them, and re-layouts: 13.7 us -> 11.5 us
  transfers between devices with their start and end apart: 23 -> 23, of which waited for: 9 -> 11; matrix products, arithmetic and copies ran while one was open for 4% -> 4% of each run, Pallas kernels for 11% -> 11%
where the time goes in v5:
time: 150 us
  waiting for transfers between devices  76.4 us (51%)
  starting transfers between devices  34.1 us (23%)
  Pallas kernels  20.1 us (13%)
  local copies, waits for them, and re-layouts  13.8 us (9%)
  other arithmetic  2.81 us (2%)
  matrix products  1.99 us (1%)
    ppermute x6, waiting for transfers between devices, swapped(): lax.ppermute(value, axis, [(source, source ^ bits) for source in range(co...  23.5 us
    ppermute x8, waiting for transfers between devices, moved(): lax.ppermute(value, axis, [(source, (source + steps) % count) for source...  21.6 us
    ppermute x4, waiting for transfers between devices, swap(): return lax.ppermute(value, ('parts', 'seq'), pairs)  20.6 us
    ppermute x8, starting transfers between devices, moved(): lax.ppermute(value, axis, [(source, (source + steps) % count) for source...  13.6 us
    unnamed x43, local copies, waits for them, and re-layouts  11.5 us
    ppermute x5, waiting for transfers between devices, along(): return lax.ppermute(value, 'seq', pairs)  10.7 us
    pallas_call x2, Pallas kernels, output(): pl.pallas_call(functools.partial(output_kernel, axes, len(stacks), tuple(...  9.91 us
    ppermute x5, starting transfers between devices, along(): return lax.ppermute(value, 'seq', pairs)  8 us
  transfers between devices with their start and end apart: 23, of which 11 were waited for; matrix products, arithmetic and copies ran while one was open for 4% of the time, Pallas kernels for 11%

profile of v5, /device:TPU:0, one launch (start us, length us, event | category | flops | bytes accessed | tf_op | source)
XLA Modules:
  0.0 149.6 jit_solution(7256958102124230881)
XLA Ops:
  0.0 1.3 constant_dynamic-slice_fusion.3
  1.3 3.1 %collective-permute-start.2 = (bf16[512,1024]{1,0:T(8,128)(2,1)S(1)}, bf16[512,1024]{1,0:T(8,128)(2,1)}, u32[]{:S(2)}, u32[]{:S(2)}) collective-permute-start(bf16[512,1024]{1,0:T(8,128)(2,1)S(1)} %constant_dynamic-slice_fusion.3), channel_id=1, source_target_pairs={{0,4},{4,0},{8,12},{12,8},{1,5},{5,1},{9,13},{13,9},{2,6},{6,2},{1... | collective-permute-start | bytes 3145736 | tf_op jit(solution)/shard_map/ppermute | solution.py:269
  4.4 1.6 %collective-permute-start.3 = (bf16[512,1024]{1,0:T(8,128)(2,1)S(1)}, bf16[512,1024]{1,0:T(8,128)(2,1)}, u32[]{:S(2)}, u32[]{:S(2)}) collective-permute-start(bf16[512,1024]{1,0:T(8,128)(2,1)S(1)} %constant_dynamic-slice_fusion.3), channel_id=1, source_target_pairs={{4,8},{8,4},{5,9},{9,5},{6,10},{10,6},{7,11},{11,7},{20,24},{24,20... | collective-permute-start | bytes 3145736 | tf_op jit(solution)/shard_map/ppermute | solution.py:269
  6.1 2.2 %copy-done.1 = bf16[512,4096]{1,0:T(8,128)(2,1)S(1)} copy-done((bf16[512,4096]{1,0:T(8,128)(2,1)S(1)}, bf16[512,4096]{1,0:T(8,128)(2,1)}, u32[]{:S(2)}) %copy-start.1) | copy-done | bytes 4194328
  8.3 2.8 %copy-done.2 = bf16[1024,3,1024]{2,0,1:T(8,128)(2,1)S(1)} copy-done((bf16[1024,3,1024]{2,0,1:T(8,128)(2,1)S(1)}, bf16[1024,3,1024]{2,0,1:T(8,128)(2,1)}, u32[]{:S(2)}) %copy-start.2) | copy-done | bytes 6291480
  11.1 4.7 %shard_map.82 = (f32[768,256]{1,0:T(8,128)S(1)}, bf16[768,256]{1,0:T(8,128)(2,1)}, bf16[768,256]{1,0:T(8,128)(2,1)S(1)}, bf16[768,256]{1,0:T(8,128)(2,1)S(1)}) custom-call(s32[4]{0:T(128)S(1)} %pad_add_fusion.where, bf16[512,4096]{1,0:T(8,128)(2,1)S(1)} %copy-done.1, bf16[512,4096]{1,0:T(8,128)(2,1)S(1)} %copy-done.1, f32[1,4096]{1,0:T(1,128)S(1)} %bitcast.19, ...), custom_call_target="tpu_custom_call" | custom-call | flops 1610612736 | bytes 8388608 | tf_op jit(solution)/shard_map/pallas_call | solution.py:54
  15.9 0.9 copy-done.14
  16.7 2.5 %collective-permute-start.6 = (s32[384]{0:T(512)S(1)}, s32[384]{0:T(512)S(1)}, u32[]{:S(2)}, u32[]{:S(2)}) collective-permute-start(s32[384]{0:T(512)S(1)} %copy-done.17), channel_id=1, source_target_pairs={{0,12},{4,0},{8,4},{12,8},{1,13},{5,1},{9,5},{13,9},{2,14},{6,2},{... | collective-permute-start | bytes 4616 | tf_op jit(solution)/shard_map/ppermute | solution.py:17
  19.2 2.4 %collective-permute-start.5 = (s32[384]{0:T(512)S(1)}, s32[384]{0:T(512)S(1)}, u32[]{:S(2)}, u32[]{:S(2)}) collective-permute-start(s32[384]{0:T(512)S(1)} %copy-done.17), channel_id=1, source_target_pairs={{0,8},{4,12},{8,0},{12,4},{1,9},{5,13},{9,1},{13,5},{2,10},{6,14},... | collective-permute-start | bytes 4616 | tf_op jit(solution)/shard_map/ppermute | solution.py:17
  21.8 0.8 dynamic_slice.22
  22.7 5.8 %collective-permute-done.6 = s32[384]{0:T(512)S(1)} collective-permute-done((s32[384]{0:T(512)S(1)}, s32[384]{0:T(512)S(1)}, u32[]{:S(2)}, u32[]{:S(2)}) %collective-permute-start.6) | collective-permute-done | bytes 1568 | tf_op jit(solution)/shard_map/ppermute | solution.py:17
  28.5 4.0 %collective-permute-start.4 = (s32[384]{0:T(512)S(1)}, s32[384]{0:T(512)S(1)}, u32[]{:S(2)}, u32[]{:S(2)}) collective-permute-start(s32[384]{0:T(512)S(1)} %copy-done.17), channel_id=1, source_target_pairs={{0,4},{4,8},{8,12},{12,0},{1,5},{5,9},{9,13},{13,1},{2,6},{6,10},{... | collective-permute-start | bytes 4616 | tf_op jit(solution)/shard_map/ppermute | solution.py:17
  32.5 1.5 %collective-permute-start.8 = (bf16[512,1024]{1,0:T(8,128)(2,1)}, bf16[512,1024]{1,0:T(8,128)(2,1)S(1)}, u32[]{:S(2)}, u32[]{:S(2)}) collective-permute-start(bf16[512,1024]{1,0:T(8,128)(2,1)} %collective-permute-done.2.refs_6_), channel_id=1, source_target_pairs={{0,16},{16,0},{1,17},{17,1},{2,18},{18,2},{3,19},{19,3},{4,20},{20... | collective-permute-start | bytes 3145736 | tf_op jit(solution)/shard_map/ppermute | solution.py:17
  34.1 5.3 %collective-permute-done.4 = s32[384]{0:T(512)S(1)} collective-permute-done((s32[384]{0:T(512)S(1)}, s32[384]{0:T(512)S(1)}, u32[]{:S(2)}, u32[]{:S(2)}) %collective-permute-start.4) | collective-permute-done | bytes 1568 | tf_op jit(solution)/shard_map/ppermute | solution.py:17
  39.5 0.9 add_convert_fusion.1
  40.3 0.5 collective-permute-start.7
  41.0 0.4 shard_map.83.refs_4_
  41.5 8.4 %collective-permute-done = bf16[768,256]{1,0:T(8,128)(2,1)} collective-permute-done((bf16[768,256]{1,0:T(8,128)(2,1)}, bf16[768,256]{1,0:T(8,128)(2,1)}, u32[]{:S(2)}, u32[]{:S(2)}) %collective-permute-start) | collective-permute-done | bytes 393248 | tf_op jit(solution)/shard_map/ppermute | solution.py:22
  49.9 1.3 collective-permute-start.16
  51.2 7.4 %collective-permute-done.7 = bf16[768,256]{1,0:T(8,128)(2,1)} collective-permute-done((bf16[768,256]{1,0:T(8,128)(2,1)}, bf16[768,256]{1,0:T(8,128)(2,1)}, u32[]{:S(2)}, u32[]{:S(2)}) %collective-permute-start.7) | collective-permute-done | bytes 393248 | tf_op jit(solution)/shard_map/ppermute | solution.py:22
  58.7 0.7 collective-permute-start.11
  59.4 1.5 add_convert_fusion
  60.9 1.6 %collective-permute-start.9 = (bf16[3,256,256]{2,1,0:T(8,128)(2,1)S(1)}, bf16[3,256,256]{2,1,0:T(8,128)(2,1)S(1)}, u32[]{:S(2)}, u32[]{:S(2)}) collective-permute-start(bf16[3,256,256]{2,1,0:T(8,128)(2,1)S(1)} %bitcast.16), channel_id=1, source_target_pairs={{0,16},{16,0},{1,17},{17,1},{2,18},{18,2},{3,19},{19,3},{4,20},{20... | collective-permute-start | bytes 1179656 | tf_op jit(solution)/shard_map/ppermute | solution.py:17
  62.8 5.9 %collective-permute-done.9.refs_1_ = bf16[3,256,256]{2,1,0:T(8,128)(2,1)S(1)} collective-permute-done((bf16[3,256,256]{2,1,0:T(8,128)(2,1)S(1)}, bf16[3,256,256]{2,1,0:T(8,128)(2,1)S(1)}, u32[]{:S(2)}, u32[]{:S(2)}) %collective-permute-start.9) | collective-permute-done | bytes 393248 | tf_op jit(solution)/shard_map/ppermute | solution.py:17
  68.7 5.1 %shard_map.84 = (bf16[256,384]{1,0:T(8,128)(2,1)S(1)}, bf16[256,384]{1,0:T(8,128)(2,1)S(1)}, bf16[256,384]{1,0:T(8,128)(2,1)S(1)}, bf16[256,384]{1,0:T(8,128)(2,1)S(1)}) custom-call(s32[4]{0:T(128)S(1)} %pad_add_fusion.where, bf16[3,256,256]{2,1,0:T(8,128)(2,1)S(1)} %bitcast.17, bf16[3,256,256]{2,1,0:T(8,128)(2,1)S(1)} %collective-permute-done.9.refs_1_, ...), custom_call_target="tpu_custom_call" | custom-call | flops 1207959552 | bytes 1572864 | tf_op jit(solution)/shard_map/pallas_call | solution.py:156
  73.8 1.4 collective-permute-start.10
  75.2 1.1 collective-permute-start.12
  76.4 4.8 %collective-permute-done.16.refs_9_ = bf16[512,1024]{1,0:T(8,128)(2,1)} collective-permute-done((bf16[512,1024]{1,0:T(8,128)(2,1)}, bf16[512,1024]{1,0:T(8,128)(2,1)}, u32[]{:S(2)}, u32[]{:S(2)}) %collective-permute-start.16) | collective-permute-done | bytes 1048608 | tf_op jit(solution)/shard_map/ppermute | solution.py:269
  81.2 4.0 %collective-permute-start.17 = (bf16[512,1024]{1,0:T(8,128)(2,1)}, bf16[512,1024]{1,0:T(8,128)(2,1)S(1)}, u32[]{:S(2)}, u32[]{:S(2)}) collective-permute-start(bf16[512,1024]{1,0:T(8,128)(2,1)} %collective-permute-done.16.refs_9_), channel_id=1, source_target_pairs={{0,16},{12,28},{16,0},{28,12},{1,17},{13,29},{17,1},{29,13},{2,18}... | collective-permute-start | bytes 3145736 | tf_op jit(solution)/shard_map/ppermute | solution.py:275
  85.2 0.7 collective-permute-start.19
  86.0 1.9 %collective-permute-start.13 = (bf16[256,384]{1,0:T(8,128)(2,1)S(1)}, bf16[256,384]{1,0:T(8,128)(2,1)S(1)}, u32[]{:S(2)}, u32[]{:S(2)}) collective-permute-start(bf16[256,384]{1,0:T(8,128)(2,1)S(1)} %get-tuple-element.34), channel_id=1, source_target_pairs={{0,12},{4,8},{8,4},{12,0},{1,13},{5,9},{9,5},{13,1},{2,14},{6,10},... | collective-permute-start | bytes 589832 | tf_op jit(solution)/shard_map/ppermute | solution.py:22
  87.9 0.7 collective-permute-start.18
  88.6 7.7 %collective-permute-done.12 = bf16[256,384]{1,0:T(8,128)(2,1)S(1)} collective-permute-done((bf16[256,384]{1,0:T(8,128)(2,1)S(1)}, bf16[256,384]{1,0:T(8,128)(2,1)S(1)}, u32[]{:S(2)}, u32[]{:S(2)}) %collective-permute-start.12) | collective-permute-done | bytes 196640 | tf_op jit(solution)/shard_map/ppermute | solution.py:22
  96.2 1.3 collective-permute-start.20
  97.7 1.6 %collective-permute-start.15 = (bf16[1024,384]{1,0:T(8,128)(2,1)S(1)}, bf16[1024,384]{1,0:T(8,128)(2,1)}, u32[]{:S(2)}, u32[]{:S(2)}) collective-permute-start(bf16[1024,384]{1,0:T(8,128)(2,1)S(1)} %constant_dynamic-update-slice_fusion.refs_1_), channel_id=1, source_target_pairs={{0,2},{2,0},{1,3},{3,1},{4,6},{6,4},{5,7},{7,5},{8,10},{10,8},{9,1... | collective-permute-start | bytes 2359304 | tf_op jit(solution)/shard_map/ppermute | solution.py:17
  99.2 5.6 %collective-permute-done.17.refs_11_ = bf16[512,1024]{1,0:T(8,128)(2,1)S(1)} collective-permute-done((bf16[512,1024]{1,0:T(8,128)(2,1)}, bf16[512,1024]{1,0:T(8,128)(2,1)S(1)}, u32[]{:S(2)}, u32[]{:S(2)}) %collective-permute-start.17) | collective-permute-done | bytes 1048608 | tf_op jit(solution)/shard_map/ppermute | solution.py:275
  104.8 1.0 copy-done.8
  105.8 4.5 %collective-permute-done.15.refs_3_ = bf16[1024,384]{1,0:T(8,128)(2,1)} collective-permute-done((bf16[1024,384]{1,0:T(8,128)(2,1)S(1)}, bf16[1024,384]{1,0:T(8,128)(2,1)}, u32[]{:S(2)}, u32[]{:S(2)}) %collective-permute-start.15) | collective-permute-done | bytes 786464 | tf_op jit(solution)/shard_map/ppermute | solution.py:17
  110.3 1.0 copy-done.10
  111.3 1.0 copy-done.12
  112.3 5.9 %collective-permute-done.20.refs_13_ = bf16[512,1024]{1,0:T(8,128)(2,1)} collective-permute-done((bf16[512,1024]{1,0:T(8,128)(2,1)S(1)}, bf16[512,1024]{1,0:T(8,128)(2,1)}, u32[]{:S(2)}, u32[]{:S(2)}) %collective-permute-start.20) | collective-permute-done | bytes 1048608 | tf_op jit(solution)/shard_map/ppermute | solution.py:269
  118.2 2.0 %collective-permute-start.22 = (bf16[512,1024]{1,0:T(8,128)(2,1)}, bf16[512,1024]{1,0:T(8,128)(2,1)}, u32[]{:S(2)}, u32[]{:S(2)}) collective-permute-start(bf16[512,1024]{1,0:T(8,128)(2,1)} %collective-permute-done.20.refs_13_), channel_id=1, source_target_pairs={{0,16},{12,28},{16,0},{28,12},{1,17},{13,29},{17,1},{29,13},{2,18}... | collective-permute-start | bytes 3145736 | tf_op jit(solution)/shard_map/ppermute | solution.py:275
  120.2 2.0 %fusion.refs_0_ = f32[384,1024]{1,0:T(8,128)S(1)} fusion(bf16[512,4096]{1,0:T(8,128)(2,1)} %cut.1, s32[]{:T(128)S(6)} %select_n.16, s32[384]{0:T(512)S(1)} %copy-done.17), kind=kOutput, calls=%fused_computation.1 | convolution fusion | flops 402849792 | bytes 2622980 | tf_op jit(solution)/shard_map/dot_general | solution.py:351
  122.3 1.2 copy-done.9
  123.5 1.2 copy-done.11
  124.7 6.3 %shard_map.85.refs_0_ = f32[384,1024]{1,0:T(8,128)S(1)} custom-call(s32[4]{0:T(128)S(1)} %pad_add_fusion.where, f32[384,1024]{1,0:T(8,128)S(1)} %fusion.refs_0_, bf16[1024,384]{1,0:T(8,128)(2,1)S(1)} %constant_dynamic-update-slice_fusion.refs_1_, bf16[1024,384]{1,0:T(8,128)(2,1)} %collective-permute-done.14.refs_2_, ...), custom_call_target="tpu_custom_call" | custom-call | flops 2818572288 | bytes 7340032 | tf_op jit(solution)/shard_map/pallas_call | solution.py:237
  131.0 15.0 %collective-permute-done.22.refs_6_ = bf16[512,1024]{1,0:T(8,128)(2,1)} collective-permute-done((bf16[512,1024]{1,0:T(8,128)(2,1)}, bf16[512,1024]{1,0:T(8,128)(2,1)}, u32[]{:S(2)}, u32[]{:S(2)}) %collective-permute-start.22) | collective-permute-done | bytes 1048608 | tf_op jit(solution)/shard_map/ppermute | solution.py:275
  146.0 3.6 %shard_map.86 = bf16[384,1024]{1,0:T(8,128)(2,1)} custom-call(s32[4]{0:T(128)S(1)} %pad_add_fusion.where, f32[384,1024]{1,0:T(8,128)S(1)} %shard_map.85.refs_0_, bf16[1024,384]{1,0:T(8,128)(2,1)S(1)} %constant_dynamic-update-slice_fusion.refs_1_, bf16[1024,384]{1,0:T(8,128)(2,1)} %collective-permute-done.14.refs_2_, ...), custom_call_target="tpu_custom_call" | custom-call | flops 402653184 | bytes 1048576 | tf_op jit(solution)/shard_map/pallas_call | solution.py:237
  (70 shorter events, 1.1 us)
Async XLA Ops:
  0.0 34.1 %copy-start = (f32[64,128]{1,0:T(8,128)S(1)}, f32[64,128]{1,0:T(8,128)}, u32[]{:S(2)}) copy-start(f32[64,128]{1,0:T(8,128)} %param.13) | copy-start | bytes 98308
  0.0 6.1 %copy-start.15 = (f32[4096]{0:T(1024)S(1)}, f32[4096]{0:T(1024)}, u32[]{:S(2)}) copy-start(f32[4096]{0:T(1024)} %param.10) | copy-start | bytes 49156
  1.3 31.2 %collective-permute-start.2 = (bf16[512,1024]{1,0:T(8,128)(2,1)S(1)}, bf16[512,1024]{1,0:T(8,128)(2,1)}, u32[]{:S(2)}, u32[]{:S(2)}) collective-permute-start(bf16[512,1024]{1,0:T(8,128)(2,1)S(1)} %constant_dynamic-slice_fusion.3), channel_id=1, source_target_pairs={{0,4},{4,0},{8,12},{12,8},{1,5},{5,1},{9,13},{13,9},{2,6},{6,2},{1... | collective-permute-start | bytes 3145736 | tf_op jit(solution)/shard_map/ppermute | solution.py:269
  4.4 35.1 %collective-permute-start.3 = (bf16[512,1024]{1,0:T(8,128)(2,1)S(1)}, bf16[512,1024]{1,0:T(8,128)(2,1)}, u32[]{:S(2)}, u32[]{:S(2)}) collective-permute-start(bf16[512,1024]{1,0:T(8,128)(2,1)S(1)} %constant_dynamic-slice_fusion.3), channel_id=1, source_target_pairs={{4,8},{8,4},{5,9},{9,5},{6,10},{10,6},{7,11},{11,7},{20,24},{24,20... | collective-permute-start | bytes 3145736 | tf_op jit(solution)/shard_map/ppermute | solution.py:269
  6.1 2.2 %copy-start.1 = (bf16[512,4096]{1,0:T(8,128)(2,1)S(1)}, bf16[512,4096]{1,0:T(8,128)(2,1)}, u32[]{:S(2)}) copy-start(bf16[512,4096]{1,0:T(8,128)(2,1)} %cut.1) | copy-start | bytes 12582916
  8.3 2.8 %copy-start.2 = (bf16[1024,3,1024]{2,0,1:T(8,128)(2,1)S(1)}, bf16[1024,3,1024]{2,0,1:T(8,128)(2,1)}, u32[]{:S(2)}) copy-start(bf16[1024,3,1024]{2,0,1:T(8,128)(2,1)} %param.11) | copy-start | bytes 18874372
  11.1 5.6 %copy-start.17 = (s32[384]{0:T(512)S(1)}, s32[384]{0:T(512)}, u32[]{:S(2)}) copy-start(s32[384]{0:T(512)} %param.8) | copy-start | bytes 4612
  11.1 10.5 %copy-start.16 = (f32[3,3,1024]{2,1,0:T(4,128)S(1)}, f32[3,3,1024]{2,1,0:T(4,128)}, u32[]{:S(2)}) copy-start(f32[3,3,1024]{2,1,0:T(4,128)} %param.12) | copy-start | bytes 110596
  15.9 0.9 copy-start.14
  16.7 11.8 %collective-permute-start.6 = (s32[384]{0:T(512)S(1)}, s32[384]{0:T(512)S(1)}, u32[]{:S(2)}, u32[]{:S(2)}) collective-permute-start(s32[384]{0:T(512)S(1)} %copy-done.17), channel_id=1, source_target_pairs={{0,12},{4,0},{8,4},{12,8},{1,13},{5,1},{9,5},{13,9},{2,14},{6,2},{... | collective-permute-start | bytes 4616 | tf_op jit(solution)/shard_map/ppermute | solution.py:17
  19.2 14.8 %collective-permute-start.5 = (s32[384]{0:T(512)S(1)}, s32[384]{0:T(512)S(1)}, u32[]{:S(2)}, u32[]{:S(2)}) collective-permute-start(s32[384]{0:T(512)S(1)} %copy-done.17), channel_id=1, source_target_pairs={{0,8},{4,12},{8,0},{12,4},{1,9},{5,13},{9,1},{13,5},{2,10},{6,14},... | collective-permute-start | bytes 4616 | tf_op jit(solution)/shard_map/ppermute | solution.py:17
  21.6 17.8 %collective-permute-start.1 = (bf16[768,256]{1,0:T(8,128)(2,1)S(1)}, bf16[768,256]{1,0:T(8,128)(2,1)S(1)}, u32[]{:S(2)}, u32[]{:S(2)}) collective-permute-start(bf16[768,256]{1,0:T(8,128)(2,1)S(1)} %get-tuple-element.25), channel_id=1, source_target_pairs={{0,4},{4,0},{8,12},{12,8},{1,5},{5,1},{9,13},{13,9},{2,6},{6,2},{1... | collective-permute-start | bytes 1179656 | tf_op jit(solution)/shard_map/ppermute | solution.py:22
  28.5 11.0 %collective-permute-start.4 = (s32[384]{0:T(512)S(1)}, s32[384]{0:T(512)S(1)}, u32[]{:S(2)}, u32[]{:S(2)}) collective-permute-start(s32[384]{0:T(512)S(1)} %copy-done.17), channel_id=1, source_target_pairs={{0,4},{4,8},{8,12},{12,0},{1,5},{5,9},{9,13},{13,1},{2,6},{6,10},{... | collective-permute-start | bytes 4616 | tf_op jit(solution)/shard_map/ppermute | solution.py:17
  32.5 28.3 %collective-permute-start.8 = (bf16[512,1024]{1,0:T(8,128)(2,1)}, bf16[512,1024]{1,0:T(8,128)(2,1)S(1)}, u32[]{:S(2)}, u32[]{:S(2)}) collective-permute-start(bf16[512,1024]{1,0:T(8,128)(2,1)} %collective-permute-done.2.refs_6_), channel_id=1, source_target_pairs={{0,16},{16,0},{1,17},{17,1},{2,18},{18,2},{3,19},{19,3},{4,20},{20... | collective-permute-start | bytes 3145736 | tf_op jit(solution)/shard_map/ppermute | solution.py:17
  34.1 15.9 %collective-permute-start = (bf16[768,256]{1,0:T(8,128)(2,1)}, bf16[768,256]{1,0:T(8,128)(2,1)}, u32[]{:S(2)}, u32[]{:S(2)}) collective-permute-start(bf16[768,256]{1,0:T(8,128)(2,1)} %get-tuple-element.23), channel_id=1, source_target_pairs={{0,4},{4,0},{8,12},{12,8},{1,5},{5,1},{9,13},{13,9},{2,6},{6,2},{1... | collective-permute-start | bytes 1179656 | tf_op jit(solution)/shard_map/ppermute | solution.py:22
  40.3 18.3 %collective-permute-start.7 = (bf16[768,256]{1,0:T(8,128)(2,1)}, bf16[768,256]{1,0:T(8,128)(2,1)}, u32[]{:S(2)}, u32[]{:S(2)}) collective-permute-start(bf16[768,256]{1,0:T(8,128)(2,1)} %add_convert_fusion.1), channel_id=1, source_target_pairs={{0,8},{4,12},{8,0},{12,4},{1,9},{5,13},{9,1},{13,5},{2,10},{6,14},... | collective-permute-start | bytes 1179656 | tf_op jit(solution)/shard_map/ppermute | solution.py:22
  49.9 31.2 %collective-permute-start.16 = (bf16[512,1024]{1,0:T(8,128)(2,1)}, bf16[512,1024]{1,0:T(8,128)(2,1)}, u32[]{:S(2)}, u32[]{:S(2)}) collective-permute-start(bf16[512,1024]{1,0:T(8,128)(2,1)} %collective-permute-done.3.refs_8_), channel_id=1, source_target_pairs={{4,0},{8,12},{5,1},{9,13},{6,2},{10,14},{7,3},{11,15},{20,16},{24,... | collective-permute-start | bytes 3145736 | tf_op jit(solution)/shard_map/ppermute | solution.py:269
  58.7 27.3 %collective-permute-start.11 = (bf16[512,1024]{1,0:T(8,128)(2,1)}, bf16[512,1024]{1,0:T(8,128)(2,1)S(1)}, u32[]{:S(2)}, u32[]{:S(2)}) collective-permute-start(bf16[512,1024]{1,0:T(8,128)(2,1)} %collective-permute-done.2.refs_6_), channel_id=1, source_target_pairs={{4,8},{8,4},{5,9},{9,5},{6,10},{10,6},{7,11},{11,7},{20,24},{24,20... | collective-permute-start | bytes 3145736 | tf_op jit(solution)/shard_map/ppermute | solution.py:269
  60.9 12.9 %copy-start.4 = (bf16[512,1024]{1,0:T(8,128)(2,1)}, bf16[512,1024]{1,0:T(8,128)(2,1)S(1)}, u32[]{:S(2)}) copy-start(bf16[512,1024]{1,0:T(8,128)(2,1)S(1)} %collective-permute-done.8.refs_7_) | copy-start | bytes 3145732
  60.9 7.8 %collective-permute-start.9 = (bf16[3,256,256]{2,1,0:T(8,128)(2,1)S(1)}, bf16[3,256,256]{2,1,0:T(8,128)(2,1)S(1)}, u32[]{:S(2)}, u32[]{:S(2)}) collective-permute-start(bf16[3,256,256]{2,1,0:T(8,128)(2,1)S(1)} %bitcast.16), channel_id=1, source_target_pairs={{0,16},{16,0},{1,17},{17,1},{2,18},{18,2},{3,19},{19,3},{4,20},{20... | collective-permute-start | bytes 1179656 | tf_op jit(solution)/shard_map/ppermute | solution.py:17
  73.8 14.1 %collective-permute-start.10 = (bf16[256,384]{1,0:T(8,128)(2,1)S(1)}, bf16[256,384]{1,0:T(8,128)(2,1)S(1)}, u32[]{:S(2)}, u32[]{:S(2)}) collective-permute-start(bf16[256,384]{1,0:T(8,128)(2,1)S(1)} %get-tuple-element.30), channel_id=1, source_target_pairs={{0,4},{4,0},{8,12},{12,8},{1,5},{5,1},{9,13},{13,9},{2,6},{6,2},{1... | collective-permute-start | bytes 589832 | tf_op jit(solution)/shard_map/ppermute | solution.py:22
  75.2 21.0 %collective-permute-start.12 = (bf16[256,384]{1,0:T(8,128)(2,1)S(1)}, bf16[256,384]{1,0:T(8,128)(2,1)S(1)}, u32[]{:S(2)}, u32[]{:S(2)}) collective-permute-start(bf16[256,384]{1,0:T(8,128)(2,1)S(1)} %get-tuple-element.33), channel_id=1, source_target_pairs={{0,8},{4,12},{8,0},{12,4},{1,9},{5,13},{9,1},{13,5},{2,10},{6,14},... | collective-permute-start | bytes 589832 | tf_op jit(solution)/shard_map/ppermute | solution.py:22
  81.2 23.7 %collective-permute-start.17 = (bf16[512,1024]{1,0:T(8,128)(2,1)}, bf16[512,1024]{1,0:T(8,128)(2,1)S(1)}, u32[]{:S(2)}, u32[]{:S(2)}) collective-permute-start(bf16[512,1024]{1,0:T(8,128)(2,1)} %collective-permute-done.16.refs_9_), channel_id=1, source_target_pairs={{0,16},{12,28},{16,0},{28,12},{1,17},{13,29},{17,1},{29,13},{2,18}... | collective-permute-start | bytes 3145736 | tf_op jit(solution)/shard_map/ppermute | solution.py:275
  85.2 25.1 %collective-permute-start.19 = (bf16[512,1024]{1,0:T(8,128)(2,1)}, bf16[512,1024]{1,0:T(8,128)(2,1)S(1)}, u32[]{:S(2)}, u32[]{:S(2)}) collective-permute-start(bf16[512,1024]{1,0:T(8,128)(2,1)} %collective-permute-done.3.refs_8_), channel_id=1, source_target_pairs={{4,20},{8,24},{20,4},{24,8},{5,21},{9,25},{21,5},{25,9},{6,22},{10... | collective-permute-start | bytes 3145736 | tf_op jit(solution)/shard_map/ppermute | solution.py:275
  85.9 36.3 %copy-start.3 = (bf16[1024,1024]{1,0:T(8,128)(2,1)S(1)}, bf16[1024,1024]{1,0:T(8,128)(2,1)}, u32[]{:S(2)}) copy-start(bf16[1024,1024]{1,0:T(8,128)(2,1)} %refs_5_.1) | copy-start | bytes 6291460
  86.0 24.3 %copy-start.6 = (bf16[512,1024]{1,0:T(8,128)(2,1)}, bf16[512,1024]{1,0:T(8,128)(2,1)S(1)}, u32[]{:S(2)}) copy-start(bf16[512,1024]{1,0:T(8,128)(2,1)S(1)} %collective-permute-done.11.refs_12_) | copy-start | bytes 3145732
  86.0 11.6 %collective-permute-start.13 = (bf16[256,384]{1,0:T(8,128)(2,1)S(1)}, bf16[256,384]{1,0:T(8,128)(2,1)S(1)}, u32[]{:S(2)}, u32[]{:S(2)}) collective-permute-start(bf16[256,384]{1,0:T(8,128)(2,1)S(1)} %get-tuple-element.34), channel_id=1, source_target_pairs={{0,12},{4,8},{8,4},{12,0},{1,13},{5,9},{9,5},{13,1},{2,14},{6,10},... | collective-permute-start | bytes 589832 | tf_op jit(solution)/shard_map/ppermute | solution.py:22
  87.9 23.4 %collective-permute-start.18 = (bf16[512,1024]{1,0:T(8,128)(2,1)S(1)}, bf16[512,1024]{1,0:T(8,128)(2,1)S(1)}, u32[]{:S(2)}, u32[]{:S(2)}) collective-permute-start(bf16[512,1024]{1,0:T(8,128)(2,1)S(1)} %collective-permute-done.11.refs_12_), channel_id=1, source_target_pairs={{4,20},{8,24},{20,4},{24,8},{5,21},{9,25},{21,5},{25,9},{6,22},{10... | collective-permute-start | bytes 3145736 | tf_op jit(solution)/shard_map/ppermute | solution.py:275
  96.2 21.9 %collective-permute-start.20 = (bf16[512,1024]{1,0:T(8,128)(2,1)S(1)}, bf16[512,1024]{1,0:T(8,128)(2,1)}, u32[]{:S(2)}, u32[]{:S(2)}) collective-permute-start(bf16[512,1024]{1,0:T(8,128)(2,1)S(1)} %collective-permute-done.11.refs_12_), channel_id=1, source_target_pairs={{4,0},{8,12},{5,1},{9,13},{6,2},{10,14},{7,3},{11,15},{20,16},{24,... | collective-permute-start | bytes 3145736 | tf_op jit(solution)/shard_map/ppermute | solution.py:269
  97.7 12.6 %collective-permute-start.15 = (bf16[1024,384]{1,0:T(8,128)(2,1)S(1)}, bf16[1024,384]{1,0:T(8,128)(2,1)}, u32[]{:S(2)}, u32[]{:S(2)}) collective-permute-start(bf16[1024,384]{1,0:T(8,128)(2,1)S(1)} %constant_dynamic-update-slice_fusion.refs_1_), channel_id=1, source_target_pairs={{0,2},{2,0},{1,3},{3,1},{4,6},{6,4},{5,7},{7,5},{8,10},{10,8},{9,1... | collective-permute-start | bytes 2359304 | tf_op jit(solution)/shard_map/ppermute | solution.py:17
  104.8 1.0 copy-start.8
  105.8 16.4 %collective-permute-start.14 = (bf16[1024,384]{1,0:T(8,128)(2,1)S(1)}, bf16[1024,384]{1,0:T(8,128)(2,1)}, u32[]{:S(2)}, u32[]{:S(2)}) collective-permute-start(bf16[1024,384]{1,0:T(8,128)(2,1)S(1)} %constant_dynamic-update-slice_fusion.refs_1_), channel_id=1, source_target_pairs={{0,1},{1,0},{2,3},{3,2},{4,5},{5,4},{6,7},{7,6},{8,9},{9,8},{10,11... | collective-permute-start | bytes 2359304 | tf_op jit(solution)/shard_map/ppermute | solution.py:17
  110.3 1.0 copy-start.10
  111.3 1.0 copy-start.12
  118.2 4.0 %collective-permute-start.21 = (bf16[1024,384]{1,0:T(8,128)(2,1)}, bf16[1024,384]{1,0:T(8,128)(2,1)}, u32[]{:S(2)}, u32[]{:S(2)}) collective-permute-start(bf16[1024,384]{1,0:T(8,128)(2,1)} %collective-permute-done.15.refs_3_), channel_id=1, source_target_pairs={{0,1},{1,0},{2,3},{3,2},{4,5},{5,4},{6,7},{7,6},{8,9},{9,8},{10,11... | collective-permute-start | bytes 2359304 | tf_op jit(solution)/shard_map/ppermute | solution.py:17
  118.2 27.8 %collective-permute-start.22 = (bf16[512,1024]{1,0:T(8,128)(2,1)}, bf16[512,1024]{1,0:T(8,128)(2,1)}, u32[]{:S(2)}, u32[]{:S(2)}) collective-permute-start(bf16[512,1024]{1,0:T(8,128)(2,1)} %collective-permute-done.20.refs_13_), channel_id=1, source_target_pairs={{0,16},{12,28},{16,0},{28,12},{1,17},{13,29},{17,1},{29,13},{2,18}... | collective-permute-start | bytes 3145736 | tf_op jit(solution)/shard_map/ppermute | solution.py:275
  120.2 2.0 %copy-start.5 = (bf16[512,1024]{1,0:T(8,128)(2,1)S(1)}, bf16[512,1024]{1,0:T(8,128)(2,1)}, u32[]{:S(2)}) copy-start(bf16[512,1024]{1,0:T(8,128)(2,1)} %copy-done.4) | copy-start | bytes 3145732
  120.2 2.0 %copy-start.7 = (bf16[512,1024]{1,0:T(8,128)(2,1)S(1)}, bf16[512,1024]{1,0:T(8,128)(2,1)}, u32[]{:S(2)}) copy-start(bf16[512,1024]{1,0:T(8,128)(2,1)} %copy-done.6) | copy-start | bytes 3145732
  122.3 1.2 copy-start.9
  123.5 1.2 copy-start.11
  124.7 21.3 %copy-start.13 = (bf16[512,1024]{1,0:T(8,128)(2,1)S(1)}, bf16[512,1024]{1,0:T(8,128)(2,1)}, u32[]{:S(2)}) copy-start(bf16[512,1024]{1,0:T(8,128)(2,1)} %copy-done.12) | copy-start | bytes 3145732
